TPU v7x, 512 devices: a whole 4x4x16 slice. The times are simulated.
512 devices in a mesh: cells: 64 (over z, x), days: 8 (over y, core).
Axes of the slice: x: 4, y: 4, z: 16, core: 2. Of those that a mesh axis runs over, the one named last changes fastest.
Arguments:
- field: float32 [2048, 262144], P('days', 'cells'), may hold values from -600 to 600, as said below
- pcs: float32 [100, 2048], P(None, 'days'), may hold values from -6 to 6
Outputs:
- rotated_loadings: float32 [100, 262144], P(None, ('cells', 'days'))
- series: float32 [100, 2048], P(None, 'days')
Inputs may be any that keep to these rules, and one draw needn't show every extreme that they name: `field`: each entry is a day factor times a cell factor times a bounded random value.
All inputs are finite; a program needn't handle non-finite values.
Results may differ from a plain program's by a relative error of at most 0.00022.
Values sent between devices are 32-bit elements; how exact they have to be, the bound alone decides.
No kernel may reach another device: no remote copies, remote signals or barrier semaphores. Data moves between devices by JAX's collectives and lax.ppermute only.
A program may use at most 64 MiB of HBM per device.

v0:
```python
import jax
import jax.numpy as jnp
from jax import lax
from jax.sharding import PartitionSpec as P

ITERS = 3
NS_STEPS = 12


HIGH = lax.Precision.HIGHEST


def rows_dot(left, right):
    return lax.dot_general(
        left, right, (((1,), (1,)), ((), ())), precision=HIGH, preferred_element_type=jnp.float32
    )


def polar(grad):
    x = grad / (jnp.sqrt(jnp.sum(grad * grad)) + 1e-06)
    for step in range(NS_STEPS):
        inner = jnp.dot(x.T, x, precision=HIGH)
        x = 1.5 * x - 0.5 * jnp.dot(x, inner, precision=HIGH)
    return x


def varimax(loadings, summer, cells_total):
    rotation = jnp.eye(loadings.shape[0], dtype=jnp.float32)
    for step in range(ITERS):
        turned = jnp.dot(rotation.T, loadings, precision=HIGH)
        cube, cross, colsq = summer(
            (
                rows_dot(loadings, turned * turned * turned),
                rows_dot(loadings, turned),
                jnp.sum(turned * turned, axis=1),
            )
        )
        grad = cube - cross * colsq[None, :] / cells_total
        rotation = polar(grad)
    return jnp.dot(rotation.T, loadings, precision=HIGH)


def on_device(field, pcs):
    days_total = pcs.shape[1] * lax.axis_size("days")
    cells_total = field.shape[1] * lax.axis_size("cells")
    partial_value = jnp.dot(pcs, field, precision=HIGH) * (1.0 / days_total**0.5)
    loadings = lax.psum(partial_value, "days")

    def summer(terms):
        return lax.psum(terms, "cells")

    full_rotated = varimax(loadings, summer, cells_total)
    share = full_rotated.shape[1] // lax.axis_size("days")
    rotated_loadings = lax.dynamic_slice_in_dim(
        full_rotated, lax.axis_index("days") * share, share, 1
    )
    terms = rows_dot(full_rotated, field) * (days_total**0.5 / cells_total)
    series = lax.psum(terms, "cells")
    return (rotated_loadings, series)


def solution(mesh):
    placed = (P("days", "cells"), P(None, "days"))
    return jax.shard_map(
        on_device,
        mesh=mesh,
        in_specs=placed,
        out_specs=(P(None, ("cells", "days")), P(None, "days")),
        check_vma=False,
    )
```

profile of v0, /device:TPU:1, one launch (start us, length us, event | category | flops | bytes accessed | tf_op | source)
XLA Modules:
  0.0 1175.8 jit_solution(8427311078409844537)
XLA Ops:
  7.2 0.8 copy-done
  8.1 5.6 convolution_multiply_fusion
  13.8 83.6 %all-reduce.9.cloned.1.call-done = f32[100,4096]{1,0:T(8,128)} async-done(((f32[100,4096]{1,0:T(8,128)}), f32[100,4096]{1,0:T(8,128)}) %all-reduce.9.cloned.1.call-update) | async-done | bytes 1638416 | tf_op jit(solution)/shard_map/psum | solution.py:47
  97.3 3.3 multiply_reduce_fusion.2
  100.7 2.1 fusion.43
  102.8 2.3 fusion
  105.3 250.4 %all-reduce.17.cloned.1.call-done = (f32[100,100]{1,0:T(8,128)}, f32[100,100]{1,0:T(8,128)}, f32[100]{0:T(128)}) async-done(((f32[100,100]{1,0:T(8,128)}, f32[100,100]{1,0:T(8,128)}, f32[100]{0:T(128)}), (f32[100,100]{1,0:T(8,128)}, f32[100,100]{1,0:T(8,128)}, f32[100]{0:T(128)})) %all-reduce.17.cloned.1.call-update) | async-done | bytes 80416 | tf_op jit(solution)/shard_map/psum | solution.py:50
  355.7 1.5 multiply_reduce_fusion.5
  357.9 0.3 fusion.40
  358.4 0.3 fusion.44
  359.0 0.3 fusion.45
  360.0 0.3 fusion.47
  360.6 0.3 fusion.48
  361.1 0.3 fusion.49
  361.7 0.3 fusion.50
  362.2 0.3 fusion.51
  362.7 0.3 fusion.52
  363.3 0.3 fusion.53
  364.4 2.3 multiply_reduce_fusion.1
  366.7 2.1 fusion.55
  368.9 2.3 fusion.1
  371.4 255.2 %all-reduce.15.cloned.1.call-done = (f32[100,100]{1,0:T(8,128)}, f32[100,100]{1,0:T(8,128)}, f32[100]{0:T(128)}) async-done(((f32[100,100]{1,0:T(8,128)}, f32[100,100]{1,0:T(8,128)}, f32[100]{0:T(128)}), (f32[100,100]{1,0:T(8,128)}, f32[100,100]{1,0:T(8,128)}, f32[100]{0:T(128)})) %all-reduce.15.cloned.1.call-update) | async-done | bytes 80416 | tf_op jit(solution)/shard_map/psum | solution.py:50
  626.6 1.5 multiply_reduce_fusion.4
  628.7 0.3 fusion.41
  629.3 0.3 fusion.56
  629.8 0.3 fusion.57
  630.4 0.3 fusion.58
  630.9 0.3 fusion.59
  631.4 0.3 fusion.60
  632.0 0.3 fusion.61
  633.1 0.3 fusion.63
  634.1 0.3 fusion.65
  634.7 0.3 fusion.66
  635.2 2.3 multiply_reduce_fusion
  637.6 2.1 fusion.67
  639.7 2.3 fusion.2
  642.0 0.3 all-reduce.11.cloned.1.call-start
  642.3 255.1 %all-reduce.13.cloned.1.call-done = (f32[100,100]{1,0:T(8,128)}, f32[100,100]{1,0:T(8,128)}, f32[100]{0:T(128)}) async-done(((f32[100,100]{1,0:T(8,128)}, f32[100,100]{1,0:T(8,128)}, f32[100]{0:T(128)}), (f32[100,100]{1,0:T(8,128)}, f32[100,100]{1,0:T(8,128)}, f32[100]{0:T(128)})) %all-reduce.13.cloned.1.call-update) | async-done | bytes 80416 | tf_op jit(solution)/shard_map/psum | solution.py:50
  897.5 1.5 multiply_reduce_fusion.3
  899.6 0.3 fusion.42
  901.8 0.3 fusion.71
  902.3 0.3 fusion.72
  903.9 0.3 fusion.75
  906.1 1.6 fusion.79
  907.7 4.7 convolution_multiply_fusion.1
  912.4 0.7 constant_dynamic-slice_fusion
  913.1 254.6 %all-reduce.11.cloned.1.call-done = f32[100,256]{1,0:T(8,128)} async-done(((f32[100,256]{1,0:T(8,128)}), f32[100,256]{1,0:T(8,128)}) %all-reduce.11.cloned.1.call-update) | async-done | bytes 102416 | tf_op jit(solution)/shard_map/psum | solution.py:58
  1167.8 1.5 copy.15
  (62 shorter events, 12.7 us)
Async XLA Ops:
  7.2 0.9 copy-start
  7.2 90.1 %all-reduce.9.cloned.1.call-start = ((), (), s32[]{:S(2)}) async-start(), calls=%async_computation | async-start | bytes 3407872 | tf_op jit(solution)/shard_map/psum | solution.py:47
  13.7 342.0 %all-reduce.17.cloned.1.call-start = ((), (), s32[]{:S(2)}) async-start(), calls=%async_computation.4 | async-start | bytes 214016 | tf_op jit(solution)/shard_map/psum | solution.py:50
  97.3 3.3 copy-start.1
  105.1 521.5 %all-reduce.15.cloned.1.call-start = ((), (), s32[]{:S(2)}) async-start(), calls=%async_computation.3 | async-start | bytes 214016 | tf_op jit(solution)/shard_map/psum | solution.py:50
  371.1 526.3 %all-reduce.13.cloned.1.call-start = ((), (), s32[]{:S(2)}) async-start(), calls=%async_computation.2 | async-start | bytes 214016 | tf_op jit(solution)/shard_map/psum | solution.py:50
  642.0 525.8 %all-reduce.11.cloned.1.call-start = ((), (), s32[]{:S(2)}) async-start(), calls=%async_computation.1 | async-start | bytes 212992 | tf_op jit(solution)/shard_map/psum | solution.py:58
  904.8 2.9 copy-start.2
Sparse Core Ops, SparseCore 0:
  13.8 83.4 all-reduce.8
  105.2 250.4 all-reduce.16
  371.3 255.2 all-reduce.14
  642.1 255.2 all-reduce.12
  912.6 255.1 all-reduce.10
where the time goes:
time: 1190 us; the launch traced here: 1180 us
  waiting for transfers between devices  1100 us (92%)
  matrix products  52.1 us (4%)
  between operations  16.4 us (1%)
    psum x3, waiting for transfers between devices, summer(): return lax.psum(terms, 'cells')  761 us
    psum x1, waiting for transfers between devices, on_device(): series = lax.psum(terms, 'cells')  255 us
    psum x1, waiting for transfers between devices, on_device(): loadings = lax.psum(partial_value, 'days')  83.6 us
  transfers between devices with their start and end apart: 5, of which 5 were waited for; matrix products, arithmetic and copies ran while one was open for 0% of the time, Pallas kernels for 0%

commit v1 on v0

v1 whole, which is shorter than its diff:
```python
import jax
import jax.numpy as jnp
from jax import lax
from jax.sharding import Mesh, PartitionSpec as P

ITERS = 3
NS_STEPS = 12
Z, X, Y, CORE = 16, 4, 4, 2
PLANE = ("x", "y", "core")
DAY = ("y", "core")
PAD = 128
N_PLANE = X * Y * CORE
ROWS = PAD // N_PLANE

HIGH = lax.Precision.HIGH


def dot(left, right):
    return jnp.dot(left, right, precision=HIGH, preferred_element_type=jnp.float32)


def rows_dot(left, right):
    return lax.dot_general(
        left, right, (((1,), (1,)), ((), ())), precision=HIGH, preferred_element_type=jnp.float32
    )


def cols_dot(left, right):
    return lax.dot_general(
        left, right, (((0,), (0,)), ((), ())), precision=HIGH, preferred_element_type=jnp.float32
    )


def polar(grad):
    x = grad / (jnp.sqrt(jnp.sum(grad * grad)) + 1e-06)
    for step in range(NS_STEPS):
        inner = cols_dot(x, x)
        x = 1.5 * x - 0.5 * dot(x, inner)
    return x


def swap(value, axes):
    return lax.all_to_all(value, axes, 0, 0)


def spread(value, count):
    return jnp.broadcast_to(value, (count,) + value.shape)


def plane_scatter(terms):
    k = terms[0].shape[0]
    padded = [jnp.pad(t, ((0, PAD - k), (0, PAD - k))).reshape(N_PLANE, ROWS, PAD) for t in terms]
    return jnp.sum(swap(jnp.concatenate(padded, axis=1), PLANE), axis=0)


def on_device(field, pcs):
    k, days_here = pcs.shape
    groups = Y * CORE
    days_total = days_here * groups
    share = field.shape[1] // groups
    cells_total = field.shape[1] * Z * X
    parts = jnp.stack([dot(pcs, field[:, g * share : (g + 1) * share]) for g in range(groups)])
    loadings = jnp.sum(swap(parts, DAY), axis=0) * (1.0 / days_total**0.5)

    every = lax.all_gather(loadings, DAY)

    cubed = loadings * loadings * loadings
    chunk = plane_scatter([rows_dot(loadings, cubed), rows_dot(loadings, loadings)])
    chunk = jnp.sum(swap(spread(chunk, Z), "z"), axis=0)
    got = swap(spread(chunk, N_PLANE), PLANE)
    cube = got[:, :ROWS].reshape(PAD, PAD)[:k, :k]
    corr = got[:, ROWS:].reshape(PAD, PAD)[:k, :k]
    colsq = jnp.sum(jnp.eye(k, dtype=jnp.float32) * corr, axis=0)
    rotation = polar(cube - corr * colsq[None, :] / cells_total)

    terms = sum(
        lax.dot_general(
            field[:, g * share : (g + 1) * share],
            every[g],
            (((1,), (1,)), ((), ())),
            precision=HIGH,
            preferred_element_type=jnp.float32,
        )
        for g in range(groups)
    ) * (days_total**0.5 / cells_total)
    piece = days_here // Z
    terms = jnp.pad(terms, ((0, 0), (0, PAD - k))).reshape(Z, piece, PAD)

    turned = cols_dot(rotation, loadings)
    chunk = plane_scatter([rows_dot(loadings, turned * turned * turned)])
    sent = jnp.concatenate([spread(chunk, Z), terms], axis=1)
    chunk = jnp.sum(swap(sent, "z"), axis=0)
    got = swap(spread(chunk, N_PLANE), PLANE)
    cube = got[:, :ROWS].reshape(PAD, PAD)[:k, :k]
    mine = lax.axis_index(DAY)
    terms = got[:, ROWS:].reshape(X, groups, piece, PAD)
    terms = jnp.sum(lax.dynamic_index_in_dim(terms, mine, 1, keepdims=False), axis=0)
    cross = dot(corr, rotation)
    colsq = jnp.sum(rotation * cross, axis=0)
    rotation = polar(cube - cross * colsq[None, :] / cells_total)

    turned = cols_dot(rotation, loadings)
    chunk = plane_scatter([rows_dot(loadings, turned * turned * turned)])
    got = swap(spread(jnp.concatenate([chunk, terms], axis=0), Z), "z")
    terms = got[:, ROWS:].reshape(days_here, PAD)[:, :k]
    chunk = jnp.sum(got[:, :ROWS], axis=0)
    got = swap(spread(chunk, N_PLANE), PLANE)
    cube = got.reshape(PAD, PAD)[:k, :k]
    cross = dot(corr, rotation)
    colsq = jnp.sum(rotation * cross, axis=0)
    rotation = polar(cube - cross * colsq[None, :] / cells_total)

    series = lax.dot_general(
        rotation, terms, (((0,), (1,)), ((), ())), precision=HIGH, preferred_element_type=jnp.float32
    )
    return (cols_dot(rotation, loadings), series)


def solution(mesh):
    split = Mesh(mesh.devices.reshape(Z, X, Y, CORE), ("z", "x", "y", "core"))
    placed = (P(DAY, ("z", "x")), P(None, DAY))
    return jax.shard_map(
        on_device,
        mesh=split,
        in_specs=placed,
        out_specs=(P(None, ("z", "x", "y", "core")), P(None, DAY)),
        check_vma=False,
    )
```

time: 1190 us -> 248 us (0.21); the launches traced: 1180 us -> 247 us
  waiting for transfers between devices: 1100 us -> 33.9 us
  blocking collectives: 0 us -> 122 us
  starting transfers between devices: 0.87 us -> 25.7 us
    psum x5 -> x0, waiting for transfers between devices: 1100 us -> none  [the longest x3 761 us: summer(): return lax.psum(terms, 'cells')]
    all_to_all x0 -> x6, blocking collectives: none -> 122 us  [swap(): return lax.all_to_all(value, axes, 0, 0)]
    all_to_all x0 -> x4, waiting for transfers between devices: none -> 31.5 us  [swap(): return lax.all_to_all(value, axes, 0, 0)]
    all_to_all x0 -> x4, starting transfers between devices: none -> 25.6 us  [swap(): return lax.all_to_all(value, axes, 0, 0)]
    dot_general x7 -> x4, matrix products: 17.9 us -> 1.03 us  [rows_dot(): lax.dot_general(left, right, (((1,), (1,)), ((), ())), precision=HIGH, pr...]
    dot_general x77 -> x94, matrix products: 34.2 us -> 41.2 us  [the longest x46 17.9 us: dot(): jnp.dot(left, right, precision=HIGH, preferred_element_type=jnp.float32)]
  transfers between devices with their start and end apart: 5 -> 5, of which waited for: 5 -> 5; matrix products, arithmetic and copies ran while one was open for 0% -> 3% of each run, Pallas kernels for 0% -> 0%
where the time goes in v1:
time: 248 us; the launch traced here: 247 us
  blocking collectives  122 us (49%)
  matrix products  42.3 us (17%)
  waiting for transfers between devices  33.9 us (14%)
  starting transfers between devices  25.7 us (10%)
  between operations  16.6 us (7%)
  local copies, waits for them, and re-layouts  3.85 us (2%)
  other arithmetic  3.02 us (1%)
    all_to_all x6, blocking collectives, swap(): return lax.all_to_all(value, axes, 0, 0)  122 us
    all_to_all x4, waiting for transfers between devices, swap(): return lax.all_to_all(value, axes, 0, 0)  31.5 us
    all_to_all x4, starting transfers between devices, swap(): return lax.all_to_all(value, axes, 0, 0)  25.6 us
    dot_general x46, matrix products, dot(): jnp.dot(left, right, precision=HIGH, preferred_element_type=jnp.float32)  17.9 us
    dot_general x8, matrix products, on_device(): lax.dot_general(field[:, g * share:(g + 1) * share], every[g], (((1,), (1...  11.8 us
    dot_general x39, matrix products, cols_dot(): lax.dot_general(left, right, (((0,), (0,)), ((), ())), precision=HIGH, pr...  10.7 us
  transfers between devices with their start and end apart: 5, of which 5 were waited for; matrix products, arithmetic and copies ran while one was open for 3% of the time, Pallas kernels for 0%

profile of v1, /device:TPU:1, one launch (start us, length us, event | category | flops | bytes accessed | tf_op | source)
XLA Modules:
  0.0 247.0 jit_solution(12986953723149635453)
XLA Ops:
  7.2 0.9 copy-done
  8.1 1.3 fusion.7
  9.4 1.3 fusion.6
  10.7 1.3 fusion.5
  12.1 1.3 fusion.4
  13.4 1.3 fusion.3
  14.7 1.3 fusion.2
  16.0 1.3 fusion.1
  17.4 1.3 fusion
  18.7 31.6 %all_to_all.50 = f32[8,100,512]{2,1,0:T(8,128)S(1)} all-to-all(f32[8,100,512]{2,1,0:T(8,128)S(1)} %fusion), channel_id=1, replica_groups=mesh['z'=16,'x'=4,'y'=4,'core'=2] {'y','core'}, dimensions={0} | all-to-all | bytes 3276800 | tf_op jit(solution)/shard_map/all_to_all | solution.py:43
  50.5 0.3 fusion.63
  51.1 11.3 %all_to_all.51 = f32[32,8,128]{2,1,0:T(8,128)S(1)} all-to-all(f32[32,8,128]{2,1,0:T(8,128)S(1)} %pad_maximum_fusion.1), channel_id=1, replica_groups=mesh['z'=16,'x'=4,'y'=4,'core'=2] {'x','y','core'}, dimensions={0} | all-to-all | bytes 262144 | tf_op jit(solution)/shard_map/all_to_all | solution.py:43
  62.5 24.9 %all_to_all.52 = f32[16,8,128]{2,1,0:T(8,128)S(1)} all-to-all(f32[16,8,128]{2,1,0:T(8,128)S(1)} %broadcast_in_dim.21), channel_id=1, replica_groups=mesh['z'=16,'x'=4,'y'=4,'core'=2] {'z'}, dimensions={0} | all-to-all | bytes 131072 | tf_op jit(solution)/shard_map/all_to_all | solution.py:43
  87.4 0.7 broadcast_in_dim.22
  88.1 5.6 %all-to-all-start.3 = ((f32[32,8,128]{2,1,0:T(8,128)}), f32[32,8,128]{2,1,0:T(8,128)S(1)}, u32[]{:S(2)}, u32[]{:S(2)}) async-start(f32[32,8,128]{2,1,0:T(8,128)} %broadcast_in_dim.22), calls=%async_computation.3 | async-start | bytes 262144 | tf_op jit(solution)/shard_map/all_to_all | solution.py:43
  93.7 0.7 multiply_bitcast_fusion
  94.5 7.0 %all-to-all-done.3 = f32[32,8,128]{2,1,0:T(8,128)S(1)} async-done(((f32[32,8,128]{2,1,0:T(8,128)}), f32[32,8,128]{2,1,0:T(8,128)S(1)}, u32[]{:S(2)}, u32[]{:S(2)}) %all-to-all-start.3) | async-done | bytes 131104 | tf_op jit(solution)/shard_map/all_to_all | solution.py:43
  101.6 0.6 multiply_reduce_fusion.4
  104.7 0.3 fusion.106
  108.2 0.3 fusion.73
  108.5 0.3 fusion.66
  108.8 10.9 %all_to_all.53 = f32[32,4,128]{2,1,0:T(4,128)S(1)} all-to-all(f32[32,4,128]{2,1,0:T(4,128)S(1)} %bitcast.227), channel_id=1, replica_groups=mesh['z'=16,'x'=4,'y'=4,'core'=2] {'x','y','core'}, dimensions={0} | all-to-all | bytes 131072 | tf_op jit(solution)/shard_map/all_to_all | solution.py:43
  119.8 2.4 all-gather.4.cloned.1.call-done
  122.2 1.7 fusion.60
  123.9 1.5 convolution_add_fusion.6
  125.4 1.4 convolution_add_fusion.5
  126.9 1.4 convolution_add_fusion.4
  128.3 1.4 convolution_add_fusion.3
  129.7 1.4 convolution_add_fusion.2
  131.2 1.4 convolution_add_fusion.1
  132.6 1.4 fusion.9
  134.2 24.6 %all_to_all.54 = f32[16,20,128]{2,1,0:T(8,128)S(1)} all-to-all(f32[16,20,128]{2,1,0:T(8,128)S(1)} %pad_maximum_fusion), channel_id=1, replica_groups=mesh['z'=16,'x'=4,'y'=4,'core'=2] {'z'}, dimensions={0} | all-to-all | bytes 327680 | tf_op jit(solution)/shard_map/all_to_all | solution.py:43
  158.8 0.8 broadcast_in_dim.24
  159.6 9.0 %all-to-all-start.6 = ((f32[32,20,128]{2,1,0:T(8,128)}), f32[32,20,128]{2,1,0:T(8,128)S(1)}, u32[]{:S(2)}, u32[]{:S(2)}) async-start(f32[32,20,128]{2,1,0:T(8,128)} %broadcast_in_dim.24), calls=%async_computation.6 | async-start | bytes 786432 | tf_op jit(solution)/shard_map/all_to_all | solution.py:43
  168.8 10.1 %all-to-all-done.6 = f32[32,20,128]{2,1,0:T(8,128)S(1)} async-done(((f32[32,20,128]{2,1,0:T(8,128)}), f32[32,20,128]{2,1,0:T(8,128)S(1)}, u32[]{:S(2)}, u32[]{:S(2)}) %all-to-all-start.6) | async-done | bytes 327712 | tf_op jit(solution)/shard_map/all_to_all | solution.py:43
  178.9 0.6 multiply_reduce_fusion.2
  185.6 0.3 fusion.70
  185.9 0.3 fusion.67
  186.2 0.6 pad.21
  186.8 3.6 %all-to-all-start.7 = ((f32[32,4,128]{2,1,0:T(4,128)}), f32[32,4,128]{2,1,0:T(4,128)S(1)}, u32[]{:S(2)}, u32[]{:S(2)}) async-start(f32[32,4,128]{2,1,0:T(4,128)} %bitcast.25), calls=%async_computation.7 | async-start | bytes 131072 | tf_op jit(solution)/shard_map/all_to_all | solution.py:43
  190.5 7.2 %all-to-all-done.7 = f32[32,4,128]{2,1,0:T(4,128)S(1)} async-done(((f32[32,4,128]{2,1,0:T(4,128)}), f32[32,4,128]{2,1,0:T(4,128)S(1)}, u32[]{:S(2)}, u32[]{:S(2)}) %all-to-all-start.7) | async-done | bytes 65568 | tf_op jit(solution)/shard_map/all_to_all | solution.py:43
  197.8 18.4 %all_to_all.55 = f32[16,20,128]{2,1,0:T(8,128)S(1)} all-to-all(f32[16,20,128]{2,1,0:T(8,128)S(1)} %broadcast_in_dim.25), channel_id=1, replica_groups=mesh['z'=16,'x'=4,'y'=4,'core'=2] {'z'}, dimensions={0} | all-to-all | bytes 327680 | tf_op jit(solution)/shard_map/all_to_all | solution.py:43
  216.2 0.6 broadcast_in_dim.26
  216.9 7.4 %all-to-all-start.9 = ((f32[32,4,128]{2,1,0:T(4,128)}), f32[32,4,128]{2,1,0:T(4,128)S(1)}, u32[]{:S(2)}, u32[]{:S(2)}) async-start(f32[32,4,128]{2,1,0:T(4,128)} %broadcast_in_dim.26), calls=%async_computation.9 | async-start | bytes 131072 | tf_op jit(solution)/shard_map/all_to_all | solution.py:43
  224.5 7.1 %all-to-all-done.9 = f32[32,4,128]{2,1,0:T(4,128)S(1)} async-done(((f32[32,4,128]{2,1,0:T(4,128)}), f32[32,4,128]{2,1,0:T(4,128)S(1)}, u32[]{:S(2)}, u32[]{:S(2)}) %all-to-all-start.9) | async-done | bytes 65568 | tf_op jit(solution)/shard_map/all_to_all | solution.py:43
  231.6 0.6 multiply_reduce_fusion
  238.3 1.0 fusion.78
  239.3 0.9 fusion.68
  (103 shorter events, 17.1 us)
Async XLA Ops:
  7.2 0.9 copy-start
  88.1 13.4 %all-to-all-start.3 = ((f32[32,8,128]{2,1,0:T(8,128)}), f32[32,8,128]{2,1,0:T(8,128)S(1)}, u32[]{:S(2)}, u32[]{:S(2)}) async-start(f32[32,8,128]{2,1,0:T(8,128)} %broadcast_in_dim.22), calls=%async_computation.3 | async-start | bytes 262144 | tf_op jit(solution)/shard_map/all_to_all | solution.py:43
  93.7 28.5 %all-gather.4.cloned.1.call-start = ((), (), s32[]{:S(2)}) async-start(), calls=%async_computation.10 | async-start | bytes 1916928 | tf_op jit(solution)/shard_map/all_gather | solution.py:65
  122.2 3.2 %copy-start.1 = (f32[8,100,512]{2,1,0:T(8,128)S(1)}, f32[8,100,512]{2,1,0:T(8,128)}, u32[]{:S(2)}) copy-start(f32[8,100,512]{2,1,0:T(8,128)} %all-gather.4.cloned.1.call-done) | copy-start | bytes 4915204
  159.6 19.3 %all-to-all-start.6 = ((f32[32,20,128]{2,1,0:T(8,128)}), f32[32,20,128]{2,1,0:T(8,128)S(1)}, u32[]{:S(2)}, u32[]{:S(2)}) async-start(f32[32,20,128]{2,1,0:T(8,128)} %broadcast_in_dim.24), calls=%async_computation.6 | async-start | bytes 786432 | tf_op jit(solution)/shard_map/all_to_all | solution.py:43
  186.8 10.9 %all-to-all-start.7 = ((f32[32,4,128]{2,1,0:T(4,128)}), f32[32,4,128]{2,1,0:T(4,128)S(1)}, u32[]{:S(2)}, u32[]{:S(2)}) async-start(f32[32,4,128]{2,1,0:T(4,128)} %bitcast.25), calls=%async_computation.7 | async-start | bytes 131072 | tf_op jit(solution)/shard_map/all_to_all | solution.py:43
  216.9 14.7 %all-to-all-start.9 = ((f32[32,4,128]{2,1,0:T(4,128)}), f32[32,4,128]{2,1,0:T(4,128)S(1)}, u32[]{:S(2)}, u32[]{:S(2)}) async-start(f32[32,4,128]{2,1,0:T(4,128)} %broadcast_in_dim.26), calls=%async_computation.9 | async-start | bytes 131072 | tf_op jit(solution)/shard_map/all_to_all | solution.py:43
Sparse Core Ops, SparseCore 0:
  97.2 24.9 all-gather.3

commit v2 on v0

v2 whole, which is shorter than its diff:
```python
import functools

import jax
import jax.numpy as jnp
from jax import lax
from jax.experimental import pallas as pl
from jax.experimental.pallas import tpu as pltpu
from jax.sharding import Mesh, PartitionSpec as P

ITERS = 3
NS_STEPS = 12
Z, X, Y, CORE = 16, 4, 4, 2
PLANE = ("x", "y", "core")
DAY = ("y", "core")
PAD = 128
N_PLANE = X * Y * CORE
ROWS = PAD // N_PLANE
F32 = jnp.float32
VMEM = pl.BlockSpec(memory_space=pltpu.VMEM)
LIMIT = 16 << 20
WIDE_LIMIT = 60 << 20


def split(value):
    high = value.astype(jnp.bfloat16)
    return high, (value - high.astype(F32)).astype(jnp.bfloat16)


def nn(left, right):
    return jnp.dot(left, right, preferred_element_type=F32)


def nt(left, right):
    return lax.dot_general(left, right, (((1,), (1,)), ((), ())), preferred_element_type=F32)


def fold(value):
    half = value.shape[1] // 2
    return value[:, :half] + value[:, half:]


def pad_rows(value, rows):
    return jnp.concatenate([value, jnp.zeros((rows - value.shape[0], value.shape[1]), F32)], axis=0)


def small_nn(left, right):
    lh, ll = split(left)
    rh, rl = split(right)
    both = jnp.concatenate([rh, rl], axis=1)
    return fold(nn(jnp.concatenate([lh, ll], axis=1), jnp.concatenate([both, both], axis=0)))


def rows_nt(left, right):
    lh, ll = split(left)
    rh, rl = split(right)
    return fold(nt(lh, jnp.concatenate([rh, rl], axis=0))) + nt(ll, rh)


def polar_rows(grad):
    norm = jnp.sqrt(jnp.sum(jnp.sum(grad * grad, axis=1, keepdims=True), axis=0, keepdims=True))
    y = grad / (norm + 1e-06)
    for step in range(NS_STEPS):
        high, low = split(y)
        down = jnp.concatenate([high, low], axis=0)
        across = jnp.concatenate([high, low], axis=1)
        inner = fold(nt(across, jnp.concatenate([down, down], axis=1)))
        ih, il = split(inner)
        again = jnp.concatenate([across, across], axis=0)
        y = 1.5 * y - 0.5 * fold(nn(jnp.concatenate([ih, il], axis=1), again))
    return y


def turn_cube(y, loadings):
    turned = small_nn(y, loadings)
    return rows_nt(turned * turned * turned, loadings)


def parts_kernel(scale, where_ref, pcs_ref, field_ref, out_ref, wide, left):
    half = wide.shape[0]

    @pl.when(pl.program_id(0) == 0)
    def _():
        wide[...] = jnp.zeros_like(wide)
        wide[0 : pcs_ref.shape[0]] = pcs_ref[...]
        high, low = split(wide[...])
        left[0:half] = high
        left[half : 2 * half] = low

    high, low = split(field_ref[...])
    both = nn(left[...], high)
    total = both[0:half] + both[half : 2 * half] + nn(left[0:half], low)
    out_ref[0] = total[0 : out_ref.shape[1]] * scale


def parts(field, pcs, core, scale):
    k, days = pcs.shape
    share = field.shape[1] // (Y * CORE)
    half = (k + 15) // 16 * 16
    rows = (k + 7) // 8 * 8
    return pl.pallas_call(
        functools.partial(parts_kernel, scale),
        out_shape=jax.ShapeDtypeStruct((Y, rows, share), F32),
        grid_spec=pltpu.PrefetchScalarGridSpec(
            num_scalar_prefetch=1,
            grid=(Y,),
            in_specs=[
                pl.BlockSpec((k, days), lambda g, where: (0, 0)),
                pl.BlockSpec((days, share), lambda g, where: (0, CORE * g + where[0])),
            ],
            out_specs=pl.BlockSpec((1, rows, share), lambda g, where: (g, 0, 0)),
            scratch_shapes=[pltpu.VMEM((half, days), F32), pltpu.VMEM((2 * half, days), jnp.bfloat16)],
        ),
        cost_estimate=pl.CostEstimate(
            flops=6 * k * days * share * Y, bytes_accessed=4 * Y * share * (days + k), transcendentals=0
        ),
        compiler_params=pltpu.CompilerParams(vmem_limit_bytes=WIDE_LIMIT),
    )(core, pcs, field)


def first_kernel(recv_ref, sent_ref, loadings_ref, padded_ref):
    loadings = recv_ref[0] + recv_ref[1] + recv_ref[2] + recv_ref[3]
    k = loadings.shape[0]
    padded_ref[...] = jnp.zeros_like(padded_ref)
    padded_ref[0:k] = loadings
    loadings_ref[...] = loadings
    loadings = padded_ref[...]
    sent_ref[0:PAD] = rows_nt(loadings * loadings * loadings, loadings)
    sent_ref[PAD : 2 * PAD] = rows_nt(loadings, loadings)


def first(recv):
    k, share = recv.shape[1:]
    return pl.pallas_call(
        first_kernel,
        out_shape=(
            jax.ShapeDtypeStruct((2 * PAD, PAD), F32),
            jax.ShapeDtypeStruct((k, share), F32),
            jax.ShapeDtypeStruct((PAD, share), F32),
        ),
        in_specs=[VMEM],
        out_specs=(VMEM, VMEM, VMEM),
        compiler_params=pltpu.CompilerParams(vmem_limit_bytes=LIMIT),
    )(recv)


def second_kernel(cells, got_ref, loadings_ref, sent_ref, y_ref):
    corr = got_ref[PAD : 2 * PAD]
    rows = lax.broadcasted_iota(jnp.int32, corr.shape, 0)
    columns = lax.broadcasted_iota(jnp.int32, corr.shape, 1)
    colsq = jnp.sum(jnp.where(rows == columns, corr, 0.0), axis=1, keepdims=True)
    y = polar_rows(got_ref[0:PAD] - corr * colsq * (1.0 / cells))
    y_ref[...] = y
    sent_ref[...] = turn_cube(y, loadings_ref[...])


def next_y(cells, cube_ref, got_ref, y_ref):
    y = y_ref[...]
    cross = small_nn(y, got_ref[PAD : 2 * PAD])
    colsq = jnp.sum(y * cross, axis=1, keepdims=True)
    return polar_rows(cube_ref[...] - cross * colsq * (1.0 / cells))


def third_kernel(cells, cube_ref, got_ref, y_ref, loadings_ref, sent_ref, out_ref):
    y = next_y(cells, cube_ref, got_ref, y_ref)
    out_ref[...] = y
    sent_ref[...] = turn_cube(y, loadings_ref[...])


def last_kernel(cells, cube_ref, got_ref, y_ref, loadings_ref, terms_ref, rotated_ref, series_ref):
    k = rotated_ref.shape[0]
    y = next_y(cells, cube_ref, got_ref, y_ref)
    rotated_ref[...] = small_nn(y, loadings_ref[...])[0:k]
    series_ref[...] = rows_nt(y, terms_ref[...])[0:k]


def whole(kernel, outs, *args):
    return pl.pallas_call(
        kernel,
        out_shape=tuple(jax.ShapeDtypeStruct(s, F32) for s in outs),
        in_specs=[VMEM] * len(args),
        out_specs=(VMEM,) * len(outs),
        compiler_params=pltpu.CompilerParams(vmem_limit_bytes=LIMIT),
    )(*args)


def terms_kernel(scale, where_ref, mine_ref, other_ref, near_ref, far_ref, out_ref):
    def product(field, loadings):
        high, low = split(field)
        lh, ll = split(pad_rows(loadings, PAD))
        return fold(nt(high, jnp.concatenate([lh, ll], axis=0))) + nt(low, lh)

    total = product(mine_ref[...], near_ref[0]) + product(other_ref[...], far_ref[0])
    g = pl.program_id(0)

    @pl.when(g == 0)
    def _():
        out_ref[...] = total * scale

    @pl.when(g > 0)
    def _():
        out_ref[...] += total * scale


def series_terms(field, near, far, where, scale):
    days = field.shape[0]
    rows, share = near.shape[1:]
    mine = lambda d, where: (0, lax.rem(where[0] + Y - d, Y) * CORE + where[1])
    other = lambda d, where: (0, lax.rem(where[0] + Y - d, Y) * CORE + 1 - where[1])
    return pl.pallas_call(
        functools.partial(terms_kernel, scale),
        out_shape=jax.ShapeDtypeStruct((days, PAD), F32),
        grid_spec=pltpu.PrefetchScalarGridSpec(
            num_scalar_prefetch=1,
            grid=(Y,),
            in_specs=[
                pl.BlockSpec((days, share), mine),
                pl.BlockSpec((days, share), other),
                pl.BlockSpec((1, rows, share), lambda d, where: (d, 0, 0)),
                pl.BlockSpec((1, rows, share), lambda d, where: (d, 0, 0)),
            ],
            out_specs=pl.BlockSpec((days, PAD), lambda d, where: (0, 0)),
        ),
        cost_estimate=pl.CostEstimate(
            flops=6 * days * PAD * share * Y * CORE,
            bytes_accessed=4 * Y * CORE * share * (days + rows),
            transcendentals=0,
        ),
        compiler_params=pltpu.CompilerParams(vmem_limit_bytes=WIDE_LIMIT),
    )(where, field, field, near, far)


def swap(value, axes):
    return lax.all_to_all(value, axes, 0, 0)


def spread(value, count):
    return jnp.broadcast_to(value, (count,) + value.shape)


def on_device(field, pcs):
    k, days_here = pcs.shape
    groups = Y * CORE
    days_total = days_here * groups
    cells_total = field.shape[1] * Z * X
    share = field.shape[1] // groups
    core = lax.axis_index("core").astype(jnp.int32)
    row = lax.axis_index("y").astype(jnp.int32)

    scale = 1.0 / days_total**0.5
    theirs = lax.ppermute(parts(field, pcs, (1 - core)[None], scale), "core", [(0, 1), (1, 0)])
    recv = swap(theirs + parts(field, pcs, core[None], scale), "y")
    sent, narrow, loadings = first(recv)

    chunk = swap(sent.reshape(N_PLANE, 2 * ROWS, PAD), PLANE)
    near = [lax.ppermute(narrow, "y", [(i, (i + d) % Y) for i in range(Y)]) for d in range(1, Y)]
    chunk, near = lax.optimization_barrier((chunk, near))
    near = jnp.stack([narrow] + near)
    far = lax.ppermute(near, "core", [(0, 1), (1, 0)])
    chunk = swap(spread(jnp.sum(chunk, axis=0), Z), "z")
    chunk, near, far = lax.optimization_barrier((chunk, near, far))
    terms = series_terms(field, near, far, jnp.stack([row, core]), days_total**0.5 / cells_total)
    base = swap(spread(jnp.sum(chunk, axis=0), N_PLANE), PLANE)
    base, terms = lax.optimization_barrier((base, terms))
    base = base.reshape(2 * PAD, PAD)
    piece = days_here // Z
    sent, y = whole(functools.partial(second_kernel, cells_total), [(PAD, PAD)] * 2, base, loadings)

    chunk = jnp.sum(swap(sent.reshape(N_PLANE, ROWS, PAD), PLANE), axis=0)
    both = jnp.concatenate([spread(chunk, Z), terms.reshape(Z, piece, PAD)], axis=1)
    both = jnp.sum(swap(both, "z"), axis=0)
    got = swap(spread(both, N_PLANE), PLANE)
    cube = got[:, :ROWS].reshape(PAD, PAD)
    terms = got[:, ROWS:].reshape(X, groups, piece, PAD)
    terms = jnp.sum(lax.dynamic_index_in_dim(terms, row * CORE + core, 1, keepdims=False), axis=0)
    sent, y = whole(
        functools.partial(third_kernel, cells_total), [(PAD, PAD)] * 2, cube, base, y, loadings
    )

    chunk = jnp.sum(swap(sent.reshape(N_PLANE, ROWS, PAD), PLANE), axis=0)
    got = swap(spread(jnp.concatenate([chunk, terms], axis=0), Z), "z")
    terms = got[:, ROWS:].reshape(days_here, PAD)
    chunk = jnp.sum(got[:, :ROWS], axis=0)
    cube = swap(spread(chunk, N_PLANE), PLANE).reshape(PAD, PAD)
    return whole(
        functools.partial(last_kernel, cells_total),
        [(k, share), (k, days_here)],
        cube, base, y, loadings, terms,
    )


def solution(mesh):
    split_mesh = Mesh(mesh.devices.reshape(Z, X, Y, CORE), ("z", "x", "y", "core"))
    placed = (P(DAY, ("z", "x")), P(None, DAY))
    return jax.shard_map(
        on_device,
        mesh=split_mesh,
        in_specs=placed,
        out_specs=(P(None, ("z", "x", "y", "core")), P(None, DAY)),
        check_vma=False,
    )
```

time: 1190 us -> 205 us (0.17); the launches traced: 1180 us -> 204 us
  waiting for transfers between devices: 1100 us -> 27.9 us
  blocking collectives: 0 us -> 92.2 us
  matrix products: 52.1 us -> 0 us
  starting transfers between devices: 0.87 us -> 49.6 us
  Pallas kernels: 0 us -> 28.6 us
  between operations: 16.4 us -> 0.82 us
    psum x5 -> x0, waiting for transfers between devices: 1100 us -> none  [the longest x3 761 us: summer(): return lax.psum(terms, 'cells')]
    all_to_all x0 -> x6, blocking collectives: none -> 92.2 us  [swap(): return lax.all_to_all(value, axes, 0, 0)]
    dot_general x84 -> x0, matrix products: 52.1 us -> none  [the longest x7 17.9 us: rows_dot(): lax.dot_general(left, right, (((1,), (1,)), ((), ())), precision=HIGH, pr...]
    all_to_all x0 -> x4, starting transfers between devices: none -> 30.1 us  [swap(): return lax.all_to_all(value, axes, 0, 0)]
    pallas_call x0 -> x7, Pallas kernels: none -> 28.6 us  [the longest x3 14.5 us: whole(): pl.pallas_call(kernel, out_shape=tuple((jax.ShapeDtypeStruct(s, F32) for...]
    all_to_all x0 -> x4, waiting for transfers between devices: none -> 27.9 us  [swap(): return lax.all_to_all(value, axes, 0, 0)]
    ppermute x0 -> x5, starting transfers between devices: none -> 19.5 us  [the longest x1 8.77 us: on_device(): lax.ppermute(parts(field, pcs, (1 - core)[None], scale), 'core', [(0, 1),...]
  transfers between devices with their start and end apart: 5 -> 9, of which waited for: 5 -> 4; matrix products, arithmetic and copies ran while one was open for 0% -> 1% of each run, Pallas kernels for 0% -> 5%
where the time goes in v2:
time: 205 us; the launch traced here: 204 us
  blocking collectives  92.2 us (45%)
  starting transfers between devices  49.6 us (24%)
  Pallas kernels  28.6 us (14%)
  waiting for transfers between devices  27.9 us (14%)
  other arithmetic  3.09 us (2%)
  local copies, waits for them, and re-layouts  2.12 us (1%)
    all_to_all x6, blocking collectives, swap(): return lax.all_to_all(value, axes, 0, 0)  92.2 us
    all_to_all x4, starting transfers between devices, swap(): return lax.all_to_all(value, axes, 0, 0)  30.1 us
    all_to_all x4, waiting for transfers between devices, swap(): return lax.all_to_all(value, axes, 0, 0)  27.9 us
    pallas_call x3, Pallas kernels, whole(): pl.pallas_call(kernel, out_shape=tuple((jax.ShapeDtypeStruct(s, F32) for...  14.5 us
    ppermute x1, starting transfers between devices, on_device(): lax.ppermute(parts(field, pcs, (1 - core)[None], scale), 'core', [(0, 1),...  8.77 us
    ppermute x3, starting transfers between devices, on_device(): lax.ppermute(narrow, 'y', [(i, (i + d) % Y) for i in range(Y)])  8.42 us
    pallas_call x2, Pallas kernels, parts(): pl.pallas_call(functools.partial(parts_kernel, scale), out_shape=jax.Shap...  8.11 us
    pallas_call x1, Pallas kernels, series_terms(): pl.pallas_call(functools.partial(terms_kernel, scale), out_shape=jax.Shap...  5.52 us
  transfers between devices with their start and end apart: 9, of which 4 were waited for; matrix products, arithmetic and copies ran while one was open for 1% of the time, Pallas kernels for 5%

profile of v2, /device:TPU:1, one launch (start us, length us, event | category | flops | bytes accessed | tf_op | source)
XLA Modules:
  0.0 204.4 jit_solution(8399392946246454304)
XLA Ops:
  0.6 4.1 %shard_map.41 = f32[4,104,512]{2,1,0:T(8,128)} custom-call(s32[1]{0:T(128)} %bitcast.where_ref, f32[100,256]{1,0:T(8,128)} %pcs_ref.3, f32[256,4096]{1,0:T(8,128)} %other_ref.1), custom_call_target="tpu_custom_call" | custom-call | flops 314572800 | bytes 2916352 | tf_op jit(solution)/shard_map/pallas_call | solution.py:100
  4.7 8.8 %collective-permute-start = (f32[4,104,512]{2,1,0:T(8,128)}, f32[4,104,512]{2,1,0:T(8,128)S(1)}, u32[]{:S(2)}, u32[]{:S(2)}) collective-permute-start(f32[4,104,512]{2,1,0:T(8,128)} %shard_map.41), channel_id=1, source_target_pairs={{0,1},{1,0},{2,3},{3,2},{4,5},{5,4},{6,7},{7,6},{8,9},{9,8},{10,11... | collective-permute-start | bytes 2555912 | tf_op jit(solution)/shard_map/ppermute | solution.py:250
  13.5 4.1 %shard_map.42 = f32[4,104,512]{2,1,0:T(8,128)} custom-call(s32[1]{0:T(128)} %bitcast.1.where_ref, f32[100,256]{1,0:T(8,128)} %pcs_ref.3, f32[256,4096]{1,0:T(8,128)} %other_ref.1), custom_call_target="tpu_custom_call" | custom-call | flops 314572800 | bytes 2916352 | tf_op jit(solution)/shard_map/pallas_call | solution.py:100
  17.5 0.0 collective-permute-done
  17.5 1.3 add.10
  18.8 15.5 %all_to_all.50.recv_ref = f32[4,104,512]{2,1,0:T(8,128)S(1)} all-to-all(f32[4,104,512]{2,1,0:T(8,128)S(1)} %add.10), channel_id=1, replica_groups=mesh['z'=16,'x'=4,'y'=4,'core'=2] {'y'}, dimensions={0} | all-to-all | bytes 1703936 | tf_op jit(solution)/shard_map/all_to_all | solution.py:233
  34.4 0.4 shard_map.43
  34.8 2.2 %collective-permute-start.1 = (f32[104,512]{1,0:T(8,128)S(1)}, f32[104,512]{1,0:T(8,128)S(1)}, u32[]{:S(2)}, u32[]{:S(2)}) collective-permute-start(f32[104,512]{1,0:T(8,128)S(1)} %get-tuple-element.19), channel_id=1, source_target_pairs={{0,2},{2,4},{4,6},{6,0},{1,3},{3,5},{5,7},{7,1},{8,10},{10,12},{12... | collective-permute-start | bytes 638984 | tf_op jit(solution)/shard_map/ppermute | solution.py:255
  37.0 3.7 %collective-permute-start.2 = (f32[104,512]{1,0:T(8,128)S(1)}, f32[104,512]{1,0:T(8,128)S(1)}, u32[]{:S(2)}, u32[]{:S(2)}) collective-permute-start(f32[104,512]{1,0:T(8,128)S(1)} %get-tuple-element.19), channel_id=1, source_target_pairs={{0,4},{2,6},{4,0},{6,2},{1,5},{3,7},{5,1},{7,3},{8,12},{10,14},{12... | collective-permute-start | bytes 638984 | tf_op jit(solution)/shard_map/ppermute | solution.py:255
  40.7 2.5 %collective-permute-start.3 = (f32[104,512]{1,0:T(8,128)S(1)}, f32[104,512]{1,0:T(8,128)S(1)}, u32[]{:S(2)}, u32[]{:S(2)}) collective-permute-start(f32[104,512]{1,0:T(8,128)S(1)} %get-tuple-element.19), channel_id=1, source_target_pairs={{0,6},{2,0},{4,2},{6,4},{1,7},{3,1},{5,3},{7,5},{8,14},{10,8},{12,... | collective-permute-start | bytes 638984 | tf_op jit(solution)/shard_map/ppermute | solution.py:255
  43.2 13.2 %all_to_all.51 = f32[32,8,128]{2,1,0:T(8,128)S(1)} all-to-all(f32[32,8,128]{2,1,0:T(8,128)S(1)} %bitcast.23), channel_id=1, replica_groups=mesh['z'=16,'x'=4,'y'=4,'core'=2] {'x','y','core'}, dimensions={0} | all-to-all | bytes 262144 | tf_op jit(solution)/shard_map/all_to_all | solution.py:233
  56.4 0.0 collective-permute-done.1
  56.4 0.0 collective-permute-done.2
  56.4 0.0 collective-permute-done.3
  56.4 0.1 pad_maximum_fusion.near_ref
  56.5 0.0 copy-start
  56.5 2.3 %collective-permute-start.4 = (f32[4,104,512]{2,1,0:T(8,128)S(1)}, f32[4,104,512]{2,1,0:T(8,128)S(1)}, u32[]{:S(2)}, u32[]{:S(2)}) collective-permute-start(f32[4,104,512]{2,1,0:T(8,128)S(1)} %pad_maximum_fusion.near_ref), channel_id=1, source_target_pairs={{0,1},{1,0},{2,3},{3,2},{4,5},{5,4},{6,7},{7,6},{8,9},{9,8},{10,11... | collective-permute-start | bytes 2555912 | tf_op jit(solution)/shard_map/ppermute | solution.py:258
  58.9 0.6 broadcast_in_dim.26
  59.5 13.6 %all-to-all-start.2 = ((f32[16,8,128]{2,1,0:T(8,128)}), f32[16,8,128]{2,1,0:T(8,128)S(1)}, u32[]{:S(2)}, u32[]{:S(2)}) async-start(f32[16,8,128]{2,1,0:T(8,128)} %broadcast_in_dim.26), calls=%async_computation.2 | async-start | bytes 131072 | tf_op jit(solution)/shard_map/all_to_all | solution.py:233
  73.1 11.6 %all-to-all-done.2 = f32[16,8,128]{2,1,0:T(8,128)S(1)} async-done(((f32[16,8,128]{2,1,0:T(8,128)}), f32[16,8,128]{2,1,0:T(8,128)S(1)}, u32[]{:S(2)}, u32[]{:S(2)}) %all-to-all-start.2) | async-done | bytes 65568 | tf_op jit(solution)/shard_map/all_to_all | solution.py:233
  84.7 0.0 collective-permute-done.4.far_ref
  84.8 0.0 copy-start.1
  84.8 0.7 broadcast_in_dim.27
  85.5 5.5 %all-to-all-start.3 = ((f32[32,8,128]{2,1,0:T(8,128)}), f32[32,8,128]{2,1,0:T(8,128)S(1)}, u32[]{:S(2)}, u32[]{:S(2)}) async-start(f32[32,8,128]{2,1,0:T(8,128)} %broadcast_in_dim.27), calls=%async_computation.3 | async-start | bytes 262144 | tf_op jit(solution)/shard_map/all_to_all | solution.py:233
  91.0 0.6 pad_add_fusion.where_ref
  91.6 0.0 copy-done
  91.6 0.0 copy-done.1
  91.6 5.5 %shard_map.44 = f32[256,128]{1,0:T(8,128)} custom-call(s32[2]{0:T(128)} %pad_add_fusion.where_ref, f32[256,4096]{1,0:T(8,128)} %other_ref.1, f32[256,4096]{1,0:T(8,128)} %other_ref.1, f32[4,104,512]{2,1,0:T(8,128)} %copy-done, f32[4,104,512]{2,1,0:T(8,128)} %copy-done.1), custom_call_target="tpu_custom_call" | custom-call | flops 805306368 | bytes 5898240 | tf_op jit(solution)/shard_map/pallas_call | solution.py:209
  97.2 1.7 all-to-all-done.3
  98.9 4.3 %shard_map.45 = (f32[128,128]{1,0:T(8,128)S(1)}, f32[128,128]{1,0:T(8,128)S(1)}) custom-call(f32[256,128]{1,0:T(8,128)S(1)} %bitcast.16, f32[128,512]{1,0:T(8,128)S(1)} %get-tuple-element.28.loadings_ref), custom_call_target="tpu_custom_call" | custom-call | tf_op jit(solution)/shard_map/pallas_call | solution.py:177
  103.2 13.0 %all_to_all.52 = f32[32,4,128]{2,1,0:T(4,128)S(1)} all-to-all(f32[32,4,128]{2,1,0:T(4,128)S(1)} %bitcast.24), channel_id=1, replica_groups=mesh['z'=16,'x'=4,'y'=4,'core'=2] {'x','y','core'}, dimensions={0} | all-to-all | bytes 131072 | tf_op jit(solution)/shard_map/all_to_all | solution.py:233
  116.2 0.9 pad_maximum_fusion.1
  117.2 15.5 %all_to_all.53 = f32[16,20,128]{2,1,0:T(8,128)S(1)} all-to-all(f32[16,20,128]{2,1,0:T(8,128)S(1)} %pad_maximum_fusion.1), channel_id=1, replica_groups=mesh['z'=16,'x'=4,'y'=4,'core'=2] {'z'}, dimensions={0} | all-to-all | bytes 327680 | tf_op jit(solution)/shard_map/all_to_all | solution.py:233
  132.7 17.4 %all_to_all.54 = f32[32,20,128]{2,1,0:T(8,128)S(1)} all-to-all(f32[32,20,128]{2,1,0:T(8,128)S(1)} %broadcast_in_dim.29), channel_id=1, replica_groups=mesh['z'=16,'x'=4,'y'=4,'core'=2] {'x','y','core'}, dimensions={0} | all-to-all | bytes 655360 | tf_op jit(solution)/shard_map/all_to_all | solution.py:233
  150.1 5.1 %shard_map.46 = (f32[128,128]{1,0:T(8,128)}, f32[128,128]{1,0:T(8,128)S(1)}) custom-call(f32[128,128]{1,0:T(8,128)S(1)} %bitcast.21, f32[256,128]{1,0:T(8,128)S(1)} %bitcast.17, f32[128,128]{1,0:T(8,128)S(1)} %get-tuple-element.31.y_ref, f32[128,512]{1,0:T(8,128)S(1)} %get-tuple-element.28.loadings_ref), custom_call_target="tpu_custom_call" | custom-call | tf_op jit(solution)/shard_map/pallas_call | solution.py:177
  155.3 3.6 %all-to-all-start.7 = ((f32[32,4,128]{2,1,0:T(4,128)}), f32[32,4,128]{2,1,0:T(4,128)S(1)}, u32[]{:S(2)}, u32[]{:S(2)}) async-start(f32[32,4,128]{2,1,0:T(4,128)} %bitcast.12), calls=%async_computation.7 | async-start | bytes 131072 | tf_op jit(solution)/shard_map/all_to_all | solution.py:233
  159.0 7.2 %all-to-all-done.7 = f32[32,4,128]{2,1,0:T(4,128)S(1)} async-done(((f32[32,4,128]{2,1,0:T(4,128)}), f32[32,4,128]{2,1,0:T(4,128)S(1)}, u32[]{:S(2)}, u32[]{:S(2)}) %all-to-all-start.7) | async-done | bytes 65568 | tf_op jit(solution)/shard_map/all_to_all | solution.py:233
  166.3 17.7 %all_to_all.55 = f32[16,20,128]{2,1,0:T(8,128)S(1)} all-to-all(f32[16,20,128]{2,1,0:T(8,128)S(1)} %broadcast_in_dim.30), channel_id=1, replica_groups=mesh['z'=16,'x'=4,'y'=4,'core'=2] {'z'}, dimensions={0} | all-to-all | bytes 327680 | tf_op jit(solution)/shard_map/all_to_all | solution.py:233
  183.9 0.6 broadcast_in_dim.31
  184.6 7.4 %all-to-all-start.9 = ((f32[32,4,128]{2,1,0:T(4,128)}), f32[32,4,128]{2,1,0:T(4,128)S(1)}, u32[]{:S(2)}, u32[]{:S(2)}) async-start(f32[32,4,128]{2,1,0:T(4,128)} %broadcast_in_dim.31), calls=%async_computation.9 | async-start | bytes 131072 | tf_op jit(solution)/shard_map/all_to_all | solution.py:233
  192.0 7.3 %all-to-all-done.9 = f32[32,4,128]{2,1,0:T(4,128)S(1)} async-done(((f32[32,4,128]{2,1,0:T(4,128)}), f32[32,4,128]{2,1,0:T(4,128)S(1)}, u32[]{:S(2)}, u32[]{:S(2)}) %all-to-all-start.9) | async-done | bytes 65568 | tf_op jit(solution)/shard_map/all_to_all | solution.py:233
  199.3 5.1 %shard_map.47 = (f32[100,512]{1,0:T(8,128)}, f32[100,256]{1,0:T(8,128)}) custom-call(f32[128,128]{1,0:T(8,128)S(1)} %bitcast.20, f32[256,128]{1,0:T(8,128)S(1)} %bitcast.18, f32[128,128]{1,0:T(8,128)S(1)} %get-tuple-element.33.y_ref, f32[128,512]{1,0:T(8,128)S(1)} %get-tuple-element.28.loadings_ref, f32[256,128]{1,0:T(8,128)S(1)} %bitcast.19), custom_call_target="tpu_custom_call" | custom-call | tf_op jit(solution)/shard_map/pallas_call | solution.py:177
  (14 shorter events, 0.3 us)
Async XLA Ops:
  4.7 12.8 %collective-permute-start = (f32[4,104,512]{2,1,0:T(8,128)}, f32[4,104,512]{2,1,0:T(8,128)S(1)}, u32[]{:S(2)}, u32[]{:S(2)}) collective-permute-start(f32[4,104,512]{2,1,0:T(8,128)} %shard_map.41), channel_id=1, source_target_pairs={{0,1},{1,0},{2,3},{3,2},{4,5},{5,4},{6,7},{7,6},{8,9},{9,8},{10,11... | collective-permute-start | bytes 2555912 | tf_op jit(solution)/shard_map/ppermute | solution.py:250
  34.8 21.6 %collective-permute-start.1 = (f32[104,512]{1,0:T(8,128)S(1)}, f32[104,512]{1,0:T(8,128)S(1)}, u32[]{:S(2)}, u32[]{:S(2)}) collective-permute-start(f32[104,512]{1,0:T(8,128)S(1)} %get-tuple-element.19), channel_id=1, source_target_pairs={{0,2},{2,4},{4,6},{6,0},{1,3},{3,5},{5,7},{7,1},{8,10},{10,12},{12... | collective-permute-start | bytes 638984 | tf_op jit(solution)/shard_map/ppermute | solution.py:255
  37.0 19.4 %collective-permute-start.2 = (f32[104,512]{1,0:T(8,128)S(1)}, f32[104,512]{1,0:T(8,128)S(1)}, u32[]{:S(2)}, u32[]{:S(2)}) collective-permute-start(f32[104,512]{1,0:T(8,128)S(1)} %get-tuple-element.19), channel_id=1, source_target_pairs={{0,4},{2,6},{4,0},{6,2},{1,5},{3,7},{5,1},{7,3},{8,12},{10,14},{12... | collective-permute-start | bytes 638984 | tf_op jit(solution)/shard_map/ppermute | solution.py:255
  40.7 15.7 %collective-permute-start.3 = (f32[104,512]{1,0:T(8,128)S(1)}, f32[104,512]{1,0:T(8,128)S(1)}, u32[]{:S(2)}, u32[]{:S(2)}) collective-permute-start(f32[104,512]{1,0:T(8,128)S(1)} %get-tuple-element.19), channel_id=1, source_target_pairs={{0,6},{2,0},{4,2},{6,4},{1,7},{3,1},{5,3},{7,5},{8,14},{10,8},{12,... | collective-permute-start | bytes 638984 | tf_op jit(solution)/shard_map/ppermute | solution.py:255
  56.5 35.1 %copy-start = (f32[4,104,512]{2,1,0:T(8,128)}, f32[4,104,512]{2,1,0:T(8,128)S(1)}, u32[]{:S(2)}) copy-start(f32[4,104,512]{2,1,0:T(8,128)S(1)} %pad_maximum_fusion.near_ref) | copy-start | bytes 2555908
  56.5 28.2 %collective-permute-start.4 = (f32[4,104,512]{2,1,0:T(8,128)S(1)}, f32[4,104,512]{2,1,0:T(8,128)S(1)}, u32[]{:S(2)}, u32[]{:S(2)}) collective-permute-start(f32[4,104,512]{2,1,0:T(8,128)S(1)} %pad_maximum_fusion.near_ref), channel_id=1, source_target_pairs={{0,1},{1,0},{2,3},{3,2},{4,5},{5,4},{6,7},{7,6},{8,9},{9,8},{10,11... | collective-permute-start | bytes 2555912 | tf_op jit(solution)/shard_map/ppermute | solution.py:258
  59.5 25.2 %all-to-all-start.2 = ((f32[16,8,128]{2,1,0:T(8,128)}), f32[16,8,128]{2,1,0:T(8,128)S(1)}, u32[]{:S(2)}, u32[]{:S(2)}) async-start(f32[16,8,128]{2,1,0:T(8,128)} %broadcast_in_dim.26), calls=%async_computation.2 | async-start | bytes 131072 | tf_op jit(solution)/shard_map/all_to_all | solution.py:233
  84.8 6.9 %copy-start.1 = (f32[4,104,512]{2,1,0:T(8,128)}, f32[4,104,512]{2,1,0:T(8,128)S(1)}, u32[]{:S(2)}) copy-start(f32[4,104,512]{2,1,0:T(8,128)S(1)} %collective-permute-done.4.far_ref) | copy-start | bytes 2555908
  85.5 13.4 %all-to-all-start.3 = ((f32[32,8,128]{2,1,0:T(8,128)}), f32[32,8,128]{2,1,0:T(8,128)S(1)}, u32[]{:S(2)}, u32[]{:S(2)}) async-start(f32[32,8,128]{2,1,0:T(8,128)} %broadcast_in_dim.27), calls=%async_computation.3 | async-start | bytes 262144 | tf_op jit(solution)/shard_map/all_to_all | solution.py:233
  155.3 10.9 %all-to-all-start.7 = ((f32[32,4,128]{2,1,0:T(4,128)}), f32[32,4,128]{2,1,0:T(4,128)S(1)}, u32[]{:S(2)}, u32[]{:S(2)}) async-start(f32[32,4,128]{2,1,0:T(4,128)} %bitcast.12), calls=%async_computation.7 | async-start | bytes 131072 | tf_op jit(solution)/shard_map/all_to_all | solution.py:233
  184.6 14.7 %all-to-all-start.9 = ((f32[32,4,128]{2,1,0:T(4,128)}), f32[32,4,128]{2,1,0:T(4,128)S(1)}, u32[]{:S(2)}, u32[]{:S(2)}) async-start(f32[32,4,128]{2,1,0:T(4,128)} %broadcast_in_dim.31), calls=%async_computation.9 | async-start | bytes 131072 | tf_op jit(solution)/shard_map/all_to_all | solution.py:233

commit v3 on v2

--- a/solution.py
+++ b/solution.py
@@ -17,8 +17,7 @@
 ROWS = PAD // N_PLANE
 F32 = jnp.float32
 VMEM = pl.BlockSpec(memory_space=pltpu.VMEM)
-LIMIT = 16 << 20
-WIDE_LIMIT = 60 << 20
+LIMIT = 24 << 20
 
 
 def split(value):
@@ -75,21 +74,21 @@
     return rows_nt(turned * turned * turned, loadings)
 
 
-def parts_kernel(scale, where_ref, pcs_ref, field_ref, out_ref, wide, left):
+def columns(field_ref, group, share):
+    return field_ref[:, pl.ds(pl.multiple_of(group * share, share), share)]
+
+
+def parts_kernel(scale, core_ref, pcs_ref, field_ref, out_ref, wide):
+    wide[...] = jnp.zeros_like(wide)
+    wide[0 : pcs_ref.shape[0]] = pcs_ref[...] * scale
     half = wide.shape[0]
-
-    @pl.when(pl.program_id(0) == 0)
-    def _():
-        wide[...] = jnp.zeros_like(wide)
-        wide[0 : pcs_ref.shape[0]] = pcs_ref[...]
-        high, low = split(wide[...])
-        left[0:half] = high
-        left[half : 2 * half] = low
-
-    high, low = split(field_ref[...])
-    both = nn(left[...], high)
-    total = both[0:half] + both[half : 2 * half] + nn(left[0:half], low)
-    out_ref[0] = total[0 : out_ref.shape[1]] * scale
+    left_high, left_low = split(wide[...])
+    left = jnp.concatenate([left_high, left_low], axis=0)
+    for g in range(Y):
+        high, low = split(columns(field_ref, CORE * g + core_ref[0], out_ref.shape[2]))
+        both = nn(left, high)
+        total = both[0:half] + both[half : 2 * half] + nn(left_high, low)
+        out_ref[g] = total[0 : out_ref.shape[1]]
 
 
 def parts(field, pcs, core, scale):
@@ -100,20 +99,13 @@
     return pl.pallas_call(
         functools.partial(parts_kernel, scale),
         out_shape=jax.ShapeDtypeStruct((Y, rows, share), F32),
-        grid_spec=pltpu.PrefetchScalarGridSpec(
-            num_scalar_prefetch=1,
-            grid=(Y,),
-            in_specs=[
-                pl.BlockSpec((k, days), lambda g, where: (0, 0)),
-                pl.BlockSpec((days, share), lambda g, where: (0, CORE * g + where[0])),
-            ],
-            out_specs=pl.BlockSpec((1, rows, share), lambda g, where: (g, 0, 0)),
-            scratch_shapes=[pltpu.VMEM((half, days), F32), pltpu.VMEM((2 * half, days), jnp.bfloat16)],
-        ),
+        in_specs=[pl.BlockSpec(memory_space=pltpu.SMEM), VMEM, VMEM],
+        out_specs=VMEM,
+        scratch_shapes=[pltpu.VMEM((half, days), F32)],
         cost_estimate=pl.CostEstimate(
             flops=6 * k * days * share * Y, bytes_accessed=4 * Y * share * (days + k), transcendentals=0
         ),
-        compiler_params=pltpu.CompilerParams(vmem_limit_bytes=WIDE_LIMIT),
+        compiler_params=pltpu.CompilerParams(vmem_limit_bytes=LIMIT),
     )(core, pcs, field)
 
 
@@ -183,50 +175,34 @@
     )(*args)
 
 
-def terms_kernel(scale, where_ref, mine_ref, other_ref, near_ref, far_ref, out_ref):
-    def product(field, loadings):
-        high, low = split(field)
-        lh, ll = split(pad_rows(loadings, PAD))
-        return fold(nt(high, jnp.concatenate([lh, ll], axis=0))) + nt(low, lh)
-
-    total = product(mine_ref[...], near_ref[0]) + product(other_ref[...], far_ref[0])
-    g = pl.program_id(0)
-
-    @pl.when(g == 0)
-    def _():
-        out_ref[...] = total * scale
-
-    @pl.when(g > 0)
-    def _():
-        out_ref[...] += total * scale
+def terms_kernel(scale, where_ref, field_ref, near_ref, far_ref, out_ref):
+    row, core = where_ref[0], where_ref[1]
+    share = near_ref.shape[2]
+    total = jnp.zeros(out_ref.shape, F32)
+    for d in range(Y):
+        group = CORE * lax.rem(row + Y - d, Y)
+        for owner, loadings in ((core, near_ref[d]), (1 - core, far_ref[d])):
+            lh, ll = split(pad_rows(loadings, PAD))
+            high, low = split(columns(field_ref, group + owner, share))
+            total += fold(nt(high, jnp.concatenate([lh, ll], axis=0))) + nt(low, lh)
+    out_ref[...] = total * scale
 
 
 def series_terms(field, near, far, where, scale):
     days = field.shape[0]
     rows, share = near.shape[1:]
-    mine = lambda d, where: (0, lax.rem(where[0] + Y - d, Y) * CORE + where[1])
-    other = lambda d, where: (0, lax.rem(where[0] + Y - d, Y) * CORE + 1 - where[1])
     return pl.pallas_call(
         functools.partial(terms_kernel, scale),
         out_shape=jax.ShapeDtypeStruct((days, PAD), F32),
-        grid_spec=pltpu.PrefetchScalarGridSpec(
-            num_scalar_prefetch=1,
-            grid=(Y,),
-            in_specs=[
-                pl.BlockSpec((days, share), mine),
-                pl.BlockSpec((days, share), other),
-                pl.BlockSpec((1, rows, share), lambda d, where: (d, 0, 0)),
-                pl.BlockSpec((1, rows, share), lambda d, where: (d, 0, 0)),
-            ],
-            out_specs=pl.BlockSpec((days, PAD), lambda d, where: (0, 0)),
-        ),
+        in_specs=[pl.BlockSpec(memory_space=pltpu.SMEM), VMEM, VMEM, VMEM],
+        out_specs=VMEM,
         cost_estimate=pl.CostEstimate(
             flops=6 * days * PAD * share * Y * CORE,
             bytes_accessed=4 * Y * CORE * share * (days + rows),
             transcendentals=0,
         ),
-        compiler_params=pltpu.CompilerParams(vmem_limit_bytes=WIDE_LIMIT),
-    )(where, field, field, near, far)
+        compiler_params=pltpu.CompilerParams(vmem_limit_bytes=LIMIT),
+    )(where, field, near, far)
 
 
 def swap(value, axes):
@@ -253,19 +229,19 @@
 
     chunk = swap(sent.reshape(N_PLANE, 2 * ROWS, PAD), PLANE)
     near = [lax.ppermute(narrow, "y", [(i, (i + d) % Y) for i in range(Y)]) for d in range(1, Y)]
-    chunk, near = lax.optimization_barrier((chunk, near))
+    chunk = swap(spread(jnp.sum(chunk, axis=0), Z), "z")
+    base = swap(spread(jnp.sum(chunk, axis=0), N_PLANE), PLANE)
+    base, near = lax.optimization_barrier((base, near))
     near = jnp.stack([narrow] + near)
     far = lax.ppermute(near, "core", [(0, 1), (1, 0)])
-    chunk = swap(spread(jnp.sum(chunk, axis=0), Z), "z")
-    chunk, near, far = lax.optimization_barrier((chunk, near, far))
-    terms = series_terms(field, near, far, jnp.stack([row, core]), days_total**0.5 / cells_total)
-    base = swap(spread(jnp.sum(chunk, axis=0), N_PLANE), PLANE)
-    base, terms = lax.optimization_barrier((base, terms))
     base = base.reshape(2 * PAD, PAD)
     piece = days_here // Z
     sent, y = whole(functools.partial(second_kernel, cells_total), [(PAD, PAD)] * 2, base, loadings)
 
-    chunk = jnp.sum(swap(sent.reshape(N_PLANE, ROWS, PAD), PLANE), axis=0)
+    sent, near, far = lax.optimization_barrier((sent, near, far))
+    terms = series_terms(field, near, far, jnp.stack([row, core]), days_total**0.5 / cells_total)
+    chunk, terms = lax.optimization_barrier((swap(sent.reshape(N_PLANE, ROWS, PAD), PLANE), terms))
+    chunk = jnp.sum(chunk, axis=0)
     both = jnp.concatenate([spread(chunk, Z), terms.reshape(Z, piece, PAD)], axis=1)
     both = jnp.sum(swap(both, "z"), axis=0)
     got = swap(spread(both, N_PLANE), PLANE)

time: 205 us -> 196 us (0.956)
  Pallas kernels: 28.6 us -> 18.6 us
  blocking collectives: 92.2 us -> 84.2 us
  local copies, waits for them, and re-layouts: 2.12 us -> 7.31 us
  starting transfers between devices: 49.6 us -> 53.2 us
  other arithmetic: 3.09 us -> 0.52 us
  waiting for transfers between devices: 27.9 us -> 30.2 us
    all_to_all x6 -> x5, blocking collectives: 92.2 us -> 84.2 us  [swap(): return lax.all_to_all(value, axes, 0, 0)]
    pallas_call x2, Pallas kernels: 8.11 us -> 1.19 us  [parts(): pl.pallas_call(functools.partial(parts_kernel, scale), out_shape=jax.Shap...]
    unnamed x4 -> x8, local copies, waits for them, and re-layouts: 0.01 us -> 5.27 us
    pallas_call x1, Pallas kernels: 5.52 us -> 1.81 us  [series_terms(): pl.pallas_call(functools.partial(terms_kernel, scale), out_shape=jax.Shap...]
    all_to_all x4 -> x5, starting transfers between devices: 30.1 us -> 33.5 us  [swap(): return lax.all_to_all(value, axes, 0, 0)]
    all_to_all x4 -> x5, waiting for transfers between devices: 27.9 us -> 28.9 us  [swap(): return lax.all_to_all(value, axes, 0, 0)]
  transfers between devices with their start and end apart: 9 -> 10, of which waited for: 4 -> 6; matrix products, arithmetic and copies ran while one was open for 1% -> 0% of each run, Pallas kernels for 5% -> 4%
where the time goes in v3:
time: 196 us; the launch traced here: 195 us
  blocking collectives  84.2 us (43%)
  starting transfers between devices  53.2 us (27%)
  waiting for transfers between devices  30.2 us (15%)
  Pallas kernels  18.6 us (9%)
  local copies, waits for them, and re-layouts  7.31 us (4%)
    all_to_all x5, blocking collectives, swap(): return lax.all_to_all(value, axes, 0, 0)  84.2 us
    all_to_all x5, starting transfers between devices, swap(): return lax.all_to_all(value, axes, 0, 0)  33.5 us
    all_to_all x5, waiting for transfers between devices, swap(): return lax.all_to_all(value, axes, 0, 0)  28.9 us
    pallas_call x3, Pallas kernels, whole(): pl.pallas_call(kernel, out_shape=tuple((jax.ShapeDtypeStruct(s, F32) for...  15.2 us
    ppermute x1, starting transfers between devices, on_device(): lax.ppermute(parts(field, pcs, (1 - core)[None], scale), 'core', [(0, 1),...  8.92 us
    ppermute x3, starting transfers between devices, on_device(): lax.ppermute(narrow, 'y', [(i, (i + d) % Y) for i in range(Y)])  8.49 us
    unnamed x8, local copies, waits for them, and re-layouts  5.27 us
  transfers between devices with their start and end apart: 10, of which 6 were waited for; matrix products, arithmetic and copies ran while one was open for 0% of the time, Pallas kernels for 4%

profile of v3, /device:TPU:1, one launch (start us, length us, event | category | flops | bytes accessed | tf_op | source)
XLA Modules:
  0.0 194.9 jit_solution(5395680216662612266)
XLA Ops:
  0.6 0.0 copy-start
  0.6 2.2 %copy-done = f32[256,4096]{1,0:T(8,128)S(1)} copy-done((f32[256,4096]{1,0:T(8,128)S(1)}, f32[256,4096]{1,0:T(8,128)}, u32[]{:S(2)}) %copy-start) | copy-done | bytes 4194328
  2.8 0.0 copy-start.3
  2.8 0.9 copy-done.3
  3.7 0.0 copy-start.1
  3.7 0.6 shard_map.41
  4.3 8.9 %collective-permute-start = (f32[4,104,512]{2,1,0:T(8,128)S(1)}, f32[4,104,512]{2,1,0:T(8,128)S(1)}, u32[]{:S(2)}, u32[]{:S(2)}) collective-permute-start(f32[4,104,512]{2,1,0:T(8,128)S(1)} %shard_map.41), channel_id=1, source_target_pairs={{0,1},{1,0},{2,3},{3,2},{4,5},{5,4},{6,7},{7,6},{8,9},{9,8},{10,11... | collective-permute-start | bytes 2555912 | tf_op jit(solution)/shard_map/ppermute | solution.py:226
  13.3 0.0 copy-done.1
  13.3 0.6 shard_map.42
  13.9 1.4 collective-permute-done
  15.2 0.2 add.10
  15.4 14.8 %all_to_all.50.recv_ref = f32[4,104,512]{2,1,0:T(8,128)S(1)} all-to-all(f32[4,104,512]{2,1,0:T(8,128)S(1)} %add.10), channel_id=1, replica_groups=mesh['z'=16,'x'=4,'y'=4,'core'=2] {'y'}, dimensions={0} | all-to-all | bytes 1703936 | tf_op jit(solution)/shard_map/all_to_all | solution.py:209
  30.2 0.4 shard_map.43
  30.6 11.9 %all_to_all.51 = f32[32,8,128]{2,1,0:T(8,128)S(1)} all-to-all(f32[32,8,128]{2,1,0:T(8,128)S(1)} %bitcast.24), channel_id=1, replica_groups=mesh['z'=16,'x'=4,'y'=4,'core'=2] {'x','y','core'}, dimensions={0} | all-to-all | bytes 262144 | tf_op jit(solution)/shard_map/all_to_all | solution.py:209
  42.6 0.6 broadcast_in_dim.26
  43.3 13.3 %all-to-all-start.2 = ((f32[16,8,128]{2,1,0:T(8,128)}), f32[16,8,128]{2,1,0:T(8,128)S(1)}, u32[]{:S(2)}, u32[]{:S(2)}) async-start(f32[16,8,128]{2,1,0:T(8,128)} %broadcast_in_dim.26), calls=%async_computation.2 | async-start | bytes 131072 | tf_op jit(solution)/shard_map/all_to_all | solution.py:209
  56.5 2.2 %collective-permute-start.1 = (f32[104,512]{1,0:T(8,128)S(1)}, f32[104,512]{1,0:T(8,128)S(1)}, u32[]{:S(2)}, u32[]{:S(2)}) collective-permute-start(f32[104,512]{1,0:T(8,128)S(1)} %get-tuple-element.19), channel_id=1, source_target_pairs={{0,2},{2,4},{4,6},{6,0},{1,3},{3,5},{5,7},{7,1},{8,10},{10,12},{12... | collective-permute-start | bytes 638984 | tf_op jit(solution)/shard_map/ppermute | solution.py:231
  58.7 3.8 %collective-permute-start.2 = (f32[104,512]{1,0:T(8,128)S(1)}, f32[104,512]{1,0:T(8,128)S(1)}, u32[]{:S(2)}, u32[]{:S(2)}) collective-permute-start(f32[104,512]{1,0:T(8,128)S(1)} %get-tuple-element.19), channel_id=1, source_target_pairs={{0,4},{2,6},{4,0},{6,2},{1,5},{3,7},{5,1},{7,3},{8,12},{10,14},{12... | collective-permute-start | bytes 638984 | tf_op jit(solution)/shard_map/ppermute | solution.py:231
  62.5 2.6 %collective-permute-start.3 = (f32[104,512]{1,0:T(8,128)S(1)}, f32[104,512]{1,0:T(8,128)S(1)}, u32[]{:S(2)}, u32[]{:S(2)}) collective-permute-start(f32[104,512]{1,0:T(8,128)S(1)} %get-tuple-element.19), channel_id=1, source_target_pairs={{0,6},{2,0},{4,2},{6,4},{1,7},{3,1},{5,3},{7,5},{8,14},{10,8},{12,... | collective-permute-start | bytes 638984 | tf_op jit(solution)/shard_map/ppermute | solution.py:231
  65.0 3.1 %all-to-all-done.2 = f32[16,8,128]{2,1,0:T(8,128)S(1)} async-done(((f32[16,8,128]{2,1,0:T(8,128)}), f32[16,8,128]{2,1,0:T(8,128)S(1)}, u32[]{:S(2)}, u32[]{:S(2)}) %all-to-all-start.2) | async-done | bytes 65568 | tf_op jit(solution)/shard_map/all_to_all | solution.py:209
  68.1 0.7 broadcast_in_dim.27
  68.8 5.6 %all-to-all-start.3 = ((f32[32,8,128]{2,1,0:T(8,128)}), f32[32,8,128]{2,1,0:T(8,128)S(1)}, u32[]{:S(2)}, u32[]{:S(2)}) async-start(f32[32,8,128]{2,1,0:T(8,128)} %broadcast_in_dim.27), calls=%async_computation.3 | async-start | bytes 262144 | tf_op jit(solution)/shard_map/all_to_all | solution.py:209
  74.4 0.0 collective-permute-done.1
  74.4 0.0 collective-permute-done.2
  74.4 0.0 collective-permute-done.3
  74.5 7.8 %all-to-all-done.3 = f32[32,8,128]{2,1,0:T(8,128)S(1)} async-done(((f32[32,8,128]{2,1,0:T(8,128)}), f32[32,8,128]{2,1,0:T(8,128)S(1)}, u32[]{:S(2)}, u32[]{:S(2)}) %all-to-all-start.3) | async-done | bytes 131104 | tf_op jit(solution)/shard_map/all_to_all | solution.py:209
  82.2 0.1 pad_maximum_fusion.near_ref
  82.3 2.3 %collective-permute-start.4 = (f32[4,104,512]{2,1,0:T(8,128)S(1)}, f32[4,104,512]{2,1,0:T(8,128)S(1)}, u32[]{:S(2)}, u32[]{:S(2)}) collective-permute-start(f32[4,104,512]{2,1,0:T(8,128)S(1)} %pad_maximum_fusion.near_ref), channel_id=1, source_target_pairs={{0,1},{1,0},{2,3},{3,2},{4,5},{5,4},{6,7},{7,6},{8,9},{9,8},{10,11... | collective-permute-start | bytes 2555912 | tf_op jit(solution)/shard_map/ppermute | solution.py:236
  84.6 0.1 pad_add_fusion.where_ref
  84.7 5.0 %shard_map.44 = (f32[128,128]{1,0:T(8,128)}, f32[128,128]{1,0:T(8,128)S(1)}) custom-call(f32[256,128]{1,0:T(8,128)S(1)} %bitcast.16, f32[128,512]{1,0:T(8,128)S(1)} %get-tuple-element.21.loadings_ref), custom_call_target="tpu_custom_call" | custom-call | tf_op jit(solution)/shard_map/pallas_call | solution.py:169
  89.7 0.0 collective-permute-done.4.far_ref
  89.7 3.6 %all-to-all-start.4 = ((f32[32,4,128]{2,1,0:T(4,128)}), f32[32,4,128]{2,1,0:T(4,128)S(1)}, u32[]{:S(2)}, u32[]{:S(2)}) async-start(f32[32,4,128]{2,1,0:T(4,128)} %bitcast.8), calls=%async_computation.4 | async-start | bytes 131072 | tf_op jit(solution)/shard_map/all_to_all | solution.py:209
  93.3 0.0 copy-start.2
  93.3 2.2 %copy-done.2 = f32[256,4096]{1,0:T(8,128)S(1)} copy-done((f32[256,4096]{1,0:T(8,128)S(1)}, f32[256,4096]{1,0:T(8,128)}, u32[]{:S(2)}) %copy-start.2) | copy-done | bytes 4194328
  95.5 1.8 shard_map.45
  97.3 3.4 %all-to-all-done.4 = f32[32,4,128]{2,1,0:T(4,128)S(1)} async-done(((f32[32,4,128]{2,1,0:T(4,128)}), f32[32,4,128]{2,1,0:T(4,128)S(1)}, u32[]{:S(2)}, u32[]{:S(2)}) %all-to-all-start.4) | async-done | bytes 65568 | tf_op jit(solution)/shard_map/all_to_all | solution.py:209
  100.9 21.8 %all_to_all.52 = f32[16,20,128]{2,1,0:T(8,128)S(1)} all-to-all(f32[16,20,128]{2,1,0:T(8,128)S(1)} %pad_maximum_fusion.1), channel_id=1, replica_groups=mesh['z'=16,'x'=4,'y'=4,'core'=2] {'z'}, dimensions={0} | all-to-all | bytes 327680 | tf_op jit(solution)/shard_map/all_to_all | solution.py:209
  122.7 17.2 %all_to_all.53 = f32[32,20,128]{2,1,0:T(8,128)S(1)} all-to-all(f32[32,20,128]{2,1,0:T(8,128)S(1)} %broadcast_in_dim.29), channel_id=1, replica_groups=mesh['z'=16,'x'=4,'y'=4,'core'=2] {'x','y','core'}, dimensions={0} | all-to-all | bytes 655360 | tf_op jit(solution)/shard_map/all_to_all | solution.py:209
  139.9 5.1 %shard_map.46 = (f32[128,128]{1,0:T(8,128)}, f32[128,128]{1,0:T(8,128)S(1)}) custom-call(f32[128,128]{1,0:T(8,128)S(1)} %bitcast.22, f32[256,128]{1,0:T(8,128)S(1)} %bitcast.17, f32[128,128]{1,0:T(8,128)S(1)} %get-tuple-element.31.y_ref, f32[128,512]{1,0:T(8,128)S(1)} %get-tuple-element.21.loadings_ref), custom_call_target="tpu_custom_call" | custom-call | tf_op jit(solution)/shard_map/pallas_call | solution.py:169
  145.1 3.6 %all-to-all-start.7 = ((f32[32,4,128]{2,1,0:T(4,128)}), f32[32,4,128]{2,1,0:T(4,128)S(1)}, u32[]{:S(2)}, u32[]{:S(2)}) async-start(f32[32,4,128]{2,1,0:T(4,128)} %bitcast.12), calls=%async_computation.7 | async-start | bytes 131072 | tf_op jit(solution)/shard_map/all_to_all | solution.py:209
  148.8 7.2 %all-to-all-done.7 = f32[32,4,128]{2,1,0:T(4,128)S(1)} async-done(((f32[32,4,128]{2,1,0:T(4,128)}), f32[32,4,128]{2,1,0:T(4,128)S(1)}, u32[]{:S(2)}, u32[]{:S(2)}) %all-to-all-start.7) | async-done | bytes 65568 | tf_op jit(solution)/shard_map/all_to_all | solution.py:209
  156.0 18.4 %all_to_all.54 = f32[16,20,128]{2,1,0:T(8,128)S(1)} all-to-all(f32[16,20,128]{2,1,0:T(8,128)S(1)} %broadcast_in_dim.30), channel_id=1, replica_groups=mesh['z'=16,'x'=4,'y'=4,'core'=2] {'z'}, dimensions={0} | all-to-all | bytes 327680 | tf_op jit(solution)/shard_map/all_to_all | solution.py:209
  174.5 0.6 broadcast_in_dim.31
  175.1 7.4 %all-to-all-start.9 = ((f32[32,4,128]{2,1,0:T(4,128)}), f32[32,4,128]{2,1,0:T(4,128)S(1)}, u32[]{:S(2)}, u32[]{:S(2)}) async-start(f32[32,4,128]{2,1,0:T(4,128)} %broadcast_in_dim.31), calls=%async_computation.9 | async-start | bytes 131072 | tf_op jit(solution)/shard_map/all_to_all | solution.py:209
  182.5 7.3 %all-to-all-done.9 = f32[32,4,128]{2,1,0:T(4,128)S(1)} async-done(((f32[32,4,128]{2,1,0:T(4,128)}), f32[32,4,128]{2,1,0:T(4,128)S(1)}, u32[]{:S(2)}, u32[]{:S(2)}) %all-to-all-start.9) | async-done | bytes 65568 | tf_op jit(solution)/shard_map/all_to_all | solution.py:209
  189.9 5.1 %shard_map.47 = (f32[100,512]{1,0:T(8,128)}, f32[100,256]{1,0:T(8,128)}) custom-call(f32[128,128]{1,0:T(8,128)S(1)} %bitcast.21, f32[256,128]{1,0:T(8,128)S(1)} %bitcast.18, f32[128,128]{1,0:T(8,128)S(1)} %get-tuple-element.33.y_ref, f32[128,512]{1,0:T(8,128)S(1)} %get-tuple-element.21.loadings_ref, f32[256,128]{1,0:T(8,128)S(1)} %bitcast.19), custom_call_target="tpu_custom_call" | custom-call | tf_op jit(solution)/shard_map/pallas_call | solution.py:169
  (15 shorter events, 0.3 us)
Async XLA Ops:
  0.6 2.2 %copy-start = (f32[256,4096]{1,0:T(8,128)S(1)}, f32[256,4096]{1,0:T(8,128)}, u32[]{:S(2)}) copy-start(f32[256,4096]{1,0:T(8,128)} %field_ref.5) | copy-start | bytes 12582916
  2.8 0.9 copy-start.3
  3.7 9.5 %copy-start.1 = (f32[256,4096]{1,0:T(8,128)S(1)}, f32[256,4096]{1,0:T(8,128)}, u32[]{:S(2)}) copy-start(f32[256,4096]{1,0:T(8,128)} %field_ref.5) | copy-start | bytes 12582916
  4.3 10.9 %collective-permute-start = (f32[4,104,512]{2,1,0:T(8,128)S(1)}, f32[4,104,512]{2,1,0:T(8,128)S(1)}, u32[]{:S(2)}, u32[]{:S(2)}) collective-permute-start(f32[4,104,512]{2,1,0:T(8,128)S(1)} %shard_map.41), channel_id=1, source_target_pairs={{0,1},{1,0},{2,3},{3,2},{4,5},{5,4},{6,7},{7,6},{8,9},{9,8},{10,11... | collective-permute-start | bytes 2555912 | tf_op jit(solution)/shard_map/ppermute | solution.py:226
  43.3 24.9 %all-to-all-start.2 = ((f32[16,8,128]{2,1,0:T(8,128)}), f32[16,8,128]{2,1,0:T(8,128)S(1)}, u32[]{:S(2)}, u32[]{:S(2)}) async-start(f32[16,8,128]{2,1,0:T(8,128)} %broadcast_in_dim.26), calls=%async_computation.2 | async-start | bytes 131072 | tf_op jit(solution)/shard_map/all_to_all | solution.py:209
  56.5 17.9 %collective-permute-start.1 = (f32[104,512]{1,0:T(8,128)S(1)}, f32[104,512]{1,0:T(8,128)S(1)}, u32[]{:S(2)}, u32[]{:S(2)}) collective-permute-start(f32[104,512]{1,0:T(8,128)S(1)} %get-tuple-element.19), channel_id=1, source_target_pairs={{0,2},{2,4},{4,6},{6,0},{1,3},{3,5},{5,7},{7,1},{8,10},{10,12},{12... | collective-permute-start | bytes 638984 | tf_op jit(solution)/shard_map/ppermute | solution.py:231
  58.7 15.8 %collective-permute-start.2 = (f32[104,512]{1,0:T(8,128)S(1)}, f32[104,512]{1,0:T(8,128)S(1)}, u32[]{:S(2)}, u32[]{:S(2)}) collective-permute-start(f32[104,512]{1,0:T(8,128)S(1)} %get-tuple-element.19), channel_id=1, source_target_pairs={{0,4},{2,6},{4,0},{6,2},{1,5},{3,7},{5,1},{7,3},{8,12},{10,14},{12... | collective-permute-start | bytes 638984 | tf_op jit(solution)/shard_map/ppermute | solution.py:231
  62.5 12.0 %collective-permute-start.3 = (f32[104,512]{1,0:T(8,128)S(1)}, f32[104,512]{1,0:T(8,128)S(1)}, u32[]{:S(2)}, u32[]{:S(2)}) collective-permute-start(f32[104,512]{1,0:T(8,128)S(1)} %get-tuple-element.19), channel_id=1, source_target_pairs={{0,6},{2,0},{4,2},{6,4},{1,7},{3,1},{5,3},{7,5},{8,14},{10,8},{12,... | collective-permute-start | bytes 638984 | tf_op jit(solution)/shard_map/ppermute | solution.py:231
  68.8 13.4 %all-to-all-start.3 = ((f32[32,8,128]{2,1,0:T(8,128)}), f32[32,8,128]{2,1,0:T(8,128)S(1)}, u32[]{:S(2)}, u32[]{:S(2)}) async-start(f32[32,8,128]{2,1,0:T(8,128)} %broadcast_in_dim.27), calls=%async_computation.3 | async-start | bytes 262144 | tf_op jit(solution)/shard_map/all_to_all | solution.py:209
  82.3 7.4 %collective-permute-start.4 = (f32[4,104,512]{2,1,0:T(8,128)S(1)}, f32[4,104,512]{2,1,0:T(8,128)S(1)}, u32[]{:S(2)}, u32[]{:S(2)}) collective-permute-start(f32[4,104,512]{2,1,0:T(8,128)S(1)} %pad_maximum_fusion.near_ref), channel_id=1, source_target_pairs={{0,1},{1,0},{2,3},{3,2},{4,5},{5,4},{6,7},{7,6},{8,9},{9,8},{10,11... | collective-permute-start | bytes 2555912 | tf_op jit(solution)/shard_map/ppermute | solution.py:236
  89.7 11.1 %all-to-all-start.4 = ((f32[32,4,128]{2,1,0:T(4,128)}), f32[32,4,128]{2,1,0:T(4,128)S(1)}, u32[]{:S(2)}, u32[]{:S(2)}) async-start(f32[32,4,128]{2,1,0:T(4,128)} %bitcast.8), calls=%async_computation.4 | async-start | bytes 131072 | tf_op jit(solution)/shard_map/all_to_all | solution.py:209
  93.3 2.2 %copy-start.2 = (f32[256,4096]{1,0:T(8,128)S(1)}, f32[256,4096]{1,0:T(8,128)}, u32[]{:S(2)}) copy-start(f32[256,4096]{1,0:T(8,128)} %field_ref.5) | copy-start | bytes 12582916
  145.1 10.9 %all-to-all-start.7 = ((f32[32,4,128]{2,1,0:T(4,128)}), f32[32,4,128]{2,1,0:T(4,128)S(1)}, u32[]{:S(2)}, u32[]{:S(2)}) async-start(f32[32,4,128]{2,1,0:T(4,128)} %bitcast.12), calls=%async_computation.7 | async-start | bytes 131072 | tf_op jit(solution)/shard_map/all_to_all | solution.py:209
  175.1 14.7 %all-to-all-start.9 = ((f32[32,4,128]{2,1,0:T(4,128)}), f32[32,4,128]{2,1,0:T(4,128)S(1)}, u32[]{:S(2)}, u32[]{:S(2)}) async-start(f32[32,4,128]{2,1,0:T(4,128)} %broadcast_in_dim.31), calls=%async_computation.9 | async-start | bytes 131072 | tf_op jit(solution)/shard_map/all_to_all | solution.py:209

commit v4 on v3

--- a/solution.py
+++ b/solution.py
@@ -18,6 +18,7 @@
 F32 = jnp.float32
 VMEM = pl.BlockSpec(memory_space=pltpu.VMEM)
 LIMIT = 24 << 20
+WIDE_LIMIT = 52 << 20
 
 
 def split(value):
@@ -78,14 +79,23 @@
     return field_ref[:, pl.ds(pl.multiple_of(group * share, share), share)]
 
 
-def parts_kernel(scale, core_ref, pcs_ref, field_ref, out_ref, wide):
+def parts_kernel(scale, core_ref, pcs_ref, field_ref, out_ref, pcs, wide, field, sems):
+    share = out_ref.shape[2]
+    copies = [pltpu.make_async_copy(pcs_ref, pcs, sems.at[Y])]
+    for g in range(Y):
+        start = pl.multiple_of((CORE * g + core_ref[0]) * share, share)
+        copies.append(pltpu.make_async_copy(field_ref.at[:, pl.ds(start, share)], field.at[g], sems.at[g]))
+    for copy in copies:
+        copy.start()
     wide[...] = jnp.zeros_like(wide)
-    wide[0 : pcs_ref.shape[0]] = pcs_ref[...] * scale
+    copies[0].wait()
+    wide[0 : pcs.shape[0]] = pcs[...] * scale
     half = wide.shape[0]
     left_high, left_low = split(wide[...])
     left = jnp.concatenate([left_high, left_low], axis=0)
     for g in range(Y):
-        high, low = split(columns(field_ref, CORE * g + core_ref[0], out_ref.shape[2]))
+        copies[1 + g].wait()
+        high, low = split(field[g])
         both = nn(left, high)
         total = both[0:half] + both[half : 2 * half] + nn(left_high, low)
         out_ref[g] = total[0 : out_ref.shape[1]]
@@ -96,16 +106,22 @@
     share = field.shape[1] // (Y * CORE)
     half = (k + 15) // 16 * 16
     rows = (k + 7) // 8 * 8
+    far = pl.BlockSpec(memory_space=pl.ANY)
     return pl.pallas_call(
         functools.partial(parts_kernel, scale),
         out_shape=jax.ShapeDtypeStruct((Y, rows, share), F32),
-        in_specs=[pl.BlockSpec(memory_space=pltpu.SMEM), VMEM, VMEM],
+        in_specs=[pl.BlockSpec(memory_space=pltpu.SMEM), far, far],
         out_specs=VMEM,
-        scratch_shapes=[pltpu.VMEM((half, days), F32)],
+        scratch_shapes=[
+            pltpu.VMEM((k, days), F32),
+            pltpu.VMEM((half, days), F32),
+            pltpu.VMEM((Y, days, share), F32),
+            pltpu.SemaphoreType.DMA((Y + 1,)),
+        ],
         cost_estimate=pl.CostEstimate(
             flops=6 * k * days * share * Y, bytes_accessed=4 * Y * share * (days + k), transcendentals=0
         ),
-        compiler_params=pltpu.CompilerParams(vmem_limit_bytes=LIMIT),
+        compiler_params=pltpu.CompilerParams(vmem_limit_bytes=WIDE_LIMIT),
     )(core, pcs, field)
 
 
@@ -255,7 +271,7 @@
     chunk = jnp.sum(swap(sent.reshape(N_PLANE, ROWS, PAD), PLANE), axis=0)
     got = swap(spread(jnp.concatenate([chunk, terms], axis=0), Z), "z")
     terms = got[:, ROWS:].reshape(days_here, PAD)
-    chunk = jnp.sum(got[:, :ROWS], axis=0)
+    chunk, terms = lax.optimization_barrier((jnp.sum(got[:, :ROWS], axis=0), terms))
     cube = swap(spread(chunk, N_PLANE), PLANE).reshape(PAD, PAD)
     return whole(
         functools.partial(last_kernel, cells_total),

time: 196 us -> 195 us (level)
  blocking collectives: 84.2 us -> 98.7 us
  waiting for transfers between devices: 30.2 us -> 21.5 us
  starting transfers between devices: 53.2 us -> 45.7 us
  Pallas kernels: 18.6 us -> 21.9 us
  local copies, waits for them, and re-layouts: 7.31 us -> 4.49 us
    all_to_all x5 -> x6, blocking collectives: 84.2 us -> 98.7 us  [swap(): return lax.all_to_all(value, axes, 0, 0)]
    all_to_all x5 -> x4, starting transfers between devices: 33.5 us -> 26.2 us  [swap(): return lax.all_to_all(value, axes, 0, 0)]
    all_to_all x5 -> x4, waiting for transfers between devices: 28.9 us -> 21.5 us  [swap(): return lax.all_to_all(value, axes, 0, 0)]
    pallas_call x2, Pallas kernels: 1.19 us -> 4.5 us  [parts(): pl.pallas_call(functools.partial(parts_kernel, scale), out_shape=jax.Shap...]
    unnamed x8 -> x6, local copies, waits for them, and re-layouts: 5.27 us -> 3.08 us
  transfers between devices with their start and end apart: 10 -> 9, of which waited for: 6 -> 4; matrix products, arithmetic and copies ran while one was open for 0% -> 0% of each run, Pallas kernels for 4% -> 5%
where the time goes in v4:
time: 195 us; the launch traced here: 194 us
  blocking collectives  98.7 us (51%)
  starting transfers between devices  45.7 us (23%)
  Pallas kernels  21.9 us (11%)
  waiting for transfers between devices  21.5 us (11%)
  local copies, waits for them, and re-layouts  4.49 us (2%)
    all_to_all x6, blocking collectives, swap(): return lax.all_to_all(value, axes, 0, 0)  98.7 us
    all_to_all x4, starting transfers between devices, swap(): return lax.all_to_all(value, axes, 0, 0)  26.2 us
    all_to_all x4, waiting for transfers between devices, swap(): return lax.all_to_all(value, axes, 0, 0)  21.5 us
    pallas_call x3, Pallas kernels, whole(): pl.pallas_call(kernel, out_shape=tuple((jax.ShapeDtypeStruct(s, F32) for...  15.2 us
    ppermute x1, starting transfers between devices, on_device(): lax.ppermute(parts(field, pcs, (1 - core)[None], scale), 'core', [(0, 1),...  8.79 us
    ppermute x3, starting transfers between devices, on_device(): lax.ppermute(narrow, 'y', [(i, (i + d) % Y) for i in range(Y)])  8.49 us
    pallas_call x2, Pallas kernels, parts(): pl.pallas_call(functools.partial(parts_kernel, scale), out_shape=jax.Shap...  4.5 us
  transfers between devices with their start and end apart: 9, of which 4 were waited for; matrix products, arithmetic and copies ran while one was open for 0% of the time, Pallas kernels for 5%

profile of v4, /device:TPU:1, one launch (start us, length us, event | category | flops | bytes accessed | tf_op | source)
XLA Modules:
  0.0 193.7 jit_solution(17115609496315098765)
XLA Ops:
  0.6 0.0 copy-start.1
  0.6 0.9 copy-done.1
  1.5 0.0 copy-start.2
  1.5 2.2 %shard_map.41 = f32[4,104,512]{2,1,0:T(8,128)S(1)} custom-call(s32[1]{0:T(128)} %bitcast.core_ref, f32[100,256]{1,0:T(8,128)S(1)} %copy-done.1, f32[256,4096]{1,0:T(8,128)} %field_ref.5), custom_call_target="tpu_custom_call" | custom-call | flops 314572800 | bytes 2916352 | tf_op jit(solution)/shard_map/pallas_call | solution.py:110
  3.8 8.8 %collective-permute-start = (f32[4,104,512]{2,1,0:T(8,128)S(1)}, f32[4,104,512]{2,1,0:T(8,128)S(1)}, u32[]{:S(2)}, u32[]{:S(2)}) collective-permute-start(f32[4,104,512]{2,1,0:T(8,128)S(1)} %shard_map.41), channel_id=1, source_target_pairs={{0,1},{1,0},{2,3},{3,2},{4,5},{5,4},{6,7},{7,6},{8,9},{9,8},{10,11... | collective-permute-start | bytes 2555912 | tf_op jit(solution)/shard_map/ppermute | solution.py:242
  12.6 0.0 copy-done.2
  12.6 2.3 %shard_map.42 = f32[4,104,512]{2,1,0:T(8,128)S(1)} custom-call(s32[1]{0:T(128)} %bitcast.1.core_ref, f32[100,256]{1,0:T(8,128)S(1)} %copy-done.2, f32[256,4096]{1,0:T(8,128)} %field_ref.5), custom_call_target="tpu_custom_call" | custom-call | flops 314572800 | bytes 2916352 | tf_op jit(solution)/shard_map/pallas_call | solution.py:110
  14.9 0.0 collective-permute-done
  14.9 0.2 add.10
  15.0 15.5 %all_to_all.50.recv_ref = f32[4,104,512]{2,1,0:T(8,128)S(1)} all-to-all(f32[4,104,512]{2,1,0:T(8,128)S(1)} %add.10), channel_id=1, replica_groups=mesh['z'=16,'x'=4,'y'=4,'core'=2] {'y'}, dimensions={0} | all-to-all | bytes 1703936 | tf_op jit(solution)/shard_map/all_to_all | solution.py:225
  30.5 0.4 shard_map.43
  30.9 11.3 %all_to_all.51 = f32[32,8,128]{2,1,0:T(8,128)S(1)} all-to-all(f32[32,8,128]{2,1,0:T(8,128)S(1)} %bitcast.24), channel_id=1, replica_groups=mesh['z'=16,'x'=4,'y'=4,'core'=2] {'x','y','core'}, dimensions={0} | all-to-all | bytes 262144 | tf_op jit(solution)/shard_map/all_to_all | solution.py:225
  42.3 0.6 broadcast_in_dim.26
  42.9 13.2 %all-to-all-start.2 = ((f32[16,8,128]{2,1,0:T(8,128)}), f32[16,8,128]{2,1,0:T(8,128)S(1)}, u32[]{:S(2)}, u32[]{:S(2)}) async-start(f32[16,8,128]{2,1,0:T(8,128)} %broadcast_in_dim.26), calls=%async_computation.2 | async-start | bytes 131072 | tf_op jit(solution)/shard_map/all_to_all | solution.py:225
  56.2 2.2 %collective-permute-start.1 = (f32[104,512]{1,0:T(8,128)S(1)}, f32[104,512]{1,0:T(8,128)S(1)}, u32[]{:S(2)}, u32[]{:S(2)}) collective-permute-start(f32[104,512]{1,0:T(8,128)S(1)} %get-tuple-element.21), channel_id=1, source_target_pairs={{0,2},{2,4},{4,6},{6,0},{1,3},{3,5},{5,7},{7,1},{8,10},{10,12},{12... | collective-permute-start | bytes 638984 | tf_op jit(solution)/shard_map/ppermute | solution.py:247
  58.3 3.8 %collective-permute-start.2 = (f32[104,512]{1,0:T(8,128)S(1)}, f32[104,512]{1,0:T(8,128)S(1)}, u32[]{:S(2)}, u32[]{:S(2)}) collective-permute-start(f32[104,512]{1,0:T(8,128)S(1)} %get-tuple-element.21), channel_id=1, source_target_pairs={{0,4},{2,6},{4,0},{6,2},{1,5},{3,7},{5,1},{7,3},{8,12},{10,14},{12... | collective-permute-start | bytes 638984 | tf_op jit(solution)/shard_map/ppermute | solution.py:247
  62.1 2.6 %collective-permute-start.3 = (f32[104,512]{1,0:T(8,128)S(1)}, f32[104,512]{1,0:T(8,128)S(1)}, u32[]{:S(2)}, u32[]{:S(2)}) collective-permute-start(f32[104,512]{1,0:T(8,128)S(1)} %get-tuple-element.21), channel_id=1, source_target_pairs={{0,6},{2,0},{4,2},{6,4},{1,7},{3,1},{5,3},{7,5},{8,14},{10,8},{12,... | collective-permute-start | bytes 638984 | tf_op jit(solution)/shard_map/ppermute | solution.py:247
  64.7 3.1 %all-to-all-done.2 = f32[16,8,128]{2,1,0:T(8,128)S(1)} async-done(((f32[16,8,128]{2,1,0:T(8,128)}), f32[16,8,128]{2,1,0:T(8,128)S(1)}, u32[]{:S(2)}, u32[]{:S(2)}) %all-to-all-start.2) | async-done | bytes 65568 | tf_op jit(solution)/shard_map/all_to_all | solution.py:225
  67.8 0.7 broadcast_in_dim.27
  68.4 5.6 %all-to-all-start.3 = ((f32[32,8,128]{2,1,0:T(8,128)}), f32[32,8,128]{2,1,0:T(8,128)S(1)}, u32[]{:S(2)}, u32[]{:S(2)}) async-start(f32[32,8,128]{2,1,0:T(8,128)} %broadcast_in_dim.27), calls=%async_computation.3 | async-start | bytes 262144 | tf_op jit(solution)/shard_map/all_to_all | solution.py:225
  74.1 0.0 collective-permute-done.1
  74.1 0.0 collective-permute-done.2
  74.1 0.0 collective-permute-done.3
  74.1 7.8 %all-to-all-done.3 = f32[32,8,128]{2,1,0:T(8,128)S(1)} async-done(((f32[32,8,128]{2,1,0:T(8,128)}), f32[32,8,128]{2,1,0:T(8,128)S(1)}, u32[]{:S(2)}, u32[]{:S(2)}) %all-to-all-start.3) | async-done | bytes 131104 | tf_op jit(solution)/shard_map/all_to_all | solution.py:225
  81.9 0.1 pad_maximum_fusion.near_ref
  81.9 2.3 %collective-permute-start.4 = (f32[4,104,512]{2,1,0:T(8,128)S(1)}, f32[4,104,512]{2,1,0:T(8,128)S(1)}, u32[]{:S(2)}, u32[]{:S(2)}) collective-permute-start(f32[4,104,512]{2,1,0:T(8,128)S(1)} %pad_maximum_fusion.near_ref), channel_id=1, source_target_pairs={{0,1},{1,0},{2,3},{3,2},{4,5},{5,4},{6,7},{7,6},{8,9},{9,8},{10,11... | collective-permute-start | bytes 2555912 | tf_op jit(solution)/shard_map/ppermute | solution.py:252
  84.3 0.1 pad_add_fusion.where_ref
  84.3 5.0 %shard_map.44 = (f32[128,128]{1,0:T(8,128)}, f32[128,128]{1,0:T(8,128)S(1)}) custom-call(f32[256,128]{1,0:T(8,128)S(1)} %bitcast.16, f32[128,512]{1,0:T(8,128)S(1)} %get-tuple-element.23.loadings_ref), custom_call_target="tpu_custom_call" | custom-call | tf_op jit(solution)/shard_map/pallas_call | solution.py:185
  89.3 0.0 collective-permute-done.4.far_ref
  89.3 3.6 %all-to-all-start.4 = ((f32[32,4,128]{2,1,0:T(4,128)}), f32[32,4,128]{2,1,0:T(4,128)S(1)}, u32[]{:S(2)}, u32[]{:S(2)}) async-start(f32[32,4,128]{2,1,0:T(4,128)} %bitcast.8), calls=%async_computation.4 | async-start | bytes 131072 | tf_op jit(solution)/shard_map/all_to_all | solution.py:225
  93.0 0.0 copy-start
  93.0 2.2 %copy-done = f32[256,4096]{1,0:T(8,128)S(1)} copy-done((f32[256,4096]{1,0:T(8,128)S(1)}, f32[256,4096]{1,0:T(8,128)}, u32[]{:S(2)}) %copy-start) | copy-done | bytes 4194328
  95.2 1.8 shard_map.45
  97.0 3.5 %all-to-all-done.4 = f32[32,4,128]{2,1,0:T(4,128)S(1)} async-done(((f32[32,4,128]{2,1,0:T(4,128)}), f32[32,4,128]{2,1,0:T(4,128)S(1)}, u32[]{:S(2)}, u32[]{:S(2)}) %all-to-all-start.4) | async-done | bytes 65568 | tf_op jit(solution)/shard_map/all_to_all | solution.py:225
  100.5 21.8 %all_to_all.52 = f32[16,20,128]{2,1,0:T(8,128)S(1)} all-to-all(f32[16,20,128]{2,1,0:T(8,128)S(1)} %pad_maximum_fusion.1), channel_id=1, replica_groups=mesh['z'=16,'x'=4,'y'=4,'core'=2] {'z'}, dimensions={0} | all-to-all | bytes 327680 | tf_op jit(solution)/shard_map/all_to_all | solution.py:225
  122.4 17.2 %all_to_all.53 = f32[32,20,128]{2,1,0:T(8,128)S(1)} all-to-all(f32[32,20,128]{2,1,0:T(8,128)S(1)} %broadcast_in_dim.29), channel_id=1, replica_groups=mesh['z'=16,'x'=4,'y'=4,'core'=2] {'x','y','core'}, dimensions={0} | all-to-all | bytes 655360 | tf_op jit(solution)/shard_map/all_to_all | solution.py:225
  139.6 5.1 %shard_map.46 = (f32[128,128]{1,0:T(8,128)}, f32[128,128]{1,0:T(8,128)S(1)}) custom-call(f32[128,128]{1,0:T(8,128)S(1)} %bitcast.22, f32[256,128]{1,0:T(8,128)S(1)} %bitcast.17, f32[128,128]{1,0:T(8,128)S(1)} %get-tuple-element.33.y_ref, f32[128,512]{1,0:T(8,128)S(1)} %get-tuple-element.23.loadings_ref), custom_call_target="tpu_custom_call" | custom-call | tf_op jit(solution)/shard_map/pallas_call | solution.py:185
  144.7 3.6 %all-to-all-start.7 = ((f32[32,4,128]{2,1,0:T(4,128)}), f32[32,4,128]{2,1,0:T(4,128)S(1)}, u32[]{:S(2)}, u32[]{:S(2)}) async-start(f32[32,4,128]{2,1,0:T(4,128)} %bitcast.12), calls=%async_computation.7 | async-start | bytes 131072 | tf_op jit(solution)/shard_map/all_to_all | solution.py:225
  148.4 7.2 %all-to-all-done.7 = f32[32,4,128]{2,1,0:T(4,128)S(1)} async-done(((f32[32,4,128]{2,1,0:T(4,128)}), f32[32,4,128]{2,1,0:T(4,128)S(1)}, u32[]{:S(2)}, u32[]{:S(2)}) %all-to-all-start.7) | async-done | bytes 65568 | tf_op jit(solution)/shard_map/all_to_all | solution.py:225
  155.7 18.4 %all_to_all.54 = f32[16,20,128]{2,1,0:T(8,128)S(1)} all-to-all(f32[16,20,128]{2,1,0:T(8,128)S(1)} %broadcast_in_dim.30), channel_id=1, replica_groups=mesh['z'=16,'x'=4,'y'=4,'core'=2] {'z'}, dimensions={0} | all-to-all | bytes 327680 | tf_op jit(solution)/shard_map/all_to_all | solution.py:225
  174.2 14.5 %all_to_all.55 = f32[32,4,128]{2,1,0:T(4,128)S(1)} all-to-all(f32[32,4,128]{2,1,0:T(4,128)S(1)} %broadcast_in_dim.31), channel_id=1, replica_groups=mesh['z'=16,'x'=4,'y'=4,'core'=2] {'x','y','core'}, dimensions={0} | all-to-all | bytes 131072 | tf_op jit(solution)/shard_map/all_to_all | solution.py:225
  188.7 5.1 %shard_map.47 = (f32[100,512]{1,0:T(8,128)}, f32[100,256]{1,0:T(8,128)}) custom-call(f32[128,128]{1,0:T(8,128)S(1)} %bitcast.21, f32[256,128]{1,0:T(8,128)S(1)} %bitcast.18, f32[128,128]{1,0:T(8,128)S(1)} %get-tuple-element.36.y_ref, f32[128,512]{1,0:T(8,128)S(1)} %get-tuple-element.23.loadings_ref, f32[256,128]{1,0:T(8,128)S(1)} %bitcast.19), custom_call_target="tpu_custom_call" | custom-call | tf_op jit(solution)/shard_map/pallas_call | solution.py:185
  (16 shorter events, 0.3 us)
Async XLA Ops:
  0.6 0.9 copy-start.1
  1.5 11.0 %copy-start.2 = (f32[100,256]{1,0:T(8,128)S(1)}, f32[100,256]{1,0:T(8,128)}, u32[]{:S(2)}) copy-start(f32[100,256]{1,0:T(8,128)} %pcs_ref.3) | copy-start | bytes 307204
  3.8 11.1 %collective-permute-start = (f32[4,104,512]{2,1,0:T(8,128)S(1)}, f32[4,104,512]{2,1,0:T(8,128)S(1)}, u32[]{:S(2)}, u32[]{:S(2)}) collective-permute-start(f32[4,104,512]{2,1,0:T(8,128)S(1)} %shard_map.41), channel_id=1, source_target_pairs={{0,1},{1,0},{2,3},{3,2},{4,5},{5,4},{6,7},{7,6},{8,9},{9,8},{10,11... | collective-permute-start | bytes 2555912 | tf_op jit(solution)/shard_map/ppermute | solution.py:242
  42.9 24.9 %all-to-all-start.2 = ((f32[16,8,128]{2,1,0:T(8,128)}), f32[16,8,128]{2,1,0:T(8,128)S(1)}, u32[]{:S(2)}, u32[]{:S(2)}) async-start(f32[16,8,128]{2,1,0:T(8,128)} %broadcast_in_dim.26), calls=%async_computation.2 | async-start | bytes 131072 | tf_op jit(solution)/shard_map/all_to_all | solution.py:225
  56.2 17.9 %collective-permute-start.1 = (f32[104,512]{1,0:T(8,128)S(1)}, f32[104,512]{1,0:T(8,128)S(1)}, u32[]{:S(2)}, u32[]{:S(2)}) collective-permute-start(f32[104,512]{1,0:T(8,128)S(1)} %get-tuple-element.21), channel_id=1, source_target_pairs={{0,2},{2,4},{4,6},{6,0},{1,3},{3,5},{5,7},{7,1},{8,10},{10,12},{12... | collective-permute-start | bytes 638984 | tf_op jit(solution)/shard_map/ppermute | solution.py:247
  58.3 15.8 %collective-permute-start.2 = (f32[104,512]{1,0:T(8,128)S(1)}, f32[104,512]{1,0:T(8,128)S(1)}, u32[]{:S(2)}, u32[]{:S(2)}) collective-permute-start(f32[104,512]{1,0:T(8,128)S(1)} %get-tuple-element.21), channel_id=1, source_target_pairs={{0,4},{2,6},{4,0},{6,2},{1,5},{3,7},{5,1},{7,3},{8,12},{10,14},{12... | collective-permute-start | bytes 638984 | tf_op jit(solution)/shard_map/ppermute | solution.py:247
  62.1 12.0 %collective-permute-start.3 = (f32[104,512]{1,0:T(8,128)S(1)}, f32[104,512]{1,0:T(8,128)S(1)}, u32[]{:S(2)}, u32[]{:S(2)}) collective-permute-start(f32[104,512]{1,0:T(8,128)S(1)} %get-tuple-element.21), channel_id=1, source_target_pairs={{0,6},{2,0},{4,2},{6,4},{1,7},{3,1},{5,3},{7,5},{8,14},{10,8},{12,... | collective-permute-start | bytes 638984 | tf_op jit(solution)/shard_map/ppermute | solution.py:247
  68.4 13.4 %all-to-all-start.3 = ((f32[32,8,128]{2,1,0:T(8,128)}), f32[32,8,128]{2,1,0:T(8,128)S(1)}, u32[]{:S(2)}, u32[]{:S(2)}) async-start(f32[32,8,128]{2,1,0:T(8,128)} %broadcast_in_dim.27), calls=%async_computation.3 | async-start | bytes 262144 | tf_op jit(solution)/shard_map/all_to_all | solution.py:225
  81.9 7.4 %collective-permute-start.4 = (f32[4,104,512]{2,1,0:T(8,128)S(1)}, f32[4,104,512]{2,1,0:T(8,128)S(1)}, u32[]{:S(2)}, u32[]{:S(2)}) collective-permute-start(f32[4,104,512]{2,1,0:T(8,128)S(1)} %pad_maximum_fusion.near_ref), channel_id=1, source_target_pairs={{0,1},{1,0},{2,3},{3,2},{4,5},{5,4},{6,7},{7,6},{8,9},{9,8},{10,11... | collective-permute-start | bytes 2555912 | tf_op jit(solution)/shard_map/ppermute | solution.py:252
  89.3 11.1 %all-to-all-start.4 = ((f32[32,4,128]{2,1,0:T(4,128)}), f32[32,4,128]{2,1,0:T(4,128)S(1)}, u32[]{:S(2)}, u32[]{:S(2)}) async-start(f32[32,4,128]{2,1,0:T(4,128)} %bitcast.8), calls=%async_computation.4 | async-start | bytes 131072 | tf_op jit(solution)/shard_map/all_to_all | solution.py:225
  93.0 2.2 %copy-start = (f32[256,4096]{1,0:T(8,128)S(1)}, f32[256,4096]{1,0:T(8,128)}, u32[]{:S(2)}) copy-start(f32[256,4096]{1,0:T(8,128)} %field_ref.5) | copy-start | bytes 12582916
  144.7 10.9 %all-to-all-start.7 = ((f32[32,4,128]{2,1,0:T(4,128)}), f32[32,4,128]{2,1,0:T(4,128)S(1)}, u32[]{:S(2)}, u32[]{:S(2)}) async-start(f32[32,4,128]{2,1,0:T(4,128)} %bitcast.12), calls=%async_computation.7 | async-start | bytes 131072 | tf_op jit(solution)/shard_map/all_to_all | solution.py:225

commit v5 on v4

--- a/solution.py
+++ b/solution.py
@@ -18,6 +18,7 @@
 F32 = jnp.float32
 VMEM = pl.BlockSpec(memory_space=pltpu.VMEM)
 LIMIT = 24 << 20
+FLOPS = 5000000000
 WIDE_LIMIT = 52 << 20
 
 
@@ -187,6 +188,7 @@
         out_shape=tuple(jax.ShapeDtypeStruct(s, F32) for s in outs),
         in_specs=[VMEM] * len(args),
         out_specs=(VMEM,) * len(outs),
+        cost_estimate=pl.CostEstimate(flops=FLOPS, bytes_accessed=0, transcendentals=0),
         compiler_params=pltpu.CompilerParams(vmem_limit_bytes=LIMIT),
     )(*args)
 
@@ -247,14 +249,13 @@
     near = [lax.ppermute(narrow, "y", [(i, (i + d) % Y) for i in range(Y)]) for d in range(1, Y)]
     chunk = swap(spread(jnp.sum(chunk, axis=0), Z), "z")
     base = swap(spread(jnp.sum(chunk, axis=0), N_PLANE), PLANE)
-    base, near = lax.optimization_barrier((base, near))
-    near = jnp.stack([narrow] + near)
-    far = lax.ppermute(near, "core", [(0, 1), (1, 0)])
     base = base.reshape(2 * PAD, PAD)
     piece = days_here // Z
     sent, y = whole(functools.partial(second_kernel, cells_total), [(PAD, PAD)] * 2, base, loadings)
 
-    sent, near, far = lax.optimization_barrier((sent, near, far))
+    sent, near = lax.optimization_barrier((sent, near))
+    near = jnp.stack([narrow] + near)
+    far = lax.ppermute(near, "core", [(0, 1), (1, 0)])
     terms = series_terms(field, near, far, jnp.stack([row, core]), days_total**0.5 / cells_total)
     chunk, terms = lax.optimization_barrier((swap(sent.reshape(N_PLANE, ROWS, PAD), PLANE), terms))
     chunk = jnp.sum(chunk, axis=0)

time: 195 us -> 196 us (level)
  blocking collectives: 98.7 us -> 117 us
  waiting for transfers between devices: 21.5 us -> 11.5 us
  starting transfers between devices: 45.7 us -> 39.2 us
    all_to_all x6 -> x7, blocking collectives: 98.7 us -> 117 us  [swap(): return lax.all_to_all(value, axes, 0, 0)]
    all_to_all x4 -> x3, waiting for transfers between devices: 21.5 us -> 10.6 us  [swap(): return lax.all_to_all(value, axes, 0, 0)]
    all_to_all x4 -> x3, starting transfers between devices: 26.2 us -> 16.6 us  [swap(): return lax.all_to_all(value, axes, 0, 0)]
    ppermute x3, starting transfers between devices: 8.49 us -> 10.7 us  [on_device(): lax.ppermute(narrow, 'y', [(i, (i + d) % Y) for i in range(Y)])]
  transfers between devices with their start and end apart: 9 -> 8, of which waited for: 4 -> 4; matrix products, arithmetic and copies ran while one was open for 0% -> 0% of each run, Pallas kernels for 5% -> 5%
where the time goes in v5:
time: 196 us; the launch traced here: 195 us
  blocking collectives  117 us (60%)
  starting transfers between devices  39.2 us (20%)
  Pallas kernels  21.9 us (11%)
  waiting for transfers between devices  11.5 us (6%)
  local copies, waits for them, and re-layouts  3.86 us (2%)
    all_to_all x7, blocking collectives, swap(): return lax.all_to_all(value, axes, 0, 0)  117 us
    all_to_all x3, starting transfers between devices, swap(): return lax.all_to_all(value, axes, 0, 0)  16.6 us
    pallas_call x3, Pallas kernels, whole(): pl.pallas_call(kernel, out_shape=tuple((jax.ShapeDtypeStruct(s, F32) for...  15.2 us
    ppermute x3, starting transfers between devices, on_device(): lax.ppermute(narrow, 'y', [(i, (i + d) % Y) for i in range(Y)])  10.7 us
    all_to_all x3, waiting for transfers between devices, swap(): return lax.all_to_all(value, axes, 0, 0)  10.6 us
    ppermute x1, starting transfers between devices, on_device(): lax.ppermute(parts(field, pcs, (1 - core)[None], scale), 'core', [(0, 1),...  8.79 us
    pallas_call x2, Pallas kernels, parts(): pl.pallas_call(functools.partial(parts_kernel, scale), out_shape=jax.Shap...  4.5 us
  transfers between devices with their start and end apart: 8, of which 4 were waited for; matrix products, arithmetic and copies ran while one was open for 0% of the time, Pallas kernels for 5%

profile of v5, /device:TPU:1, one launch (start us, length us, event | category | flops | bytes accessed | tf_op | source)
XLA Modules:
  0.0 194.7 jit_solution(10866653764945635551)
XLA Ops:
  0.6 0.0 copy-start.1
  0.6 0.9 copy-done.1
  1.5 0.0 copy-start.2
  1.5 2.2 %shard_map.41 = f32[4,104,512]{2,1,0:T(8,128)S(1)} custom-call(s32[1]{0:T(128)} %bitcast.core_ref, f32[100,256]{1,0:T(8,128)S(1)} %copy-done.1, f32[256,4096]{1,0:T(8,128)} %field_ref.5), custom_call_target="tpu_custom_call" | custom-call | flops 314572800 | bytes 2916352 | tf_op jit(solution)/shard_map/pallas_call | solution.py:111
  3.8 8.8 %collective-permute-start = (f32[4,104,512]{2,1,0:T(8,128)S(1)}, f32[4,104,512]{2,1,0:T(8,128)S(1)}, u32[]{:S(2)}, u32[]{:S(2)}) collective-permute-start(f32[4,104,512]{2,1,0:T(8,128)S(1)} %shard_map.41), channel_id=1, source_target_pairs={{0,1},{1,0},{2,3},{3,2},{4,5},{5,4},{6,7},{7,6},{8,9},{9,8},{10,11... | collective-permute-start | bytes 2555912 | tf_op jit(solution)/shard_map/ppermute | solution.py:244
  12.6 0.0 copy-done.2
  12.6 2.3 %shard_map.42 = f32[4,104,512]{2,1,0:T(8,128)S(1)} custom-call(s32[1]{0:T(128)} %bitcast.1.core_ref, f32[100,256]{1,0:T(8,128)S(1)} %copy-done.2, f32[256,4096]{1,0:T(8,128)} %field_ref.5), custom_call_target="tpu_custom_call" | custom-call | flops 314572800 | bytes 2916352 | tf_op jit(solution)/shard_map/pallas_call | solution.py:111
  14.9 0.0 collective-permute-done
  14.9 0.2 add.10
  15.0 15.5 %all_to_all.50.recv_ref = f32[4,104,512]{2,1,0:T(8,128)S(1)} all-to-all(f32[4,104,512]{2,1,0:T(8,128)S(1)} %add.10), channel_id=1, replica_groups=mesh['z'=16,'x'=4,'y'=4,'core'=2] {'y'}, dimensions={0} | all-to-all | bytes 1703936 | tf_op jit(solution)/shard_map/all_to_all | solution.py:227
  30.5 0.4 shard_map.43
  30.9 11.3 %all_to_all.51 = f32[32,8,128]{2,1,0:T(8,128)S(1)} all-to-all(f32[32,8,128]{2,1,0:T(8,128)S(1)} %bitcast.22), channel_id=1, replica_groups=mesh['z'=16,'x'=4,'y'=4,'core'=2] {'x','y','core'}, dimensions={0} | all-to-all | bytes 262144 | tf_op jit(solution)/shard_map/all_to_all | solution.py:227
  42.3 24.6 %all_to_all.52 = f32[16,8,128]{2,1,0:T(8,128)S(1)} all-to-all(f32[16,8,128]{2,1,0:T(8,128)S(1)} %broadcast_in_dim.26), channel_id=1, replica_groups=mesh['z'=16,'x'=4,'y'=4,'core'=2] {'z'}, dimensions={0} | all-to-all | bytes 131072 | tf_op jit(solution)/shard_map/all_to_all | solution.py:227
  66.9 0.7 broadcast_in_dim.27
  67.6 5.6 %all-to-all-start.3 = ((f32[32,8,128]{2,1,0:T(8,128)}), f32[32,8,128]{2,1,0:T(8,128)S(1)}, u32[]{:S(2)}, u32[]{:S(2)}) async-start(f32[32,8,128]{2,1,0:T(8,128)} %broadcast_in_dim.27), calls=%async_computation.3 | async-start | bytes 262144 | tf_op jit(solution)/shard_map/all_to_all | solution.py:227
  73.2 3.3 %collective-permute-start.1 = (f32[104,512]{1,0:T(8,128)S(1)}, f32[104,512]{1,0:T(8,128)S(1)}, u32[]{:S(2)}, u32[]{:S(2)}) collective-permute-start(f32[104,512]{1,0:T(8,128)S(1)} %get-tuple-element.20), channel_id=1, source_target_pairs={{0,2},{2,4},{4,6},{6,0},{1,3},{3,5},{5,7},{7,1},{8,10},{10,12},{12... | collective-permute-start | bytes 638984 | tf_op jit(solution)/shard_map/ppermute | solution.py:249
  76.5 4.3 %collective-permute-start.2 = (f32[104,512]{1,0:T(8,128)S(1)}, f32[104,512]{1,0:T(8,128)S(1)}, u32[]{:S(2)}, u32[]{:S(2)}) collective-permute-start(f32[104,512]{1,0:T(8,128)S(1)} %get-tuple-element.20), channel_id=1, source_target_pairs={{0,4},{2,6},{4,0},{6,2},{1,5},{3,7},{5,1},{7,3},{8,12},{10,14},{12... | collective-permute-start | bytes 638984 | tf_op jit(solution)/shard_map/ppermute | solution.py:249
  80.9 3.1 %collective-permute-start.3 = (f32[104,512]{1,0:T(8,128)S(1)}, f32[104,512]{1,0:T(8,128)S(1)}, u32[]{:S(2)}, u32[]{:S(2)}) collective-permute-start(f32[104,512]{1,0:T(8,128)S(1)} %get-tuple-element.20), channel_id=1, source_target_pairs={{0,6},{2,0},{4,2},{6,4},{1,7},{3,1},{5,3},{7,5},{8,14},{10,8},{12,... | collective-permute-start | bytes 638984 | tf_op jit(solution)/shard_map/ppermute | solution.py:249
  84.0 0.0 all-to-all-done.3
  84.0 5.0 %shard_map.44 = (f32[128,128]{1,0:T(8,128)}, f32[128,128]{1,0:T(8,128)S(1)}) custom-call(f32[256,128]{1,0:T(8,128)S(1)} %bitcast.18, f32[128,512]{1,0:T(8,128)S(1)} %get-tuple-element.18.loadings_ref), custom_call_target="tpu_custom_call" | custom-call | flops 5000000000 | tf_op jit(solution)/shard_map/pallas_call | solution.py:186
  88.9 0.0 collective-permute-done.1
  88.9 0.4 collective-permute-done.2
  89.4 0.5 collective-permute-done.3
  89.8 0.1 pad_maximum_fusion.near_ref
  89.9 3.1 %collective-permute-start.4 = (f32[4,104,512]{2,1,0:T(8,128)S(1)}, f32[4,104,512]{2,1,0:T(8,128)S(1)}, u32[]{:S(2)}, u32[]{:S(2)}) collective-permute-start(f32[4,104,512]{2,1,0:T(8,128)S(1)} %pad_maximum_fusion.near_ref), channel_id=1, source_target_pairs={{0,1},{1,0},{2,3},{3,2},{4,5},{5,4},{6,7},{7,6},{8,9},{9,8},{10,11... | collective-permute-start | bytes 2555912 | tf_op jit(solution)/shard_map/ppermute | solution.py:258
  93.0 0.1 pad_add_fusion.where_ref
  93.1 7.3 %all-to-all-start.4 = ((f32[32,4,128]{2,1,0:T(4,128)}), f32[32,4,128]{2,1,0:T(4,128)S(1)}, u32[]{:S(2)}, u32[]{:S(2)}) async-start(f32[32,4,128]{2,1,0:T(4,128)} %bitcast.4), calls=%async_computation.4 | async-start | bytes 131072 | tf_op jit(solution)/shard_map/all_to_all | solution.py:227
  100.4 0.0 collective-permute-done.4.far_ref
  100.4 0.0 copy-start
  100.4 2.2 %copy-done = f32[256,4096]{1,0:T(8,128)S(1)} copy-done((f32[256,4096]{1,0:T(8,128)S(1)}, f32[256,4096]{1,0:T(8,128)}, u32[]{:S(2)}) %copy-start) | copy-done | bytes 4194328
  102.6 1.8 shard_map.45
  104.4 3.3 %all-to-all-done.4 = f32[32,4,128]{2,1,0:T(4,128)S(1)} async-done(((f32[32,4,128]{2,1,0:T(4,128)}), f32[32,4,128]{2,1,0:T(4,128)S(1)}, u32[]{:S(2)}, u32[]{:S(2)}) %all-to-all-start.4) | async-done | bytes 65568 | tf_op jit(solution)/shard_map/all_to_all | solution.py:227
  107.9 15.6 %all_to_all.53 = f32[16,20,128]{2,1,0:T(8,128)S(1)} all-to-all(f32[16,20,128]{2,1,0:T(8,128)S(1)} %pad_maximum_fusion.1), channel_id=1, replica_groups=mesh['z'=16,'x'=4,'y'=4,'core'=2] {'z'}, dimensions={0} | all-to-all | bytes 327680 | tf_op jit(solution)/shard_map/all_to_all | solution.py:227
  123.5 17.0 %all_to_all.54 = f32[32,20,128]{2,1,0:T(8,128)S(1)} all-to-all(f32[32,20,128]{2,1,0:T(8,128)S(1)} %broadcast_in_dim.29), channel_id=1, replica_groups=mesh['z'=16,'x'=4,'y'=4,'core'=2] {'x','y','core'}, dimensions={0} | all-to-all | bytes 655360 | tf_op jit(solution)/shard_map/all_to_all | solution.py:227
  140.5 5.1 %shard_map.46 = (f32[128,128]{1,0:T(8,128)}, f32[128,128]{1,0:T(8,128)S(1)}) custom-call(f32[128,128]{1,0:T(8,128)S(1)} %bitcast.24, f32[256,128]{1,0:T(8,128)S(1)} %bitcast.19, f32[128,128]{1,0:T(8,128)S(1)} %get-tuple-element.27.y_ref, f32[128,512]{1,0:T(8,128)S(1)} %get-tuple-element.18.loadings_ref), custom_call_target="tpu_custom_call" | custom-call | flops 5000000000 | tf_op jit(solution)/shard_map/pallas_call | solution.py:186
  145.6 3.6 %all-to-all-start.7 = ((f32[32,4,128]{2,1,0:T(4,128)}), f32[32,4,128]{2,1,0:T(4,128)S(1)}, u32[]{:S(2)}, u32[]{:S(2)}) async-start(f32[32,4,128]{2,1,0:T(4,128)} %bitcast.12), calls=%async_computation.7 | async-start | bytes 131072 | tf_op jit(solution)/shard_map/all_to_all | solution.py:227
  149.3 7.2 %all-to-all-done.7 = f32[32,4,128]{2,1,0:T(4,128)S(1)} async-done(((f32[32,4,128]{2,1,0:T(4,128)}), f32[32,4,128]{2,1,0:T(4,128)S(1)}, u32[]{:S(2)}, u32[]{:S(2)}) %all-to-all-start.7) | async-done | bytes 65568 | tf_op jit(solution)/shard_map/all_to_all | solution.py:227
  156.6 18.5 %all_to_all.55 = f32[16,20,128]{2,1,0:T(8,128)S(1)} all-to-all(f32[16,20,128]{2,1,0:T(8,128)S(1)} %broadcast_in_dim.30), channel_id=1, replica_groups=mesh['z'=16,'x'=4,'y'=4,'core'=2] {'z'}, dimensions={0} | all-to-all | bytes 327680 | tf_op jit(solution)/shard_map/all_to_all | solution.py:227
  175.1 14.5 %all_to_all.56 = f32[32,4,128]{2,1,0:T(4,128)S(1)} all-to-all(f32[32,4,128]{2,1,0:T(4,128)S(1)} %broadcast_in_dim.31), channel_id=1, replica_groups=mesh['z'=16,'x'=4,'y'=4,'core'=2] {'x','y','core'}, dimensions={0} | all-to-all | bytes 131072 | tf_op jit(solution)/shard_map/all_to_all | solution.py:227
  189.7 5.1 %shard_map.47 = (f32[100,512]{1,0:T(8,128)}, f32[100,256]{1,0:T(8,128)}) custom-call(f32[128,128]{1,0:T(8,128)S(1)} %bitcast.23, f32[256,128]{1,0:T(8,128)S(1)} %bitcast.20, f32[128,128]{1,0:T(8,128)S(1)} %get-tuple-element.30.y_ref, f32[128,512]{1,0:T(8,128)S(1)} %get-tuple-element.18.loadings_ref, f32[256,128]{1,0:T(8,128)S(1)} %bitcast.21), custom_call_target="tpu_custom_call" | custom-call | flops 5000000000 | tf_op jit(solution)/shard_map/pallas_call | solution.py:186
  (17 shorter events, 0.4 us)
Async XLA Ops:
  0.6 0.9 copy-start.1
  1.5 11.0 %copy-start.2 = (f32[100,256]{1,0:T(8,128)S(1)}, f32[100,256]{1,0:T(8,128)}, u32[]{:S(2)}) copy-start(f32[100,256]{1,0:T(8,128)} %pcs_ref.3) | copy-start | bytes 307204
  3.8 11.1 %collective-permute-start = (f32[4,104,512]{2,1,0:T(8,128)S(1)}, f32[4,104,512]{2,1,0:T(8,128)S(1)}, u32[]{:S(2)}, u32[]{:S(2)}) collective-permute-start(f32[4,104,512]{2,1,0:T(8,128)S(1)} %shard_map.41), channel_id=1, source_target_pairs={{0,1},{1,0},{2,3},{3,2},{4,5},{5,4},{6,7},{7,6},{8,9},{9,8},{10,11... | collective-permute-start | bytes 2555912 | tf_op jit(solution)/shard_map/ppermute | solution.py:244
  67.6 16.4 %all-to-all-start.3 = ((f32[32,8,128]{2,1,0:T(8,128)}), f32[32,8,128]{2,1,0:T(8,128)S(1)}, u32[]{:S(2)}, u32[]{:S(2)}) async-start(f32[32,8,128]{2,1,0:T(8,128)} %broadcast_in_dim.27), calls=%async_computation.3 | async-start | bytes 262144 | tf_op jit(solution)/shard_map/all_to_all | solution.py:227
  73.2 15.7 %collective-permute-start.1 = (f32[104,512]{1,0:T(8,128)S(1)}, f32[104,512]{1,0:T(8,128)S(1)}, u32[]{:S(2)}, u32[]{:S(2)}) collective-permute-start(f32[104,512]{1,0:T(8,128)S(1)} %get-tuple-element.20), channel_id=1, source_target_pairs={{0,2},{2,4},{4,6},{6,0},{1,3},{3,5},{5,7},{7,1},{8,10},{10,12},{12... | collective-permute-start | bytes 638984 | tf_op jit(solution)/shard_map/ppermute | solution.py:249
  76.5 12.8 %collective-permute-start.2 = (f32[104,512]{1,0:T(8,128)S(1)}, f32[104,512]{1,0:T(8,128)S(1)}, u32[]{:S(2)}, u32[]{:S(2)}) collective-permute-start(f32[104,512]{1,0:T(8,128)S(1)} %get-tuple-element.20), channel_id=1, source_target_pairs={{0,4},{2,6},{4,0},{6,2},{1,5},{3,7},{5,1},{7,3},{8,12},{10,14},{12... | collective-permute-start | bytes 638984 | tf_op jit(solution)/shard_map/ppermute | solution.py:249
  80.9 9.0 %collective-permute-start.3 = (f32[104,512]{1,0:T(8,128)S(1)}, f32[104,512]{1,0:T(8,128)S(1)}, u32[]{:S(2)}, u32[]{:S(2)}) collective-permute-start(f32[104,512]{1,0:T(8,128)S(1)} %get-tuple-element.20), channel_id=1, source_target_pairs={{0,6},{2,0},{4,2},{6,4},{1,7},{3,1},{5,3},{7,5},{8,14},{10,8},{12,... | collective-permute-start | bytes 638984 | tf_op jit(solution)/shard_map/ppermute | solution.py:249
  89.9 10.5 %collective-permute-start.4 = (f32[4,104,512]{2,1,0:T(8,128)S(1)}, f32[4,104,512]{2,1,0:T(8,128)S(1)}, u32[]{:S(2)}, u32[]{:S(2)}) collective-permute-start(f32[4,104,512]{2,1,0:T(8,128)S(1)} %pad_maximum_fusion.near_ref), channel_id=1, source_target_pairs={{0,1},{1,0},{2,3},{3,2},{4,5},{5,4},{6,7},{7,6},{8,9},{9,8},{10,11... | collective-permute-start | bytes 2555912 | tf_op jit(solution)/shard_map/ppermute | solution.py:258
  93.1 14.7 %all-to-all-start.4 = ((f32[32,4,128]{2,1,0:T(4,128)}), f32[32,4,128]{2,1,0:T(4,128)S(1)}, u32[]{:S(2)}, u32[]{:S(2)}) async-start(f32[32,4,128]{2,1,0:T(4,128)} %bitcast.4), calls=%async_computation.4 | async-start | bytes 131072 | tf_op jit(solution)/shard_map/all_to_all | solution.py:227
  100.4 2.2 %copy-start = (f32[256,4096]{1,0:T(8,128)S(1)}, f32[256,4096]{1,0:T(8,128)}, u32[]{:S(2)}) copy-start(f32[256,4096]{1,0:T(8,128)} %field_ref.5) | copy-start | bytes 12582916
  145.6 10.9 %all-to-all-start.7 = ((f32[32,4,128]{2,1,0:T(4,128)}), f32[32,4,128]{2,1,0:T(4,128)S(1)}, u32[]{:S(2)}, u32[]{:S(2)}) async-start(f32[32,4,128]{2,1,0:T(4,128)} %bitcast.12), calls=%async_computation.7 | async-start | bytes 131072 | tf_op jit(solution)/shard_map/all_to_all | solution.py:227

commit v6 on v3

--- a/solution.py
+++ b/solution.py
@@ -18,6 +18,9 @@
 F32 = jnp.float32
 VMEM = pl.BlockSpec(memory_space=pltpu.VMEM)
 LIMIT = 24 << 20
+FLOPS = 5000000000
+WIDE_LIMIT = 48 << 20
+TERMS_LIMIT = 51 << 20
 
 
 def split(value):
@@ -60,12 +63,9 @@
     y = grad / (norm + 1e-06)
     for step in range(NS_STEPS):
         high, low = split(y)
-        down = jnp.concatenate([high, low], axis=0)
-        across = jnp.concatenate([high, low], axis=1)
-        inner = fold(nt(across, jnp.concatenate([down, down], axis=1)))
+        inner = fold(nt(high, jnp.concatenate([high, low], axis=0))) + nt(low, high)
         ih, il = split(inner)
-        again = jnp.concatenate([across, across], axis=0)
-        y = 1.5 * y - 0.5 * fold(nn(jnp.concatenate([ih, il], axis=1), again))
+        y = 1.5 * y - 0.5 * (fold(nn(ih, jnp.concatenate([high, low], axis=1))) + nn(il, high))
     return y
 
 
@@ -78,35 +78,78 @@
     return field_ref[:, pl.ds(pl.multiple_of(group * share, share), share)]
 
 
-def parts_kernel(scale, core_ref, pcs_ref, field_ref, out_ref, wide):
-    wide[...] = jnp.zeros_like(wide)
-    wide[0 : pcs_ref.shape[0]] = pcs_ref[...] * scale
-    half = wide.shape[0]
-    left_high, left_low = split(wide[...])
+def some_parts(left_high, left_low, field_ref, out_ref, owner, ready):
     left = jnp.concatenate([left_high, left_low], axis=0)
+    half = left_high.shape[0]
     for g in range(Y):
-        high, low = split(columns(field_ref, CORE * g + core_ref[0], out_ref.shape[2]))
+        ready(g)
+        high, low = split(columns(field_ref, CORE * g + owner, out_ref.shape[2]))
         both = nn(left, high)
         total = both[0:half] + both[half : 2 * half] + nn(left_high, low)
         out_ref[g] = total[0 : out_ref.shape[1]]
 
 
-def parts(field, pcs, core, scale):
+def scaled(pcs, wide, scale):
+    wide[...] = jnp.zeros_like(wide)
+    wide[0 : pcs.shape[0]] = pcs * scale
+    return split(wide[...])
+
+
+def their_parts_kernel(scale, core_ref, pcs_ref, field_ref, out_ref, kept_ref, wide, sems):
+    share = out_ref.shape[2]
+    theirs = 1 - core_ref[0]
+    copies = []
+    for owner in (theirs, core_ref[0]):
+        for g in range(Y):
+            place = pl.ds(pl.multiple_of((CORE * g + owner) * share, share), share)
+            copies.append(
+                pltpu.make_async_copy(field_ref.at[:, place], kept_ref.at[:, place], sems.at[len(copies)])
+            )
+    for copy in copies:
+        copy.start()
+    left_high, left_low = scaled(pcs_ref[...], wide, scale)
+    some_parts(left_high, left_low, kept_ref, out_ref, theirs, lambda g: copies[g].wait())
+    for copy in copies[Y:]:
+        copy.wait()
+
+
+def own_parts_kernel(scale, core_ref, pcs_ref, kept_ref, out_ref, wide):
+    left_high, left_low = scaled(pcs_ref[...], wide, scale)
+    some_parts(left_high, left_low, kept_ref, out_ref, core_ref[0], lambda g: None)
+
+
+def their_parts(field, pcs, core, scale):
     k, days = pcs.shape
     share = field.shape[1] // (Y * CORE)
     half = (k + 15) // 16 * 16
     rows = (k + 7) // 8 * 8
     return pl.pallas_call(
-        functools.partial(parts_kernel, scale),
+        functools.partial(their_parts_kernel, scale),
+        out_shape=(jax.ShapeDtypeStruct((Y, rows, share), F32), jax.ShapeDtypeStruct(field.shape, F32)),
+        in_specs=[pl.BlockSpec(memory_space=pltpu.SMEM), VMEM, pl.BlockSpec(memory_space=pl.ANY)],
+        out_specs=(VMEM, VMEM),
+        scratch_shapes=[pltpu.VMEM((half, days), F32), pltpu.SemaphoreType.DMA((Y * CORE,))],
+        cost_estimate=pl.CostEstimate(
+            flops=6 * k * days * share * Y, bytes_accessed=4 * days * (field.shape[1] + k), transcendentals=0
+        ),
+        compiler_params=pltpu.CompilerParams(vmem_limit_bytes=WIDE_LIMIT),
+    )(core, pcs, field)
+
+
+def own_parts(kept, pcs, core, scale):
+    k, days = pcs.shape
+    share = kept.shape[1] // (Y * CORE)
+    half = (k + 15) // 16 * 16
+    rows = (k + 7) // 8 * 8
+    return pl.pallas_call(
+        functools.partial(own_parts_kernel, scale),
         out_shape=jax.ShapeDtypeStruct((Y, rows, share), F32),
         in_specs=[pl.BlockSpec(memory_space=pltpu.SMEM), VMEM, VMEM],
         out_specs=VMEM,
         scratch_shapes=[pltpu.VMEM((half, days), F32)],
-        cost_estimate=pl.CostEstimate(
-            flops=6 * k * days * share * Y, bytes_accessed=4 * Y * share * (days + k), transcendentals=0
-        ),
+        cost_estimate=pl.CostEstimate(flops=6 * k * days * share * Y, bytes_accessed=0, transcendentals=0),
         compiler_params=pltpu.CompilerParams(vmem_limit_bytes=LIMIT),
-    )(core, pcs, field)
+    )(core, pcs, kept)
 
 
 def first_kernel(recv_ref, sent_ref, loadings_ref, padded_ref):
@@ -171,20 +214,30 @@
         out_shape=tuple(jax.ShapeDtypeStruct(s, F32) for s in outs),
         in_specs=[VMEM] * len(args),
         out_specs=(VMEM,) * len(outs),
+        cost_estimate=pl.CostEstimate(flops=FLOPS, bytes_accessed=0, transcendentals=0),
         compiler_params=pltpu.CompilerParams(vmem_limit_bytes=LIMIT),
     )(*args)
 
 
-def terms_kernel(scale, where_ref, field_ref, near_ref, far_ref, out_ref):
+def terms_kernel(scale, where_ref, field_ref, near_ref, far_ref, out_ref, field, sems):
     row, core = where_ref[0], where_ref[1]
     share = near_ref.shape[2]
+    copies = []
+    for d in range(Y):
+        for owner in (core, 1 - core):
+            start = pl.multiple_of((CORE * (row ^ d) + owner) * share, share)
+            slot = len(copies)
+            copies.append(
+                pltpu.make_async_copy(field_ref.at[:, pl.ds(start, share)], field.at[slot], sems.at[slot])
+            )
+    for copy in copies:
+        copy.start()
     total = jnp.zeros(out_ref.shape, F32)
-    for d in range(Y):
-        group = CORE * lax.rem(row + Y - d, Y)
-        for owner, loadings in ((core, near_ref[d]), (1 - core, far_ref[d])):
-            lh, ll = split(pad_rows(loadings, PAD))
-            high, low = split(columns(field_ref, group + owner, share))
-            total += fold(nt(high, jnp.concatenate([lh, ll], axis=0))) + nt(low, lh)
+    for slot in range(Y * CORE):
+        lh, ll = split(pad_rows((far_ref if slot % CORE else near_ref)[slot // CORE], PAD))
+        copies[slot].wait()
+        high, low = split(field[slot])
+        total += fold(nt(high, jnp.concatenate([lh, ll], axis=0))) + nt(low, lh)
     out_ref[...] = total * scale
 
 
@@ -194,14 +247,20 @@
     return pl.pallas_call(
         functools.partial(terms_kernel, scale),
         out_shape=jax.ShapeDtypeStruct((days, PAD), F32),
-        in_specs=[pl.BlockSpec(memory_space=pltpu.SMEM), VMEM, VMEM, VMEM],
+        in_specs=[
+            pl.BlockSpec(memory_space=pltpu.SMEM),
+            pl.BlockSpec(memory_space=pl.ANY),
+            VMEM,
+            VMEM,
+        ],
         out_specs=VMEM,
+        scratch_shapes=[pltpu.VMEM((Y * CORE, days, share), F32), pltpu.SemaphoreType.DMA((Y * CORE,))],
         cost_estimate=pl.CostEstimate(
             flops=6 * days * PAD * share * Y * CORE,
             bytes_accessed=4 * Y * CORE * share * (days + rows),
             transcendentals=0,
         ),
-        compiler_params=pltpu.CompilerParams(vmem_limit_bytes=LIMIT),
+        compiler_params=pltpu.CompilerParams(vmem_limit_bytes=TERMS_LIMIT),
     )(where, field, near, far)
 
 
@@ -223,22 +282,25 @@
     row = lax.axis_index("y").astype(jnp.int32)
 
     scale = 1.0 / days_total**0.5
-    theirs = lax.ppermute(parts(field, pcs, (1 - core)[None], scale), "core", [(0, 1), (1, 0)])
-    recv = swap(theirs + parts(field, pcs, core[None], scale), "y")
+    theirs, kept = their_parts(field, pcs, core[None], scale)
+    theirs = lax.ppermute(theirs, "core", [(0, 1), (1, 0)])
+    recv = swap(theirs + own_parts(kept, pcs, core[None], scale), "y")
     sent, narrow, loadings = first(recv)
 
     chunk = swap(sent.reshape(N_PLANE, 2 * ROWS, PAD), PLANE)
-    near = [lax.ppermute(narrow, "y", [(i, (i + d) % Y) for i in range(Y)]) for d in range(1, Y)]
+    near = lax.ppermute(narrow, "y", [(i, i ^ 1) for i in range(Y)])
     chunk = swap(spread(jnp.sum(chunk, axis=0), Z), "z")
+    chunk, near = lax.optimization_barrier((chunk, near))
+    pair = jnp.stack([narrow, near])
+    near = lax.ppermute(pair, "y", [(i, i ^ 2) for i in range(Y)])
     base = swap(spread(jnp.sum(chunk, axis=0), N_PLANE), PLANE)
-    base, near = lax.optimization_barrier((base, near))
-    near = jnp.stack([narrow] + near)
-    far = lax.ppermute(near, "core", [(0, 1), (1, 0)])
     base = base.reshape(2 * PAD, PAD)
     piece = days_here // Z
     sent, y = whole(functools.partial(second_kernel, cells_total), [(PAD, PAD)] * 2, base, loadings)
 
-    sent, near, far = lax.optimization_barrier((sent, near, far))
+    sent, near = lax.optimization_barrier((sent, near))
+    near = jnp.concatenate([pair, near], axis=0)
+    far = lax.ppermute(near, "core", [(0, 1), (1, 0)])
     terms = series_terms(field, near, far, jnp.stack([row, core]), days_total**0.5 / cells_total)
     chunk, terms = lax.optimization_barrier((swap(sent.reshape(N_PLANE, ROWS, PAD), PLANE), terms))
     chunk = jnp.sum(chunk, axis=0)
@@ -255,7 +317,7 @@
     chunk = jnp.sum(swap(sent.reshape(N_PLANE, ROWS, PAD), PLANE), axis=0)
     got = swap(spread(jnp.concatenate([chunk, terms], axis=0), Z), "z")
     terms = got[:, ROWS:].reshape(days_here, PAD)
-    chunk = jnp.sum(got[:, :ROWS], axis=0)
+    chunk, terms = lax.optimization_barrier((jnp.sum(got[:, :ROWS], axis=0), terms))
     cube = swap(spread(chunk, N_PLANE), PLANE).reshape(PAD, PAD)
     return whole(
         functools.partial(last_kernel, cells_total),

time: 196 us -> 198 us (1.010)
  blocking collectives: 84.2 us -> 97.3 us
  starting transfers between devices: 53.2 us -> 47.4 us
  local copies, waits for them, and re-layouts: 7.31 us -> 2.31 us
  Pallas kernels: 18.6 us -> 22.3 us
  waiting for transfers between devices: 30.2 us -> 26.9 us
    all_to_all x5 -> x6, blocking collectives: 84.2 us -> 97.3 us  [swap(): return lax.all_to_all(value, axes, 0, 0)]
    all_to_all x5 -> x4, waiting for transfers between devices: 28.9 us -> 16.7 us  [swap(): return lax.all_to_all(value, axes, 0, 0)]
    ppermute x4 -> x3, waiting for transfers between devices: 1.38 us -> 10.3 us  [the longest x1 5.85 us: on_device(): near = lax.ppermute(narrow, 'y', [(i, i ^ 1) for i in range(Y)])]
    all_to_all x5 -> x4, starting transfers between devices: 33.5 us -> 28.9 us  [swap(): return lax.all_to_all(value, axes, 0, 0)]
    unnamed x8 -> x2, local copies, waits for them, and re-layouts: 5.27 us -> 0.89 us
    pallas_call x1, Pallas kernels: 1.81 us -> 4.43 us  [series_terms(): pl.pallas_call(functools.partial(terms_kernel, scale), out_shape=jax.Shap...]
    ppermute x4 -> x3, starting transfers between devices: 17.4 us -> 15.8 us  [the longest x1 8.79 us: on_device(): theirs = lax.ppermute(theirs, 'core', [(0, 1), (1, 0)])]
  transfers between devices with their start and end apart: 10 -> 8, of which waited for: 6 -> 7; matrix products, arithmetic and copies ran while one was open for 0% -> 0% of each run, Pallas kernels for 4% -> 5%
where the time goes in v6:
time: 198 us
  blocking collectives  97.3 us (49%)
  starting transfers between devices  47.4 us (24%)
  waiting for transfers between devices  26.9 us (14%)
  Pallas kernels  22.3 us (11%)
  local copies, waits for them, and re-layouts  2.31 us (1%)
    all_to_all x6, blocking collectives, swap(): return lax.all_to_all(value, axes, 0, 0)  97.3 us
    all_to_all x4, starting transfers between devices, swap(): return lax.all_to_all(value, axes, 0, 0)  28.9 us
    all_to_all x4, waiting for transfers between devices, swap(): return lax.all_to_all(value, axes, 0, 0)  16.7 us
    pallas_call x3, Pallas kernels, whole(): pl.pallas_call(kernel, out_shape=tuple((jax.ShapeDtypeStruct(s, F32) for...  14.6 us
    ppermute x1, starting transfers between devices, on_device(): theirs = lax.ppermute(theirs, 'core', [(0, 1), (1, 0)])  8.79 us
    ppermute x1, waiting for transfers between devices, on_device(): near = lax.ppermute(narrow, 'y', [(i, i ^ 1) for i in range(Y)])  5.85 us
    ppermute x1, starting transfers between devices, on_device(): near = lax.ppermute(pair, 'y', [(i, i ^ 2) for i in range(Y)])  4.82 us
    pallas_call x1, Pallas kernels, series_terms(): pl.pallas_call(functools.partial(terms_kernel, scale), out_shape=jax.Shap...  4.43 us
  transfers between devices with their start and end apart: 8, of which 7 were waited for; matrix products, arithmetic and copies ran while one was open for 0% of the time, Pallas kernels for 5%

profile of v6, /device:TPU:1, one launch (start us, length us, event | category | flops | bytes accessed | tf_op | source)
XLA Modules:
  0.0 197.7 jit_solution(130278013285937310)
XLA Ops:
  0.6 0.0 copy-start
  0.6 0.9 copy-done
  1.5 2.2 %shard_map.41 = (f32[4,104,512]{2,1,0:T(8,128)S(1)}, f32[256,4096]{1,0:T(8,128)S(1)}) custom-call(s32[1]{0:T(128)} %bitcast.core_ref, f32[100,256]{1,0:T(8,128)S(1)} %copy-done, f32[256,4096]{1,0:T(8,128)} %field_ref.3), custom_call_target="tpu_custom_call" | custom-call | flops 314572800 | bytes 4296704 | tf_op jit(solution)/shard_map/pallas_call | solution.py:126
  3.8 8.8 %collective-permute-start = (f32[4,104,512]{2,1,0:T(8,128)S(1)}, f32[4,104,512]{2,1,0:T(8,128)S(1)}, u32[]{:S(2)}, u32[]{:S(2)}) collective-permute-start(f32[4,104,512]{2,1,0:T(8,128)S(1)} %get-tuple-element.19), channel_id=1, source_target_pairs={{0,1},{1,0},{2,3},{3,2},{4,5},{5,4},{6,7},{7,6},{8,9},{9,8},{10,11... | collective-permute-start | bytes 2555912 | tf_op jit(solution)/shard_map/ppermute | solution.py:286
  12.6 0.6 shard_map.42
  13.2 1.4 collective-permute-done
  14.6 0.2 add.10
  14.7 14.8 %all_to_all.50.recv_ref = f32[4,104,512]{2,1,0:T(8,128)S(1)} all-to-all(f32[4,104,512]{2,1,0:T(8,128)S(1)} %add.10), channel_id=1, replica_groups=mesh['z'=16,'x'=4,'y'=4,'core'=2] {'y'}, dimensions={0} | all-to-all | bytes 1703936 | tf_op jit(solution)/shard_map/all_to_all | solution.py:268
  29.6 0.4 shard_map.43
  30.0 11.9 %all_to_all.51 = f32[32,8,128]{2,1,0:T(8,128)S(1)} all-to-all(f32[32,8,128]{2,1,0:T(8,128)S(1)} %bitcast.20), channel_id=1, replica_groups=mesh['z'=16,'x'=4,'y'=4,'core'=2] {'x','y','core'}, dimensions={0} | all-to-all | bytes 262144 | tf_op jit(solution)/shard_map/all_to_all | solution.py:268
  41.9 0.6 broadcast_in_dim.23
  42.6 13.2 %all-to-all-start.2 = ((f32[16,8,128]{2,1,0:T(8,128)}), f32[16,8,128]{2,1,0:T(8,128)S(1)}, u32[]{:S(2)}, u32[]{:S(2)}) async-start(f32[16,8,128]{2,1,0:T(8,128)} %broadcast_in_dim.23), calls=%async_computation.2 | async-start | bytes 131072 | tf_op jit(solution)/shard_map/all_to_all | solution.py:268
  55.8 2.2 %collective-permute-start.1 = (f32[104,512]{1,0:T(8,128)S(1)}, f32[104,512]{1,0:T(8,128)S(1)}, u32[]{:S(2)}, u32[]{:S(2)}) collective-permute-start(f32[104,512]{1,0:T(8,128)S(1)} %get-tuple-element.22), channel_id=1, source_target_pairs={{0,2},{2,0},{4,6},{6,4},{1,3},{3,1},{5,7},{7,5},{8,10},{10,8},{12,... | collective-permute-start | bytes 638984 | tf_op jit(solution)/shard_map/ppermute | solution.py:291
  58.0 5.8 %collective-permute-done.1 = f32[104,512]{1,0:T(8,128)S(1)} collective-permute-done((f32[104,512]{1,0:T(8,128)S(1)}, f32[104,512]{1,0:T(8,128)S(1)}, u32[]{:S(2)}, u32[]{:S(2)}) %collective-permute-start.1) | collective-permute-done | bytes 213024 | tf_op jit(solution)/shard_map/ppermute | solution.py:291
  63.8 3.6 %all-to-all-done.2 = f32[16,8,128]{2,1,0:T(8,128)S(1)} async-done(((f32[16,8,128]{2,1,0:T(8,128)}), f32[16,8,128]{2,1,0:T(8,128)S(1)}, u32[]{:S(2)}, u32[]{:S(2)}) %all-to-all-start.2) | async-done | bytes 65568 | tf_op jit(solution)/shard_map/all_to_all | solution.py:268
  67.4 0.7 broadcast_in_dim.24
  68.1 5.6 %all-to-all-start.3 = ((f32[32,8,128]{2,1,0:T(8,128)}), f32[32,8,128]{2,1,0:T(8,128)S(1)}, u32[]{:S(2)}, u32[]{:S(2)}) async-start(f32[32,8,128]{2,1,0:T(8,128)} %broadcast_in_dim.24), calls=%async_computation.3 | async-start | bytes 262144 | tf_op jit(solution)/shard_map/all_to_all | solution.py:268
  73.8 4.8 %collective-permute-start.2 = (f32[2,104,512]{2,1,0:T(8,128)S(1)}, f32[2,104,512]{2,1,0:T(8,128)S(1)}, u32[]{:S(2)}, u32[]{:S(2)}) collective-permute-start(f32[2,104,512]{2,1,0:T(8,128)S(1)} %pad_maximum_fusion.1), channel_id=1, source_target_pairs={{0,4},{2,6},{4,0},{6,2},{1,5},{3,7},{5,1},{7,3},{8,12},{10,14},{12... | collective-permute-start | bytes 1277960 | tf_op jit(solution)/shard_map/ppermute | solution.py:295
  78.6 3.0 %all-to-all-done.3 = f32[32,8,128]{2,1,0:T(8,128)S(1)} async-done(((f32[32,8,128]{2,1,0:T(8,128)}), f32[32,8,128]{2,1,0:T(8,128)S(1)}, u32[]{:S(2)}, u32[]{:S(2)}) %all-to-all-start.3) | async-done | bytes 131104 | tf_op jit(solution)/shard_map/all_to_all | solution.py:268
  81.6 4.8 %shard_map.44 = (f32[128,128]{1,0:T(8,128)}, f32[128,128]{1,0:T(8,128)S(1)}) custom-call(f32[256,128]{1,0:T(8,128)S(1)} %bitcast.16, f32[128,512]{1,0:T(8,128)S(1)} %get-tuple-element.24.loadings_ref), custom_call_target="tpu_custom_call" | custom-call | flops 5000000000 | tf_op jit(solution)/shard_map/pallas_call | solution.py:212
  86.4 3.0 %collective-permute-done.2 = f32[2,104,512]{2,1,0:T(8,128)S(1)} collective-permute-done((f32[2,104,512]{2,1,0:T(8,128)S(1)}, f32[2,104,512]{2,1,0:T(8,128)S(1)}, u32[]{:S(2)}, u32[]{:S(2)}) %collective-permute-start.2) | collective-permute-done | bytes 426016 | tf_op jit(solution)/shard_map/ppermute | solution.py:295
  89.4 0.1 pad_maximum_fusion.near_ref
  89.5 2.7 %collective-permute-start.3 = (f32[4,104,512]{2,1,0:T(8,128)S(1)}, f32[4,104,512]{2,1,0:T(8,128)S(1)}, u32[]{:S(2)}, u32[]{:S(2)}) collective-permute-start(f32[4,104,512]{2,1,0:T(8,128)S(1)} %pad_maximum_fusion.near_ref), channel_id=1, source_target_pairs={{0,1},{1,0},{2,3},{3,2},{4,5},{5,4},{6,7},{7,6},{8,9},{9,8},{10,11... | collective-permute-start | bytes 2555912 | tf_op jit(solution)/shard_map/ppermute | solution.py:303
  92.2 0.1 pad_add_fusion.where_ref
  92.3 6.4 %all-to-all-start.4 = ((f32[32,4,128]{2,1,0:T(4,128)}), f32[32,4,128]{2,1,0:T(4,128)S(1)}, u32[]{:S(2)}, u32[]{:S(2)}) async-start(f32[32,4,128]{2,1,0:T(4,128)} %bitcast.5), calls=%async_computation.4 | async-start | bytes 131072 | tf_op jit(solution)/shard_map/all_to_all | solution.py:268
  98.7 0.0 collective-permute-done.3.far_ref
  98.7 4.4 %shard_map.45 = f32[256,128]{1,0:T(8,128)S(1)} custom-call(s32[2]{0:T(128)S(1)} %pad_add_fusion.where_ref, f32[256,4096]{1,0:T(8,128)} %field_ref.3, f32[4,104,512]{2,1,0:T(8,128)S(1)} %pad_maximum_fusion.near_ref, f32[4,104,512]{2,1,0:T(8,128)S(1)} %collective-permute-done.3.far_ref), custom_call_target="tpu_custom_call" | custom-call | flops 805306368 | bytes 5898240 | tf_op jit(solution)/shard_map/pallas_call | solution.py:247
  103.2 2.9 %all-to-all-done.4 = f32[32,4,128]{2,1,0:T(4,128)S(1)} async-done(((f32[32,4,128]{2,1,0:T(4,128)}), f32[32,4,128]{2,1,0:T(4,128)S(1)}, u32[]{:S(2)}, u32[]{:S(2)}) %all-to-all-start.4) | async-done | bytes 65568 | tf_op jit(solution)/shard_map/all_to_all | solution.py:268
  106.2 20.0 %all_to_all.52 = f32[16,20,128]{2,1,0:T(8,128)S(1)} all-to-all(f32[16,20,128]{2,1,0:T(8,128)S(1)} %pad_maximum_fusion.2), channel_id=1, replica_groups=mesh['z'=16,'x'=4,'y'=4,'core'=2] {'z'}, dimensions={0} | all-to-all | bytes 327680 | tf_op jit(solution)/shard_map/all_to_all | solution.py:268
  126.2 17.6 %all_to_all.53 = f32[32,20,128]{2,1,0:T(8,128)S(1)} all-to-all(f32[32,20,128]{2,1,0:T(8,128)S(1)} %broadcast_in_dim.26), channel_id=1, replica_groups=mesh['z'=16,'x'=4,'y'=4,'core'=2] {'x','y','core'}, dimensions={0} | all-to-all | bytes 655360 | tf_op jit(solution)/shard_map/all_to_all | solution.py:268
  143.8 4.9 %shard_map.46 = (f32[128,128]{1,0:T(8,128)}, f32[128,128]{1,0:T(8,128)S(1)}) custom-call(f32[128,128]{1,0:T(8,128)S(1)} %bitcast.22, f32[256,128]{1,0:T(8,128)S(1)} %bitcast.17, f32[128,128]{1,0:T(8,128)S(1)} %get-tuple-element.31.y_ref, f32[128,512]{1,0:T(8,128)S(1)} %get-tuple-element.24.loadings_ref), custom_call_target="tpu_custom_call" | custom-call | flops 5000000000 | tf_op jit(solution)/shard_map/pallas_call | solution.py:212
  148.8 3.6 %all-to-all-start.7 = ((f32[32,4,128]{2,1,0:T(4,128)}), f32[32,4,128]{2,1,0:T(4,128)S(1)}, u32[]{:S(2)}, u32[]{:S(2)}) async-start(f32[32,4,128]{2,1,0:T(4,128)} %bitcast.9), calls=%async_computation.7 | async-start | bytes 131072 | tf_op jit(solution)/shard_map/all_to_all | solution.py:268
  152.5 7.2 %all-to-all-done.7 = f32[32,4,128]{2,1,0:T(4,128)S(1)} async-done(((f32[32,4,128]{2,1,0:T(4,128)}), f32[32,4,128]{2,1,0:T(4,128)S(1)}, u32[]{:S(2)}, u32[]{:S(2)}) %all-to-all-start.7) | async-done | bytes 65568 | tf_op jit(solution)/shard_map/all_to_all | solution.py:268
  159.8 18.4 %all_to_all.54 = f32[16,20,128]{2,1,0:T(8,128)S(1)} all-to-all(f32[16,20,128]{2,1,0:T(8,128)S(1)} %broadcast_in_dim.27), channel_id=1, replica_groups=mesh['z'=16,'x'=4,'y'=4,'core'=2] {'z'}, dimensions={0} | all-to-all | bytes 327680 | tf_op jit(solution)/shard_map/all_to_all | solution.py:268
  178.2 14.5 %all_to_all.55 = f32[32,4,128]{2,1,0:T(4,128)S(1)} all-to-all(f32[32,4,128]{2,1,0:T(4,128)S(1)} %broadcast_in_dim.28), channel_id=1, replica_groups=mesh['z'=16,'x'=4,'y'=4,'core'=2] {'x','y','core'}, dimensions={0} | all-to-all | bytes 131072 | tf_op jit(solution)/shard_map/all_to_all | solution.py:268
  192.8 4.9 %shard_map.47 = (f32[100,512]{1,0:T(8,128)}, f32[100,256]{1,0:T(8,128)}) custom-call(f32[128,128]{1,0:T(8,128)S(1)} %bitcast.21, f32[256,128]{1,0:T(8,128)S(1)} %bitcast.18, f32[128,128]{1,0:T(8,128)S(1)} %get-tuple-element.34.y_ref, f32[128,512]{1,0:T(8,128)S(1)} %get-tuple-element.24.loadings_ref, f32[256,128]{1,0:T(8,128)S(1)} %bitcast.19), custom_call_target="tpu_custom_call" | custom-call | flops 5000000000 | tf_op jit(solution)/shard_map/pallas_call | solution.py:212
  (17 shorter events, 0.4 us)
Async XLA Ops:
  0.6 0.9 copy-start
  3.8 10.8 %collective-permute-start = (f32[4,104,512]{2,1,0:T(8,128)S(1)}, f32[4,104,512]{2,1,0:T(8,128)S(1)}, u32[]{:S(2)}, u32[]{:S(2)}) collective-permute-start(f32[4,104,512]{2,1,0:T(8,128)S(1)} %get-tuple-element.19), channel_id=1, source_target_pairs={{0,1},{1,0},{2,3},{3,2},{4,5},{5,4},{6,7},{7,6},{8,9},{9,8},{10,11... | collective-permute-start | bytes 2555912 | tf_op jit(solution)/shard_map/ppermute | solution.py:286
  42.6 24.9 %all-to-all-start.2 = ((f32[16,8,128]{2,1,0:T(8,128)}), f32[16,8,128]{2,1,0:T(8,128)S(1)}, u32[]{:S(2)}, u32[]{:S(2)}) async-start(f32[16,8,128]{2,1,0:T(8,128)} %broadcast_in_dim.23), calls=%async_computation.2 | async-start | bytes 131072 | tf_op jit(solution)/shard_map/all_to_all | solution.py:268
  55.8 8.0 %collective-permute-start.1 = (f32[104,512]{1,0:T(8,128)S(1)}, f32[104,512]{1,0:T(8,128)S(1)}, u32[]{:S(2)}, u32[]{:S(2)}) collective-permute-start(f32[104,512]{1,0:T(8,128)S(1)} %get-tuple-element.22), channel_id=1, source_target_pairs={{0,2},{2,0},{4,6},{6,4},{1,3},{3,1},{5,7},{7,5},{8,10},{10,8},{12,... | collective-permute-start | bytes 638984 | tf_op jit(solution)/shard_map/ppermute | solution.py:291
  68.1 13.4 %all-to-all-start.3 = ((f32[32,8,128]{2,1,0:T(8,128)}), f32[32,8,128]{2,1,0:T(8,128)S(1)}, u32[]{:S(2)}, u32[]{:S(2)}) async-start(f32[32,8,128]{2,1,0:T(8,128)} %broadcast_in_dim.24), calls=%async_computation.3 | async-start | bytes 262144 | tf_op jit(solution)/shard_map/all_to_all | solution.py:268
  73.8 15.6 %collective-permute-start.2 = (f32[2,104,512]{2,1,0:T(8,128)S(1)}, f32[2,104,512]{2,1,0:T(8,128)S(1)}, u32[]{:S(2)}, u32[]{:S(2)}) collective-permute-start(f32[2,104,512]{2,1,0:T(8,128)S(1)} %pad_maximum_fusion.1), channel_id=1, source_target_pairs={{0,4},{2,6},{4,0},{6,2},{1,5},{3,7},{5,1},{7,3},{8,12},{10,14},{12... | collective-permute-start | bytes 1277960 | tf_op jit(solution)/shard_map/ppermute | solution.py:295
  89.5 9.3 %collective-permute-start.3 = (f32[4,104,512]{2,1,0:T(8,128)S(1)}, f32[4,104,512]{2,1,0:T(8,128)S(1)}, u32[]{:S(2)}, u32[]{:S(2)}) collective-permute-start(f32[4,104,512]{2,1,0:T(8,128)S(1)} %pad_maximum_fusion.near_ref), channel_id=1, source_target_pairs={{0,1},{1,0},{2,3},{3,2},{4,5},{5,4},{6,7},{7,6},{8,9},{9,8},{10,11... | collective-permute-start | bytes 2555912 | tf_op jit(solution)/shard_map/ppermute | solution.py:303
  92.3 13.8 %all-to-all-start.4 = ((f32[32,4,128]{2,1,0:T(4,128)}), f32[32,4,128]{2,1,0:T(4,128)S(1)}, u32[]{:S(2)}, u32[]{:S(2)}) async-start(f32[32,4,128]{2,1,0:T(4,128)} %bitcast.5), calls=%async_computation.4 | async-start | bytes 131072 | tf_op jit(solution)/shard_map/all_to_all | solution.py:268
  148.8 10.9 %all-to-all-start.7 = ((f32[32,4,128]{2,1,0:T(4,128)}), f32[32,4,128]{2,1,0:T(4,128)S(1)}, u32[]{:S(2)}, u32[]{:S(2)}) async-start(f32[32,4,128]{2,1,0:T(4,128)} %bitcast.9), calls=%async_computation.7 | async-start | bytes 131072 | tf_op jit(solution)/shard_map/all_to_all | solution.py:268

commit v7 on v4

--- a/solution.py
+++ b/solution.py
@@ -61,12 +61,9 @@
     y = grad / (norm + 1e-06)
     for step in range(NS_STEPS):
         high, low = split(y)
-        down = jnp.concatenate([high, low], axis=0)
-        across = jnp.concatenate([high, low], axis=1)
-        inner = fold(nt(across, jnp.concatenate([down, down], axis=1)))
+        inner = fold(nt(high, jnp.concatenate([high, low], axis=0))) + nt(low, high)
         ih, il = split(inner)
-        again = jnp.concatenate([across, across], axis=0)
-        y = 1.5 * y - 0.5 * fold(nn(jnp.concatenate([ih, il], axis=1), again))
+        y = 1.5 * y - 0.5 * (fold(nn(ih, jnp.concatenate([high, low], axis=1))) + nn(il, high))
     return y
 
 
@@ -178,7 +175,11 @@
     k = rotated_ref.shape[0]
     y = next_y(cells, cube_ref, got_ref, y_ref)
     rotated_ref[...] = small_nn(y, loadings_ref[...])[0:k]
-    series_ref[...] = rows_nt(y, terms_ref[...])[0:k]
+    parts = series_ref.shape[1] // PAD
+    rows = terms_ref.shape[0] // parts
+    for part in range(parts):
+        terms = pad_rows(terms_ref[part * rows : (part + 1) * rows], PAD)
+        series_ref[:, part * PAD : (part + 1) * PAD] = small_nn(y, terms)[0:k]
 
 
 def whole(kernel, outs, *args):
@@ -193,15 +194,18 @@
 
 def terms_kernel(scale, where_ref, field_ref, near_ref, far_ref, out_ref):
     row, core = where_ref[0], where_ref[1]
-    share = near_ref.shape[2]
-    total = jnp.zeros(out_ref.shape, F32)
+    rows, share = near_ref.shape[1:]
+    days = field_ref.shape[0]
+    total = jnp.zeros((PAD, days), F32)
     for d in range(Y):
         group = CORE * lax.rem(row + Y - d, Y)
         for owner, loadings in ((core, near_ref[d]), (1 - core, far_ref[d])):
             lh, ll = split(pad_rows(loadings, PAD))
             high, low = split(columns(field_ref, group + owner, share))
-            total += fold(nt(high, jnp.concatenate([lh, ll], axis=0))) + nt(low, lh)
-    out_ref[...] = total * scale
+            both = nt(jnp.concatenate([lh, ll], axis=0), high)
+            total += both[0:PAD] + both[PAD : 2 * PAD] + nt(lh, low)
+    for part in range(days // PAD):
+        out_ref[part * rows : (part + 1) * rows] = total[0:rows, part * PAD : (part + 1) * PAD] * scale
 
 
 def series_terms(field, near, far, where, scale):
@@ -209,7 +213,7 @@
     rows, share = near.shape[1:]
     return pl.pallas_call(
         functools.partial(terms_kernel, scale),
-        out_shape=jax.ShapeDtypeStruct((days, PAD), F32),
+        out_shape=jax.ShapeDtypeStruct((days // PAD * rows, PAD), F32),
         in_specs=[pl.BlockSpec(memory_space=pltpu.SMEM), VMEM, VMEM, VMEM],
         out_specs=VMEM,
         cost_estimate=pl.CostEstimate(
@@ -251,27 +255,28 @@
     near = jnp.stack([narrow] + near)
     far = lax.ppermute(near, "core", [(0, 1), (1, 0)])
     base = base.reshape(2 * PAD, PAD)
-    piece = days_here // Z
     sent, y = whole(functools.partial(second_kernel, cells_total), [(PAD, PAD)] * 2, base, loadings)
 
     sent, near, far = lax.optimization_barrier((sent, near, far))
     terms = series_terms(field, near, far, jnp.stack([row, core]), days_total**0.5 / cells_total)
     chunk, terms = lax.optimization_barrier((swap(sent.reshape(N_PLANE, ROWS, PAD), PLANE), terms))
     chunk = jnp.sum(chunk, axis=0)
-    both = jnp.concatenate([spread(chunk, Z), terms.reshape(Z, piece, PAD)], axis=1)
+    width = ROWS * PAD
+    both = jnp.concatenate([spread(chunk.reshape(1, width), Z), terms.reshape(Z, 1, -1)], axis=2)
     both = jnp.sum(swap(both, "z"), axis=0)
     got = swap(spread(both, N_PLANE), PLANE)
-    cube = got[:, :ROWS].reshape(PAD, PAD)
-    terms = got[:, ROWS:].reshape(X, groups, piece, PAD)
+    cube = got[:, :, :width].reshape(PAD, PAD)
+    terms = got[:, :, width:].reshape(X, groups, 1, -1)
     terms = jnp.sum(lax.dynamic_index_in_dim(terms, row * CORE + core, 1, keepdims=False), axis=0)
     sent, y = whole(
         functools.partial(third_kernel, cells_total), [(PAD, PAD)] * 2, cube, base, y, loadings
     )
 
     chunk = jnp.sum(swap(sent.reshape(N_PLANE, ROWS, PAD), PLANE), axis=0)
-    got = swap(spread(jnp.concatenate([chunk, terms], axis=0), Z), "z")
-    terms = got[:, ROWS:].reshape(days_here, PAD)
-    chunk, terms = lax.optimization_barrier((jnp.sum(got[:, :ROWS], axis=0), terms))
+    got = swap(spread(jnp.concatenate([chunk.reshape(1, width), terms], axis=1), Z), "z")
+    terms = got[:, :, width:].reshape(-1, PAD)
+    chunk = jnp.sum(got[:, :, :width], axis=0).reshape(ROWS, PAD)
+    chunk, terms = lax.optimization_barrier((chunk, terms))
     cube = swap(spread(chunk, N_PLANE), PLANE).reshape(PAD, PAD)
     return whole(
         functools.partial(last_kernel, cells_total),

time: 195 us -> 190 us (0.974)
  blocking collectives: 98.7 us -> 94.1 us
    all_to_all x6, blocking collectives: 98.7 us -> 94.1 us  [swap(): return lax.all_to_all(value, axes, 0, 0)]
where the time goes in v7:
time: 190 us; the launch traced here: 189 us
  blocking collectives  94.1 us (50%)
  starting transfers between devices  45.8 us (24%)
  waiting for transfers between devices  21.5 us (11%)
  Pallas kernels  21.4 us (11%)
  local copies, waits for them, and re-layouts  4.68 us (2%)
    all_to_all x6, blocking collectives, swap(): return lax.all_to_all(value, axes, 0, 0)  94.1 us
    all_to_all x4, starting transfers between devices, swap(): return lax.all_to_all(value, axes, 0, 0)  26.2 us
    all_to_all x4, waiting for transfers between devices, swap(): return lax.all_to_all(value, axes, 0, 0)  21.5 us
    pallas_call x3, Pallas kernels, whole(): pl.pallas_call(kernel, out_shape=tuple((jax.ShapeDtypeStruct(s, F32) for...  14.6 us
    ppermute x1, starting transfers between devices, on_device(): lax.ppermute(parts(field, pcs, (1 - core)[None], scale), 'core', [(0, 1),...  8.79 us
    ppermute x3, starting transfers between devices, on_device(): lax.ppermute(narrow, 'y', [(i, (i + d) % Y) for i in range(Y)])  8.49 us
    pallas_call x2, Pallas kernels, parts(): pl.pallas_call(functools.partial(parts_kernel, scale), out_shape=jax.Shap...  4.5 us
  transfers between devices with their start and end apart: 9, of which 4 were waited for; matrix products, arithmetic and copies ran while one was open for 0% of the time, Pallas kernels for 5%

profile of v7, /device:TPU:1, one launch (start us, length us, event | category | flops | bytes accessed | tf_op | source)
XLA Modules:
  0.0 189.1 jit_solution(7575831087248102091)
XLA Ops:
  0.6 0.0 copy-start.1
  0.6 0.9 copy-done.1
  1.5 0.0 copy-start.2
  1.5 2.2 %shard_map.41 = f32[4,104,512]{2,1,0:T(8,128)S(1)} custom-call(s32[1]{0:T(128)} %bitcast.core_ref, f32[100,256]{1,0:T(8,128)S(1)} %copy-done.1, f32[256,4096]{1,0:T(8,128)} %field_ref.5), custom_call_target="tpu_custom_call" | custom-call | flops 314572800 | bytes 2916352 | tf_op jit(solution)/shard_map/pallas_call | solution.py:107
  3.8 8.8 %collective-permute-start = (f32[4,104,512]{2,1,0:T(8,128)S(1)}, f32[4,104,512]{2,1,0:T(8,128)S(1)}, u32[]{:S(2)}, u32[]{:S(2)}) collective-permute-start(f32[4,104,512]{2,1,0:T(8,128)S(1)} %shard_map.41), channel_id=1, source_target_pairs={{0,1},{1,0},{2,3},{3,2},{4,5},{5,4},{6,7},{7,6},{8,9},{9,8},{10,11... | collective-permute-start | bytes 2555912 | tf_op jit(solution)/shard_map/ppermute | solution.py:246
  12.6 0.0 copy-done.2
  12.6 2.3 %shard_map.42 = f32[4,104,512]{2,1,0:T(8,128)S(1)} custom-call(s32[1]{0:T(128)} %bitcast.1.core_ref, f32[100,256]{1,0:T(8,128)S(1)} %copy-done.2, f32[256,4096]{1,0:T(8,128)} %field_ref.5), custom_call_target="tpu_custom_call" | custom-call | flops 314572800 | bytes 2916352 | tf_op jit(solution)/shard_map/pallas_call | solution.py:107
  14.9 0.0 collective-permute-done
  14.9 0.2 add.10
  15.0 15.5 %all_to_all.50.recv_ref = f32[4,104,512]{2,1,0:T(8,128)S(1)} all-to-all(f32[4,104,512]{2,1,0:T(8,128)S(1)} %add.10), channel_id=1, replica_groups=mesh['z'=16,'x'=4,'y'=4,'core'=2] {'y'}, dimensions={0} | all-to-all | bytes 1703936 | tf_op jit(solution)/shard_map/all_to_all | solution.py:229
  30.5 0.4 shard_map.43
  30.9 11.3 %all_to_all.51 = f32[32,8,128]{2,1,0:T(8,128)S(1)} all-to-all(f32[32,8,128]{2,1,0:T(8,128)S(1)} %bitcast.27), channel_id=1, replica_groups=mesh['z'=16,'x'=4,'y'=4,'core'=2] {'x','y','core'}, dimensions={0} | all-to-all | bytes 262144 | tf_op jit(solution)/shard_map/all_to_all | solution.py:229
  42.3 0.6 broadcast_in_dim.26
  42.9 13.2 %all-to-all-start.2 = ((f32[16,8,128]{2,1,0:T(8,128)}), f32[16,8,128]{2,1,0:T(8,128)S(1)}, u32[]{:S(2)}, u32[]{:S(2)}) async-start(f32[16,8,128]{2,1,0:T(8,128)} %broadcast_in_dim.26), calls=%async_computation.2 | async-start | bytes 131072 | tf_op jit(solution)/shard_map/all_to_all | solution.py:229
  56.2 2.2 %collective-permute-start.1 = (f32[104,512]{1,0:T(8,128)S(1)}, f32[104,512]{1,0:T(8,128)S(1)}, u32[]{:S(2)}, u32[]{:S(2)}) collective-permute-start(f32[104,512]{1,0:T(8,128)S(1)} %get-tuple-element.21), channel_id=1, source_target_pairs={{0,2},{2,4},{4,6},{6,0},{1,3},{3,5},{5,7},{7,1},{8,10},{10,12},{12... | collective-permute-start | bytes 638984 | tf_op jit(solution)/shard_map/ppermute | solution.py:251
  58.3 3.8 %collective-permute-start.2 = (f32[104,512]{1,0:T(8,128)S(1)}, f32[104,512]{1,0:T(8,128)S(1)}, u32[]{:S(2)}, u32[]{:S(2)}) collective-permute-start(f32[104,512]{1,0:T(8,128)S(1)} %get-tuple-element.21), channel_id=1, source_target_pairs={{0,4},{2,6},{4,0},{6,2},{1,5},{3,7},{5,1},{7,3},{8,12},{10,14},{12... | collective-permute-start | bytes 638984 | tf_op jit(solution)/shard_map/ppermute | solution.py:251
  62.1 2.6 %collective-permute-start.3 = (f32[104,512]{1,0:T(8,128)S(1)}, f32[104,512]{1,0:T(8,128)S(1)}, u32[]{:S(2)}, u32[]{:S(2)}) collective-permute-start(f32[104,512]{1,0:T(8,128)S(1)} %get-tuple-element.21), channel_id=1, source_target_pairs={{0,6},{2,0},{4,2},{6,4},{1,7},{3,1},{5,3},{7,5},{8,14},{10,8},{12,... | collective-permute-start | bytes 638984 | tf_op jit(solution)/shard_map/ppermute | solution.py:251
  64.7 3.1 %all-to-all-done.2 = f32[16,8,128]{2,1,0:T(8,128)S(1)} async-done(((f32[16,8,128]{2,1,0:T(8,128)}), f32[16,8,128]{2,1,0:T(8,128)S(1)}, u32[]{:S(2)}, u32[]{:S(2)}) %all-to-all-start.2) | async-done | bytes 65568 | tf_op jit(solution)/shard_map/all_to_all | solution.py:229
  67.8 0.7 broadcast_in_dim.27
  68.4 5.6 %all-to-all-start.3 = ((f32[32,8,128]{2,1,0:T(8,128)}), f32[32,8,128]{2,1,0:T(8,128)S(1)}, u32[]{:S(2)}, u32[]{:S(2)}) async-start(f32[32,8,128]{2,1,0:T(8,128)} %broadcast_in_dim.27), calls=%async_computation.3 | async-start | bytes 262144 | tf_op jit(solution)/shard_map/all_to_all | solution.py:229
  74.1 0.0 collective-permute-done.1
  74.1 0.0 collective-permute-done.2
  74.1 0.0 collective-permute-done.3
  74.1 7.8 %all-to-all-done.3 = f32[32,8,128]{2,1,0:T(8,128)S(1)} async-done(((f32[32,8,128]{2,1,0:T(8,128)}), f32[32,8,128]{2,1,0:T(8,128)S(1)}, u32[]{:S(2)}, u32[]{:S(2)}) %all-to-all-start.3) | async-done | bytes 131104 | tf_op jit(solution)/shard_map/all_to_all | solution.py:229
  81.9 0.1 pad_maximum_fusion.near_ref
  81.9 2.3 %collective-permute-start.4 = (f32[4,104,512]{2,1,0:T(8,128)S(1)}, f32[4,104,512]{2,1,0:T(8,128)S(1)}, u32[]{:S(2)}, u32[]{:S(2)}) collective-permute-start(f32[4,104,512]{2,1,0:T(8,128)S(1)} %pad_maximum_fusion.near_ref), channel_id=1, source_target_pairs={{0,1},{1,0},{2,3},{3,2},{4,5},{5,4},{6,7},{7,6},{8,9},{9,8},{10,11... | collective-permute-start | bytes 2555912 | tf_op jit(solution)/shard_map/ppermute | solution.py:256
  84.3 0.1 pad_add_fusion.where_ref
  84.3 4.8 %shard_map.44 = (f32[128,128]{1,0:T(8,128)}, f32[128,128]{1,0:T(8,128)S(1)}) custom-call(f32[256,128]{1,0:T(8,128)S(1)} %bitcast.19, f32[128,512]{1,0:T(8,128)S(1)} %get-tuple-element.23.loadings_ref), custom_call_target="tpu_custom_call" | custom-call | tf_op jit(solution)/shard_map/pallas_call | solution.py:186
  89.1 0.0 collective-permute-done.4.far_ref
  89.2 3.6 %all-to-all-start.4 = ((f32[32,4,128]{2,1,0:T(4,128)}), f32[32,4,128]{2,1,0:T(4,128)S(1)}, u32[]{:S(2)}, u32[]{:S(2)}) async-start(f32[32,4,128]{2,1,0:T(4,128)} %bitcast.8), calls=%async_computation.4 | async-start | bytes 131072 | tf_op jit(solution)/shard_map/all_to_all | solution.py:229
  92.8 0.0 copy-start
  92.8 2.2 %copy-done = f32[256,4096]{1,0:T(8,128)S(1)} copy-done((f32[256,4096]{1,0:T(8,128)S(1)}, f32[256,4096]{1,0:T(8,128)}, u32[]{:S(2)}) %copy-start) | copy-done | bytes 4194328
  95.0 2.0 %shard_map.45 = f32[208,128]{1,0:T(8,128)S(1)} custom-call(s32[2]{0:T(128)S(1)} %pad_add_fusion.where_ref, f32[256,4096]{1,0:T(8,128)S(1)} %copy-done, f32[4,104,512]{2,1,0:T(8,128)S(1)} %pad_maximum_fusion.near_ref, f32[4,104,512]{2,1,0:T(8,128)S(1)} %collective-permute-done.4.far_ref), custom_call_target="tpu_custom_call" | custom-call | flops 805306368 | bytes 5898240 | tf_op jit(solution)/shard_map/pallas_call | solution.py:214
  97.0 3.3 %all-to-all-done.4 = f32[32,4,128]{2,1,0:T(4,128)S(1)} async-done(((f32[32,4,128]{2,1,0:T(4,128)}), f32[32,4,128]{2,1,0:T(4,128)S(1)}, u32[]{:S(2)}, u32[]{:S(2)}) %all-to-all-start.4) | async-done | bytes 65568 | tf_op jit(solution)/shard_map/all_to_all | solution.py:229
  100.3 0.1 pad_maximum_fusion.1
  100.4 21.1 %all_to_all.52 = f32[16,1,2176]{2,1,0:T(1,128)S(1)} all-to-all(f32[16,1,2176]{2,1,0:T(1,128)S(1)} %pad_maximum_fusion.1), channel_id=1, replica_groups=mesh['z'=16,'x'=4,'y'=4,'core'=2] {'z'}, dimensions={0} | all-to-all | bytes 278528 | tf_op jit(solution)/shard_map/all_to_all | solution.py:229
  121.5 0.1 reduce_sum.68
  121.6 0.1 broadcast_in_dim.29
  121.8 16.4 %all_to_all.53 = f32[32,1,2176]{2,1,0:T(1,128)S(1)} all-to-all(f32[32,1,2176]{2,1,0:T(1,128)S(1)} %broadcast_in_dim.29), channel_id=1, replica_groups=mesh['z'=16,'x'=4,'y'=4,'core'=2] {'x','y','core'}, dimensions={0} | all-to-all | bytes 557056 | tf_op jit(solution)/shard_map/all_to_all | solution.py:229
  138.2 4.9 %shard_map.46 = (f32[128,128]{1,0:T(8,128)}, f32[128,128]{1,0:T(8,128)S(1)}) custom-call(f32[128,128]{1,0:T(8,128)S(1)} %bitcast.25, f32[256,128]{1,0:T(8,128)S(1)} %bitcast.20, f32[128,128]{1,0:T(8,128)S(1)} %get-tuple-element.33.y_ref, f32[128,512]{1,0:T(8,128)S(1)} %get-tuple-element.23.loadings_ref), custom_call_target="tpu_custom_call" | custom-call | tf_op jit(solution)/shard_map/pallas_call | solution.py:186
  143.2 3.7 %all-to-all-start.7 = ((f32[32,4,128]{2,1,0:T(4,128)}), f32[32,4,128]{2,1,0:T(4,128)S(1)}, u32[]{:S(2)}, u32[]{:S(2)}) async-start(f32[32,4,128]{2,1,0:T(4,128)} %bitcast.13), calls=%async_computation.7 | async-start | bytes 131072 | tf_op jit(solution)/shard_map/all_to_all | solution.py:229
  147.0 7.4 %all-to-all-done.7 = f32[32,4,128]{2,1,0:T(4,128)S(1)} async-done(((f32[32,4,128]{2,1,0:T(4,128)}), f32[32,4,128]{2,1,0:T(4,128)S(1)}, u32[]{:S(2)}, u32[]{:S(2)}) %all-to-all-start.7) | async-done | bytes 65568 | tf_op jit(solution)/shard_map/all_to_all | solution.py:229
  154.4 0.1 broadcast_in_dim.30
  154.5 15.7 %all_to_all.54 = f32[16,1,2176]{2,1,0:T(1,128)S(1)} all-to-all(f32[16,1,2176]{2,1,0:T(1,128)S(1)} %broadcast_in_dim.30), channel_id=1, replica_groups=mesh['z'=16,'x'=4,'y'=4,'core'=2] {'z'}, dimensions={0} | all-to-all | bytes 278528 | tf_op jit(solution)/shard_map/all_to_all | solution.py:229
  170.3 14.0 %all_to_all.55 = f32[32,4,128]{2,1,0:T(4,128)S(1)} all-to-all(f32[32,4,128]{2,1,0:T(4,128)S(1)} %broadcast_in_dim.31), channel_id=1, replica_groups=mesh['z'=16,'x'=4,'y'=4,'core'=2] {'x','y','core'}, dimensions={0} | all-to-all | bytes 131072 | tf_op jit(solution)/shard_map/all_to_all | solution.py:229
  184.3 4.8 %shard_map.47 = (f32[100,512]{1,0:T(8,128)}, f32[100,256]{1,0:T(8,128)}) custom-call(f32[128,128]{1,0:T(8,128)S(1)} %bitcast.24, f32[256,128]{1,0:T(8,128)S(1)} %bitcast.21, f32[128,128]{1,0:T(8,128)S(1)} %get-tuple-element.36.y_ref, f32[128,512]{1,0:T(8,128)S(1)} %get-tuple-element.23.loadings_ref, f32[208,128]{1,0:T(8,128)S(1)} %bitcast.22), custom_call_target="tpu_custom_call" | custom-call | tf_op jit(solution)/shard_map/pallas_call | solution.py:186
  (13 shorter events, 0.3 us)
Async XLA Ops:
  0.6 0.9 copy-start.1
  1.5 11.0 %copy-start.2 = (f32[100,256]{1,0:T(8,128)S(1)}, f32[100,256]{1,0:T(8,128)}, u32[]{:S(2)}) copy-start(f32[100,256]{1,0:T(8,128)} %pcs_ref.3) | copy-start | bytes 307204
  3.8 11.1 %collective-permute-start = (f32[4,104,512]{2,1,0:T(8,128)S(1)}, f32[4,104,512]{2,1,0:T(8,128)S(1)}, u32[]{:S(2)}, u32[]{:S(2)}) collective-permute-start(f32[4,104,512]{2,1,0:T(8,128)S(1)} %shard_map.41), channel_id=1, source_target_pairs={{0,1},{1,0},{2,3},{3,2},{4,5},{5,4},{6,7},{7,6},{8,9},{9,8},{10,11... | collective-permute-start | bytes 2555912 | tf_op jit(solution)/shard_map/ppermute | solution.py:246
  42.9 24.9 %all-to-all-start.2 = ((f32[16,8,128]{2,1,0:T(8,128)}), f32[16,8,128]{2,1,0:T(8,128)S(1)}, u32[]{:S(2)}, u32[]{:S(2)}) async-start(f32[16,8,128]{2,1,0:T(8,128)} %broadcast_in_dim.26), calls=%async_computation.2 | async-start | bytes 131072 | tf_op jit(solution)/shard_map/all_to_all | solution.py:229
  56.2 17.9 %collective-permute-start.1 = (f32[104,512]{1,0:T(8,128)S(1)}, f32[104,512]{1,0:T(8,128)S(1)}, u32[]{:S(2)}, u32[]{:S(2)}) collective-permute-start(f32[104,512]{1,0:T(8,128)S(1)} %get-tuple-element.21), channel_id=1, source_target_pairs={{0,2},{2,4},{4,6},{6,0},{1,3},{3,5},{5,7},{7,1},{8,10},{10,12},{12... | collective-permute-start | bytes 638984 | tf_op jit(solution)/shard_map/ppermute | solution.py:251
  58.3 15.8 %collective-permute-start.2 = (f32[104,512]{1,0:T(8,128)S(1)}, f32[104,512]{1,0:T(8,128)S(1)}, u32[]{:S(2)}, u32[]{:S(2)}) collective-permute-start(f32[104,512]{1,0:T(8,128)S(1)} %get-tuple-element.21), channel_id=1, source_target_pairs={{0,4},{2,6},{4,0},{6,2},{1,5},{3,7},{5,1},{7,3},{8,12},{10,14},{12... | collective-permute-start | bytes 638984 | tf_op jit(solution)/shard_map/ppermute | solution.py:251
  62.1 12.0 %collective-permute-start.3 = (f32[104,512]{1,0:T(8,128)S(1)}, f32[104,512]{1,0:T(8,128)S(1)}, u32[]{:S(2)}, u32[]{:S(2)}) collective-permute-start(f32[104,512]{1,0:T(8,128)S(1)} %get-tuple-element.21), channel_id=1, source_target_pairs={{0,6},{2,0},{4,2},{6,4},{1,7},{3,1},{5,3},{7,5},{8,14},{10,8},{12,... | collective-permute-start | bytes 638984 | tf_op jit(solution)/shard_map/ppermute | solution.py:251
  68.4 13.4 %all-to-all-start.3 = ((f32[32,8,128]{2,1,0:T(8,128)}), f32[32,8,128]{2,1,0:T(8,128)S(1)}, u32[]{:S(2)}, u32[]{:S(2)}) async-start(f32[32,8,128]{2,1,0:T(8,128)} %broadcast_in_dim.27), calls=%async_computation.3 | async-start | bytes 262144 | tf_op jit(solution)/shard_map/all_to_all | solution.py:229
  81.9 7.2 %collective-permute-start.4 = (f32[4,104,512]{2,1,0:T(8,128)S(1)}, f32[4,104,512]{2,1,0:T(8,128)S(1)}, u32[]{:S(2)}, u32[]{:S(2)}) collective-permute-start(f32[4,104,512]{2,1,0:T(8,128)S(1)} %pad_maximum_fusion.near_ref), channel_id=1, source_target_pairs={{0,1},{1,0},{2,3},{3,2},{4,5},{5,4},{6,7},{7,6},{8,9},{9,8},{10,11... | collective-permute-start | bytes 2555912 | tf_op jit(solution)/shard_map/ppermute | solution.py:256
  89.2 11.1 %all-to-all-start.4 = ((f32[32,4,128]{2,1,0:T(4,128)}), f32[32,4,128]{2,1,0:T(4,128)S(1)}, u32[]{:S(2)}, u32[]{:S(2)}) async-start(f32[32,4,128]{2,1,0:T(4,128)} %bitcast.8), calls=%async_computation.4 | async-start | bytes 131072 | tf_op jit(solution)/shard_map/all_to_all | solution.py:229
  92.8 2.2 %copy-start = (f32[256,4096]{1,0:T(8,128)S(1)}, f32[256,4096]{1,0:T(8,128)}, u32[]{:S(2)}) copy-start(f32[256,4096]{1,0:T(8,128)} %field_ref.5) | copy-start | bytes 12582916
  143.2 11.2 %all-to-all-start.7 = ((f32[32,4,128]{2,1,0:T(4,128)}), f32[32,4,128]{2,1,0:T(4,128)S(1)}, u32[]{:S(2)}, u32[]{:S(2)}) async-start(f32[32,4,128]{2,1,0:T(4,128)} %bitcast.13), calls=%async_computation.7 | async-start | bytes 131072 | tf_op jit(solution)/shard_map/all_to_all | solution.py:229

commit v8 on v7

--- a/solution.py
+++ b/solution.py
@@ -18,6 +18,7 @@
 F32 = jnp.float32
 VMEM = pl.BlockSpec(memory_space=pltpu.VMEM)
 LIMIT = 24 << 20
+FLOPS = 5000000000
 WIDE_LIMIT = 52 << 20
 
 
@@ -188,6 +189,7 @@
         out_shape=tuple(jax.ShapeDtypeStruct(s, F32) for s in outs),
         in_specs=[VMEM] * len(args),
         out_specs=(VMEM,) * len(outs),
+        cost_estimate=pl.CostEstimate(flops=FLOPS, bytes_accessed=0, transcendentals=0),
         compiler_params=pltpu.CompilerParams(vmem_limit_bytes=LIMIT),
     )(*args)
 
@@ -248,16 +250,19 @@
     sent, narrow, loadings = first(recv)
 
     chunk = swap(sent.reshape(N_PLANE, 2 * ROWS, PAD), PLANE)
-    near = [lax.ppermute(narrow, "y", [(i, (i + d) % Y) for i in range(Y)]) for d in range(1, Y)]
+    up = [(i, (i + 1) % Y) for i in range(Y)]
+    first_up = lax.ppermute(narrow, "y", up)
+    down = lax.ppermute(narrow, "y", [(j, i) for i, j in up])
+    second_up = lax.ppermute(first_up, "y", up)
     chunk = swap(spread(jnp.sum(chunk, axis=0), Z), "z")
     base = swap(spread(jnp.sum(chunk, axis=0), N_PLANE), PLANE)
-    base, near = lax.optimization_barrier((base, near))
-    near = jnp.stack([narrow] + near)
-    far = lax.ppermute(near, "core", [(0, 1), (1, 0)])
+    base, down = lax.optimization_barrier((base, down))
     base = base.reshape(2 * PAD, PAD)
     sent, y = whole(functools.partial(second_kernel, cells_total), [(PAD, PAD)] * 2, base, loadings)
 
-    sent, near, far = lax.optimization_barrier((sent, near, far))
+    sent, second_up = lax.optimization_barrier((sent, second_up))
+    near = jnp.stack([narrow, first_up, second_up, down])
+    far = lax.ppermute(near, "core", [(0, 1), (1, 0)])
     terms = series_terms(field, near, far, jnp.stack([row, core]), days_total**0.5 / cells_total)
     chunk, terms = lax.optimization_barrier((swap(sent.reshape(N_PLANE, ROWS, PAD), PLANE), terms))
     chunk = jnp.sum(chunk, axis=0)

time: 190 us -> 187 us (0.984)
  blocking collectives: 94.1 us -> 90.7 us
    all_to_all x6, blocking collectives: 94.1 us -> 90.7 us  [swap(): return lax.all_to_all(value, axes, 0, 0)]
where the time goes in v8:
time: 187 us; the launch traced here: 186 us
  blocking collectives  90.7 us (49%)
  starting transfers between devices  47.2 us (25%)
  Pallas kernels  21.4 us (11%)
  waiting for transfers between devices  20.1 us (11%)
  local copies, waits for them, and re-layouts  4.68 us (3%)
    all_to_all x6, blocking collectives, swap(): return lax.all_to_all(value, axes, 0, 0)  90.7 us
    all_to_all x4, starting transfers between devices, swap(): return lax.all_to_all(value, axes, 0, 0)  26.3 us
    all_to_all x4, waiting for transfers between devices, swap(): return lax.all_to_all(value, axes, 0, 0)  20.1 us
    pallas_call x3, Pallas kernels, whole(): pl.pallas_call(kernel, out_shape=tuple((jax.ShapeDtypeStruct(s, F32) for...  14.6 us
    ppermute x1, starting transfers between devices, on_device(): lax.ppermute(parts(field, pcs, (1 - core)[None], scale), 'core', [(0, 1),...  8.79 us
    pallas_call x2, Pallas kernels, parts(): pl.pallas_call(functools.partial(parts_kernel, scale), out_shape=jax.Shap...  4.5 us
    ppermute x1, starting transfers between devices, on_device(): down = lax.ppermute(narrow, 'y', [(j, i) for i, j in up])  4.33 us
  transfers between devices with their start and end apart: 9, of which 4 were waited for; matrix products, arithmetic and copies ran while one was open for 0% of the time, Pallas kernels for 5%

profile of v8, /device:TPU:1, one launch (start us, length us, event | category | flops | bytes accessed | tf_op | source)
XLA Modules:
  0.0 185.9 jit_solution(14809752601646623242)
XLA Ops:
  0.6 0.0 copy-start.1
  0.6 0.9 copy-done.1
  1.5 0.0 copy-start.2
  1.5 2.2 %shard_map.41 = f32[4,104,512]{2,1,0:T(8,128)S(1)} custom-call(s32[1]{0:T(128)} %bitcast.core_ref, f32[100,256]{1,0:T(8,128)S(1)} %copy-done.1, f32[256,4096]{1,0:T(8,128)} %field_ref.5), custom_call_target="tpu_custom_call" | custom-call | flops 314572800 | bytes 2916352 | tf_op jit(solution)/shard_map/pallas_call | solution.py:108
  3.8 8.8 %collective-permute-start = (f32[4,104,512]{2,1,0:T(8,128)S(1)}, f32[4,104,512]{2,1,0:T(8,128)S(1)}, u32[]{:S(2)}, u32[]{:S(2)}) collective-permute-start(f32[4,104,512]{2,1,0:T(8,128)S(1)} %shard_map.41), channel_id=1, source_target_pairs={{0,1},{1,0},{2,3},{3,2},{4,5},{5,4},{6,7},{7,6},{8,9},{9,8},{10,11... | collective-permute-start | bytes 2555912 | tf_op jit(solution)/shard_map/ppermute | solution.py:248
  12.6 0.0 copy-done.2
  12.6 2.3 %shard_map.42 = f32[4,104,512]{2,1,0:T(8,128)S(1)} custom-call(s32[1]{0:T(128)} %bitcast.1.core_ref, f32[100,256]{1,0:T(8,128)S(1)} %copy-done.2, f32[256,4096]{1,0:T(8,128)} %field_ref.5), custom_call_target="tpu_custom_call" | custom-call | flops 314572800 | bytes 2916352 | tf_op jit(solution)/shard_map/pallas_call | solution.py:108
  14.9 0.0 collective-permute-done
  14.9 0.2 add.10
  15.0 15.5 %all_to_all.50.recv_ref = f32[4,104,512]{2,1,0:T(8,128)S(1)} all-to-all(f32[4,104,512]{2,1,0:T(8,128)S(1)} %add.10), channel_id=1, replica_groups=mesh['z'=16,'x'=4,'y'=4,'core'=2] {'y'}, dimensions={0} | all-to-all | bytes 1703936 | tf_op jit(solution)/shard_map/all_to_all | solution.py:231
  30.5 0.4 shard_map.43
  30.9 11.3 %all_to_all.51 = f32[32,8,128]{2,1,0:T(8,128)S(1)} all-to-all(f32[32,8,128]{2,1,0:T(8,128)S(1)} %bitcast.24), channel_id=1, replica_groups=mesh['z'=16,'x'=4,'y'=4,'core'=2] {'x','y','core'}, dimensions={0} | all-to-all | bytes 262144 | tf_op jit(solution)/shard_map/all_to_all | solution.py:231
  42.3 0.6 broadcast_in_dim.26
  42.9 13.2 %all-to-all-start.2 = ((f32[16,8,128]{2,1,0:T(8,128)}), f32[16,8,128]{2,1,0:T(8,128)S(1)}, u32[]{:S(2)}, u32[]{:S(2)}) async-start(f32[16,8,128]{2,1,0:T(8,128)} %broadcast_in_dim.26), calls=%async_computation.2 | async-start | bytes 131072 | tf_op jit(solution)/shard_map/all_to_all | solution.py:231
  56.2 2.2 %collective-permute-start.2 = (f32[104,512]{1,0:T(8,128)S(1)}, f32[104,512]{1,0:T(8,128)S(1)}, u32[]{:S(2)}, u32[]{:S(2)}) collective-permute-start(f32[104,512]{1,0:T(8,128)S(1)} %get-tuple-element.18), channel_id=1, source_target_pairs={{0,2},{2,4},{4,6},{6,0},{1,3},{3,5},{5,7},{7,1},{8,10},{10,12},{12... | collective-permute-start | bytes 638984 | tf_op jit(solution)/shard_map/ppermute | solution.py:254
  58.3 4.3 %collective-permute-start.1 = (f32[104,512]{1,0:T(8,128)S(1)}, f32[104,512]{1,0:T(8,128)S(1)}, u32[]{:S(2)}, u32[]{:S(2)}) collective-permute-start(f32[104,512]{1,0:T(8,128)S(1)} %get-tuple-element.18), channel_id=1, source_target_pairs={{2,0},{4,2},{6,4},{0,6},{3,1},{5,3},{7,5},{1,7},{10,8},{12,10},{14... | collective-permute-start | bytes 638984 | tf_op jit(solution)/shard_map/ppermute | solution.py:255
  62.7 5.1 %all-to-all-done.2 = f32[16,8,128]{2,1,0:T(8,128)S(1)} async-done(((f32[16,8,128]{2,1,0:T(8,128)}), f32[16,8,128]{2,1,0:T(8,128)S(1)}, u32[]{:S(2)}, u32[]{:S(2)}) %all-to-all-start.2) | async-done | bytes 65568 | tf_op jit(solution)/shard_map/all_to_all | solution.py:231
  67.8 0.7 broadcast_in_dim.27
  68.4 5.6 %all-to-all-start.3 = ((f32[32,8,128]{2,1,0:T(8,128)}), f32[32,8,128]{2,1,0:T(8,128)S(1)}, u32[]{:S(2)}, u32[]{:S(2)}) async-start(f32[32,8,128]{2,1,0:T(8,128)} %broadcast_in_dim.27), calls=%async_computation.3 | async-start | bytes 262144 | tf_op jit(solution)/shard_map/all_to_all | solution.py:231
  74.1 0.0 collective-permute-done.2
  74.1 3.3 %collective-permute-start.3 = (f32[104,512]{1,0:T(8,128)S(1)}, f32[104,512]{1,0:T(8,128)S(1)}, u32[]{:S(2)}, u32[]{:S(2)}) collective-permute-start(f32[104,512]{1,0:T(8,128)S(1)} %collective-permute-done.2), channel_id=1, source_target_pairs={{0,2},{2,4},{4,6},{6,0},{1,3},{3,5},{5,7},{7,1},{8,10},{10,12},{12... | collective-permute-start | bytes 638984 | tf_op jit(solution)/shard_map/ppermute | solution.py:256
  77.4 0.0 collective-permute-done.1
  77.4 4.5 %all-to-all-done.3 = f32[32,8,128]{2,1,0:T(8,128)S(1)} async-done(((f32[32,8,128]{2,1,0:T(8,128)}), f32[32,8,128]{2,1,0:T(8,128)S(1)}, u32[]{:S(2)}, u32[]{:S(2)}) %all-to-all-start.3) | async-done | bytes 131104 | tf_op jit(solution)/shard_map/all_to_all | solution.py:231
  81.9 4.8 %shard_map.44 = (f32[128,128]{1,0:T(8,128)}, f32[128,128]{1,0:T(8,128)S(1)}) custom-call(f32[256,128]{1,0:T(8,128)S(1)} %bitcast.21, f32[128,512]{1,0:T(8,128)S(1)} %get-tuple-element.20.loadings_ref), custom_call_target="tpu_custom_call" | custom-call | flops 5000000000 | tf_op jit(solution)/shard_map/pallas_call | solution.py:187
  86.7 0.0 collective-permute-done.3
  86.7 0.1 pad_maximum_fusion.near_ref
  86.8 2.3 %collective-permute-start.4 = (f32[4,104,512]{2,1,0:T(8,128)S(1)}, f32[4,104,512]{2,1,0:T(8,128)S(1)}, u32[]{:S(2)}, u32[]{:S(2)}) collective-permute-start(f32[4,104,512]{2,1,0:T(8,128)S(1)} %pad_maximum_fusion.near_ref), channel_id=1, source_target_pairs={{0,1},{1,0},{2,3},{3,2},{4,5},{5,4},{6,7},{7,6},{8,9},{9,8},{10,11... | collective-permute-start | bytes 2555912 | tf_op jit(solution)/shard_map/ppermute | solution.py:265
  89.1 0.1 pad_add_fusion.where_ref
  89.1 3.8 %all-to-all-start.4 = ((f32[32,4,128]{2,1,0:T(4,128)}), f32[32,4,128]{2,1,0:T(4,128)S(1)}, u32[]{:S(2)}, u32[]{:S(2)}) async-start(f32[32,4,128]{2,1,0:T(4,128)} %bitcast.4), calls=%async_computation.4 | async-start | bytes 131072 | tf_op jit(solution)/shard_map/all_to_all | solution.py:231
  92.9 0.0 collective-permute-done.4.far_ref
  93.0 0.0 copy-start
  93.0 2.2 %copy-done = f32[256,4096]{1,0:T(8,128)S(1)} copy-done((f32[256,4096]{1,0:T(8,128)S(1)}, f32[256,4096]{1,0:T(8,128)}, u32[]{:S(2)}) %copy-start) | copy-done | bytes 4194328
  95.1 2.0 %shard_map.45 = f32[208,128]{1,0:T(8,128)S(1)} custom-call(s32[2]{0:T(128)S(1)} %pad_add_fusion.where_ref, f32[256,4096]{1,0:T(8,128)S(1)} %copy-done, f32[4,104,512]{2,1,0:T(8,128)S(1)} %pad_maximum_fusion.near_ref, f32[4,104,512]{2,1,0:T(8,128)S(1)} %collective-permute-done.4.far_ref), custom_call_target="tpu_custom_call" | custom-call | flops 805306368 | bytes 5898240 | tf_op jit(solution)/shard_map/pallas_call | solution.py:216
  97.1 3.2 %all-to-all-done.4 = f32[32,4,128]{2,1,0:T(4,128)S(1)} async-done(((f32[32,4,128]{2,1,0:T(4,128)}), f32[32,4,128]{2,1,0:T(4,128)S(1)}, u32[]{:S(2)}, u32[]{:S(2)}) %all-to-all-start.4) | async-done | bytes 65568 | tf_op jit(solution)/shard_map/all_to_all | solution.py:231
  100.4 0.1 pad_maximum_fusion.1
  100.5 17.8 %all_to_all.52 = f32[16,1,2176]{2,1,0:T(1,128)S(1)} all-to-all(f32[16,1,2176]{2,1,0:T(1,128)S(1)} %pad_maximum_fusion.1), channel_id=1, replica_groups=mesh['z'=16,'x'=4,'y'=4,'core'=2] {'z'}, dimensions={0} | all-to-all | bytes 278528 | tf_op jit(solution)/shard_map/all_to_all | solution.py:231
  118.2 0.1 reduce_sum.68
  118.3 0.1 broadcast_in_dim.29
  118.5 16.4 %all_to_all.53 = f32[32,1,2176]{2,1,0:T(1,128)S(1)} all-to-all(f32[32,1,2176]{2,1,0:T(1,128)S(1)} %broadcast_in_dim.29), channel_id=1, replica_groups=mesh['z'=16,'x'=4,'y'=4,'core'=2] {'x','y','core'}, dimensions={0} | all-to-all | bytes 557056 | tf_op jit(solution)/shard_map/all_to_all | solution.py:231
  134.9 4.9 %shard_map.46 = (f32[128,128]{1,0:T(8,128)}, f32[128,128]{1,0:T(8,128)S(1)}) custom-call(f32[128,128]{1,0:T(8,128)S(1)} %bitcast.27, f32[256,128]{1,0:T(8,128)S(1)} %bitcast.22, f32[128,128]{1,0:T(8,128)S(1)} %get-tuple-element.27.y_ref, f32[128,512]{1,0:T(8,128)S(1)} %get-tuple-element.20.loadings_ref), custom_call_target="tpu_custom_call" | custom-call | flops 5000000000 | tf_op jit(solution)/shard_map/pallas_call | solution.py:187
  139.9 3.7 %all-to-all-start.7 = ((f32[32,4,128]{2,1,0:T(4,128)}), f32[32,4,128]{2,1,0:T(4,128)S(1)}, u32[]{:S(2)}, u32[]{:S(2)}) async-start(f32[32,4,128]{2,1,0:T(4,128)} %bitcast.13), calls=%async_computation.7 | async-start | bytes 131072 | tf_op jit(solution)/shard_map/all_to_all | solution.py:231
  143.7 7.4 %all-to-all-done.7 = f32[32,4,128]{2,1,0:T(4,128)S(1)} async-done(((f32[32,4,128]{2,1,0:T(4,128)}), f32[32,4,128]{2,1,0:T(4,128)S(1)}, u32[]{:S(2)}, u32[]{:S(2)}) %all-to-all-start.7) | async-done | bytes 65568 | tf_op jit(solution)/shard_map/all_to_all | solution.py:231
  151.1 0.1 broadcast_in_dim.30
  151.2 15.7 %all_to_all.54 = f32[16,1,2176]{2,1,0:T(1,128)S(1)} all-to-all(f32[16,1,2176]{2,1,0:T(1,128)S(1)} %broadcast_in_dim.30), channel_id=1, replica_groups=mesh['z'=16,'x'=4,'y'=4,'core'=2] {'z'}, dimensions={0} | all-to-all | bytes 278528 | tf_op jit(solution)/shard_map/all_to_all | solution.py:231
  167.0 14.0 %all_to_all.55 = f32[32,4,128]{2,1,0:T(4,128)S(1)} all-to-all(f32[32,4,128]{2,1,0:T(4,128)S(1)} %broadcast_in_dim.31), channel_id=1, replica_groups=mesh['z'=16,'x'=4,'y'=4,'core'=2] {'x','y','core'}, dimensions={0} | all-to-all | bytes 131072 | tf_op jit(solution)/shard_map/all_to_all | solution.py:231
  181.0 4.8 %shard_map.47 = (f32[100,512]{1,0:T(8,128)}, f32[100,256]{1,0:T(8,128)}) custom-call(f32[128,128]{1,0:T(8,128)S(1)} %bitcast.26, f32[256,128]{1,0:T(8,128)S(1)} %bitcast.23, f32[128,128]{1,0:T(8,128)S(1)} %get-tuple-element.30.y_ref, f32[128,512]{1,0:T(8,128)S(1)} %get-tuple-element.20.loadings_ref, f32[208,128]{1,0:T(8,128)S(1)} %bitcast.25), custom_call_target="tpu_custom_call" | custom-call | flops 5000000000 | tf_op jit(solution)/shard_map/pallas_call | solution.py:187
  (13 shorter events, 0.3 us)
Async XLA Ops:
  0.6 0.9 copy-start.1
  1.5 11.0 %copy-start.2 = (f32[100,256]{1,0:T(8,128)S(1)}, f32[100,256]{1,0:T(8,128)}, u32[]{:S(2)}) copy-start(f32[100,256]{1,0:T(8,128)} %pcs_ref.3) | copy-start | bytes 307204
  3.8 11.1 %collective-permute-start = (f32[4,104,512]{2,1,0:T(8,128)S(1)}, f32[4,104,512]{2,1,0:T(8,128)S(1)}, u32[]{:S(2)}, u32[]{:S(2)}) collective-permute-start(f32[4,104,512]{2,1,0:T(8,128)S(1)} %shard_map.41), channel_id=1, source_target_pairs={{0,1},{1,0},{2,3},{3,2},{4,5},{5,4},{6,7},{7,6},{8,9},{9,8},{10,11... | collective-permute-start | bytes 2555912 | tf_op jit(solution)/shard_map/ppermute | solution.py:248
  42.9 24.9 %all-to-all-start.2 = ((f32[16,8,128]{2,1,0:T(8,128)}), f32[16,8,128]{2,1,0:T(8,128)S(1)}, u32[]{:S(2)}, u32[]{:S(2)}) async-start(f32[16,8,128]{2,1,0:T(8,128)} %broadcast_in_dim.26), calls=%async_computation.2 | async-start | bytes 131072 | tf_op jit(solution)/shard_map/all_to_all | solution.py:231
  56.2 17.9 %collective-permute-start.2 = (f32[104,512]{1,0:T(8,128)S(1)}, f32[104,512]{1,0:T(8,128)S(1)}, u32[]{:S(2)}, u32[]{:S(2)}) collective-permute-start(f32[104,512]{1,0:T(8,128)S(1)} %get-tuple-element.18), channel_id=1, source_target_pairs={{0,2},{2,4},{4,6},{6,0},{1,3},{3,5},{5,7},{7,1},{8,10},{10,12},{12... | collective-permute-start | bytes 638984 | tf_op jit(solution)/shard_map/ppermute | solution.py:254
  58.3 19.1 %collective-permute-start.1 = (f32[104,512]{1,0:T(8,128)S(1)}, f32[104,512]{1,0:T(8,128)S(1)}, u32[]{:S(2)}, u32[]{:S(2)}) collective-permute-start(f32[104,512]{1,0:T(8,128)S(1)} %get-tuple-element.18), channel_id=1, source_target_pairs={{2,0},{4,2},{6,4},{0,6},{3,1},{5,3},{7,5},{1,7},{10,8},{12,10},{14... | collective-permute-start | bytes 638984 | tf_op jit(solution)/shard_map/ppermute | solution.py:255
  68.4 13.4 %all-to-all-start.3 = ((f32[32,8,128]{2,1,0:T(8,128)}), f32[32,8,128]{2,1,0:T(8,128)S(1)}, u32[]{:S(2)}, u32[]{:S(2)}) async-start(f32[32,8,128]{2,1,0:T(8,128)} %broadcast_in_dim.27), calls=%async_computation.3 | async-start | bytes 262144 | tf_op jit(solution)/shard_map/all_to_all | solution.py:231
  74.1 12.6 %collective-permute-start.3 = (f32[104,512]{1,0:T(8,128)S(1)}, f32[104,512]{1,0:T(8,128)S(1)}, u32[]{:S(2)}, u32[]{:S(2)}) collective-permute-start(f32[104,512]{1,0:T(8,128)S(1)} %collective-permute-done.2), channel_id=1, source_target_pairs={{0,2},{2,4},{4,6},{6,0},{1,3},{3,5},{5,7},{7,1},{8,10},{10,12},{12... | collective-permute-start | bytes 638984 | tf_op jit(solution)/shard_map/ppermute | solution.py:256
  86.8 6.2 %collective-permute-start.4 = (f32[4,104,512]{2,1,0:T(8,128)S(1)}, f32[4,104,512]{2,1,0:T(8,128)S(1)}, u32[]{:S(2)}, u32[]{:S(2)}) collective-permute-start(f32[4,104,512]{2,1,0:T(8,128)S(1)} %pad_maximum_fusion.near_ref), channel_id=1, source_target_pairs={{0,1},{1,0},{2,3},{3,2},{4,5},{5,4},{6,7},{7,6},{8,9},{9,8},{10,11... | collective-permute-start | bytes 2555912 | tf_op jit(solution)/shard_map/ppermute | solution.py:265
  89.1 11.2 %all-to-all-start.4 = ((f32[32,4,128]{2,1,0:T(4,128)}), f32[32,4,128]{2,1,0:T(4,128)S(1)}, u32[]{:S(2)}, u32[]{:S(2)}) async-start(f32[32,4,128]{2,1,0:T(4,128)} %bitcast.4), calls=%async_computation.4 | async-start | bytes 131072 | tf_op jit(solution)/shard_map/all_to_all | solution.py:231
  93.0 2.2 %copy-start = (f32[256,4096]{1,0:T(8,128)S(1)}, f32[256,4096]{1,0:T(8,128)}, u32[]{:S(2)}) copy-start(f32[256,4096]{1,0:T(8,128)} %field_ref.5) | copy-start | bytes 12582916
  139.9 11.1 %all-to-all-start.7 = ((f32[32,4,128]{2,1,0:T(4,128)}), f32[32,4,128]{2,1,0:T(4,128)S(1)}, u32[]{:S(2)}, u32[]{:S(2)}) async-start(f32[32,4,128]{2,1,0:T(4,128)} %bitcast.13), calls=%async_computation.7 | async-start | bytes 131072 | tf_op jit(solution)/shard_map/all_to_all | solution.py:231

commit v9 on v8

--- a/solution.py
+++ b/solution.py
@@ -18,7 +18,7 @@
 F32 = jnp.float32
 VMEM = pl.BlockSpec(memory_space=pltpu.VMEM)
 LIMIT = 24 << 20
-FLOPS = 5000000000
+FLOPS = 10000000000
 WIDE_LIMIT = 52 << 20
 
 
@@ -256,13 +256,12 @@
     second_up = lax.ppermute(first_up, "y", up)
     chunk = swap(spread(jnp.sum(chunk, axis=0), Z), "z")
     base = swap(spread(jnp.sum(chunk, axis=0), N_PLANE), PLANE)
-    base, down = lax.optimization_barrier((base, down))
+    near = jnp.stack([narrow, first_up, second_up, down])
+    far = lax.ppermute(near, "core", [(0, 1), (1, 0)])
     base = base.reshape(2 * PAD, PAD)
     sent, y = whole(functools.partial(second_kernel, cells_total), [(PAD, PAD)] * 2, base, loadings)
 
-    sent, second_up = lax.optimization_barrier((sent, second_up))
-    near = jnp.stack([narrow, first_up, second_up, down])
-    far = lax.ppermute(near, "core", [(0, 1), (1, 0)])
+    sent, near, far = lax.optimization_barrier((sent, near, far))
     terms = series_terms(field, near, far, jnp.stack([row, core]), days_total**0.5 / cells_total)
     chunk, terms = lax.optimization_barrier((swap(sent.reshape(N_PLANE, ROWS, PAD), PLANE), terms))
     chunk = jnp.sum(chunk, axis=0)

time: 187 us -> 188 us (level)
  waiting for transfers between devices: 20.1 us -> 22.4 us
  starting transfers between devices: 47.2 us -> 45.3 us
    all_to_all x4, waiting for transfers between devices: 20.1 us -> 22.4 us  [swap(): return lax.all_to_all(value, axes, 0, 0)]
  transfers between devices with their start and end apart: 9 -> 9, of which waited for: 4 -> 4; matrix products, arithmetic and copies ran while one was open for 0% -> 1% of each run, Pallas kernels for 5% -> 5%
where the time goes in v9:
time: 188 us; the launch traced here: 187 us
  blocking collectives  92 us (49%)
  starting transfers between devices  45.3 us (24%)
  waiting for transfers between devices  22.4 us (12%)
  Pallas kernels  21.4 us (11%)
  local copies, waits for them, and re-layouts  4.68 us (2%)
    all_to_all x6, blocking collectives, swap(): return lax.all_to_all(value, axes, 0, 0)  92 us
    all_to_all x4, starting transfers between devices, swap(): return lax.all_to_all(value, axes, 0, 0)  26.8 us
    all_to_all x4, waiting for transfers between devices, swap(): return lax.all_to_all(value, axes, 0, 0)  22.4 us
    pallas_call x3, Pallas kernels, whole(): pl.pallas_call(kernel, out_shape=tuple((jax.ShapeDtypeStruct(s, F32) for...  14.6 us
    ppermute x1, starting transfers between devices, on_device(): lax.ppermute(parts(field, pcs, (1 - core)[None], scale), 'core', [(0, 1),...  8.79 us
    pallas_call x2, Pallas kernels, parts(): pl.pallas_call(functools.partial(parts_kernel, scale), out_shape=jax.Shap...  4.5 us
  transfers between devices with their start and end apart: 9, of which 4 were waited for; matrix products, arithmetic and copies ran while one was open for 1% of the time, Pallas kernels for 5%

profile of v9, /device:TPU:1, one launch (start us, length us, event | category | flops | bytes accessed | tf_op | source)
XLA Modules:
  0.0 187.4 jit_solution(8136505033618354066)
XLA Ops:
  0.6 0.0 copy-start.1
  0.6 0.9 copy-done.1
  1.5 0.0 copy-start.2
  1.5 2.2 %shard_map.41 = f32[4,104,512]{2,1,0:T(8,128)S(1)} custom-call(s32[1]{0:T(128)} %bitcast.core_ref, f32[100,256]{1,0:T(8,128)S(1)} %copy-done.1, f32[256,4096]{1,0:T(8,128)} %field_ref.5), custom_call_target="tpu_custom_call" | custom-call | flops 314572800 | bytes 2916352 | tf_op jit(solution)/shard_map/pallas_call | solution.py:108
  3.8 8.8 %collective-permute-start = (f32[4,104,512]{2,1,0:T(8,128)S(1)}, f32[4,104,512]{2,1,0:T(8,128)S(1)}, u32[]{:S(2)}, u32[]{:S(2)}) collective-permute-start(f32[4,104,512]{2,1,0:T(8,128)S(1)} %shard_map.41), channel_id=1, source_target_pairs={{0,1},{1,0},{2,3},{3,2},{4,5},{5,4},{6,7},{7,6},{8,9},{9,8},{10,11... | collective-permute-start | bytes 2555912 | tf_op jit(solution)/shard_map/ppermute | solution.py:248
  12.6 0.0 copy-done.2
  12.6 2.3 %shard_map.42 = f32[4,104,512]{2,1,0:T(8,128)S(1)} custom-call(s32[1]{0:T(128)} %bitcast.1.core_ref, f32[100,256]{1,0:T(8,128)S(1)} %copy-done.2, f32[256,4096]{1,0:T(8,128)} %field_ref.5), custom_call_target="tpu_custom_call" | custom-call | flops 314572800 | bytes 2916352 | tf_op jit(solution)/shard_map/pallas_call | solution.py:108
  14.9 0.0 collective-permute-done
  14.9 0.2 add.10
  15.0 15.5 %all_to_all.50.recv_ref = f32[4,104,512]{2,1,0:T(8,128)S(1)} all-to-all(f32[4,104,512]{2,1,0:T(8,128)S(1)} %add.10), channel_id=1, replica_groups=mesh['z'=16,'x'=4,'y'=4,'core'=2] {'y'}, dimensions={0} | all-to-all | bytes 1703936 | tf_op jit(solution)/shard_map/all_to_all | solution.py:231
  30.5 0.4 shard_map.43
  30.9 2.2 %collective-permute-start.1 = (f32[104,512]{1,0:T(8,128)S(1)}, f32[104,512]{1,0:T(8,128)S(1)}, u32[]{:S(2)}, u32[]{:S(2)}) collective-permute-start(f32[104,512]{1,0:T(8,128)S(1)} %get-tuple-element.19), channel_id=1, source_target_pairs={{0,2},{2,4},{4,6},{6,0},{1,3},{3,5},{5,7},{7,1},{8,10},{10,12},{12... | collective-permute-start | bytes 638984 | tf_op jit(solution)/shard_map/ppermute | solution.py:254
  33.1 12.7 %all_to_all.51 = f32[32,8,128]{2,1,0:T(8,128)S(1)} all-to-all(f32[32,8,128]{2,1,0:T(8,128)S(1)} %bitcast.24), channel_id=1, replica_groups=mesh['z'=16,'x'=4,'y'=4,'core'=2] {'x','y','core'}, dimensions={0} | all-to-all | bytes 262144 | tf_op jit(solution)/shard_map/all_to_all | solution.py:231
  45.9 0.6 broadcast_in_dim.26
  46.5 13.6 %all-to-all-start.2 = ((f32[16,8,128]{2,1,0:T(8,128)}), f32[16,8,128]{2,1,0:T(8,128)S(1)}, u32[]{:S(2)}, u32[]{:S(2)}) async-start(f32[16,8,128]{2,1,0:T(8,128)} %broadcast_in_dim.26), calls=%async_computation.2 | async-start | bytes 131072 | tf_op jit(solution)/shard_map/all_to_all | solution.py:231
  60.1 2.8 %collective-permute-start.3 = (f32[104,512]{1,0:T(8,128)S(1)}, f32[104,512]{1,0:T(8,128)S(1)}, u32[]{:S(2)}, u32[]{:S(2)}) collective-permute-start(f32[104,512]{1,0:T(8,128)S(1)} %get-tuple-element.19), channel_id=1, source_target_pairs={{2,0},{4,2},{6,4},{0,6},{3,1},{5,3},{7,5},{1,7},{10,8},{12,10},{14... | collective-permute-start | bytes 638984 | tf_op jit(solution)/shard_map/ppermute | solution.py:255
  63.0 0.0 collective-permute-done.1
  63.0 2.5 %collective-permute-start.2 = (f32[104,512]{1,0:T(8,128)S(1)}, f32[104,512]{1,0:T(8,128)S(1)}, u32[]{:S(2)}, u32[]{:S(2)}) collective-permute-start(f32[104,512]{1,0:T(8,128)S(1)} %collective-permute-done.1), channel_id=1, source_target_pairs={{0,2},{2,4},{4,6},{6,0},{1,3},{3,5},{5,7},{7,1},{8,10},{10,12},{12... | collective-permute-start | bytes 638984 | tf_op jit(solution)/shard_map/ppermute | solution.py:256
  65.5 0.1 pad_add_fusion.where_ref
  65.5 6.2 %all-to-all-done.2 = f32[16,8,128]{2,1,0:T(8,128)S(1)} async-done(((f32[16,8,128]{2,1,0:T(8,128)}), f32[16,8,128]{2,1,0:T(8,128)S(1)}, u32[]{:S(2)}, u32[]{:S(2)}) %all-to-all-start.2) | async-done | bytes 65568 | tf_op jit(solution)/shard_map/all_to_all | solution.py:231
  71.8 0.7 broadcast_in_dim.27
  72.4 5.6 %all-to-all-start.3 = ((f32[32,8,128]{2,1,0:T(8,128)}), f32[32,8,128]{2,1,0:T(8,128)S(1)}, u32[]{:S(2)}, u32[]{:S(2)}) async-start(f32[32,8,128]{2,1,0:T(8,128)} %broadcast_in_dim.27), calls=%async_computation.3 | async-start | bytes 262144 | tf_op jit(solution)/shard_map/all_to_all | solution.py:231
  78.0 0.0 collective-permute-done.3
  78.1 0.0 collective-permute-done.2
  78.1 0.1 pad_maximum_fusion.near_ref
  78.1 2.3 %collective-permute-start.4 = (f32[4,104,512]{2,1,0:T(8,128)S(1)}, f32[4,104,512]{2,1,0:T(8,128)S(1)}, u32[]{:S(2)}, u32[]{:S(2)}) collective-permute-start(f32[4,104,512]{2,1,0:T(8,128)S(1)} %pad_maximum_fusion.near_ref), channel_id=1, source_target_pairs={{0,1},{1,0},{2,3},{3,2},{4,5},{5,4},{6,7},{7,6},{8,9},{9,8},{10,11... | collective-permute-start | bytes 2555912 | tf_op jit(solution)/shard_map/ppermute | solution.py:260
  80.4 5.5 %all-to-all-done.3 = f32[32,8,128]{2,1,0:T(8,128)S(1)} async-done(((f32[32,8,128]{2,1,0:T(8,128)}), f32[32,8,128]{2,1,0:T(8,128)S(1)}, u32[]{:S(2)}, u32[]{:S(2)}) %all-to-all-start.3) | async-done | bytes 131104 | tf_op jit(solution)/shard_map/all_to_all | solution.py:231
  85.9 4.8 %shard_map.44 = (f32[128,128]{1,0:T(8,128)}, f32[128,128]{1,0:T(8,128)S(1)}) custom-call(f32[256,128]{1,0:T(8,128)S(1)} %bitcast.21, f32[128,512]{1,0:T(8,128)S(1)} %get-tuple-element.17.loadings_ref), custom_call_target="tpu_custom_call" | custom-call | flops 10000000000 | tf_op jit(solution)/shard_map/pallas_call | solution.py:187
  90.7 0.0 collective-permute-done.4.far_ref
  90.7 3.9 %all-to-all-start.4 = ((f32[32,4,128]{2,1,0:T(4,128)}), f32[32,4,128]{2,1,0:T(4,128)S(1)}, u32[]{:S(2)}, u32[]{:S(2)}) async-start(f32[32,4,128]{2,1,0:T(4,128)} %bitcast.8), calls=%async_computation.4 | async-start | bytes 131072 | tf_op jit(solution)/shard_map/all_to_all | solution.py:231
  94.6 0.0 copy-start
  94.6 2.2 %copy-done = f32[256,4096]{1,0:T(8,128)S(1)} copy-done((f32[256,4096]{1,0:T(8,128)S(1)}, f32[256,4096]{1,0:T(8,128)}, u32[]{:S(2)}) %copy-start) | copy-done | bytes 4194328
  96.8 2.0 %shard_map.45 = f32[208,128]{1,0:T(8,128)S(1)} custom-call(s32[2]{0:T(128)S(1)} %pad_add_fusion.where_ref, f32[256,4096]{1,0:T(8,128)S(1)} %copy-done, f32[4,104,512]{2,1,0:T(8,128)S(1)} %pad_maximum_fusion.near_ref, f32[4,104,512]{2,1,0:T(8,128)S(1)} %collective-permute-done.4.far_ref), custom_call_target="tpu_custom_call" | custom-call | flops 805306368 | bytes 5898240 | tf_op jit(solution)/shard_map/pallas_call | solution.py:216
  98.7 3.3 %all-to-all-done.4 = f32[32,4,128]{2,1,0:T(4,128)S(1)} async-done(((f32[32,4,128]{2,1,0:T(4,128)}), f32[32,4,128]{2,1,0:T(4,128)S(1)}, u32[]{:S(2)}, u32[]{:S(2)}) %all-to-all-start.4) | async-done | bytes 65568 | tf_op jit(solution)/shard_map/all_to_all | solution.py:231
  102.1 0.1 pad_maximum_fusion.1
  102.2 17.6 %all_to_all.52 = f32[16,1,2176]{2,1,0:T(1,128)S(1)} all-to-all(f32[16,1,2176]{2,1,0:T(1,128)S(1)} %pad_maximum_fusion.1), channel_id=1, replica_groups=mesh['z'=16,'x'=4,'y'=4,'core'=2] {'z'}, dimensions={0} | all-to-all | bytes 278528 | tf_op jit(solution)/shard_map/all_to_all | solution.py:231
  119.8 0.1 reduce_sum.68
  119.9 0.1 broadcast_in_dim.29
  120.1 16.4 %all_to_all.53 = f32[32,1,2176]{2,1,0:T(1,128)S(1)} all-to-all(f32[32,1,2176]{2,1,0:T(1,128)S(1)} %broadcast_in_dim.29), channel_id=1, replica_groups=mesh['z'=16,'x'=4,'y'=4,'core'=2] {'x','y','core'}, dimensions={0} | all-to-all | bytes 557056 | tf_op jit(solution)/shard_map/all_to_all | solution.py:231
  136.5 4.9 %shard_map.46 = (f32[128,128]{1,0:T(8,128)}, f32[128,128]{1,0:T(8,128)S(1)}) custom-call(f32[128,128]{1,0:T(8,128)S(1)} %bitcast.27, f32[256,128]{1,0:T(8,128)S(1)} %bitcast.22, f32[128,128]{1,0:T(8,128)S(1)} %get-tuple-element.25.y_ref, f32[128,512]{1,0:T(8,128)S(1)} %get-tuple-element.17.loadings_ref), custom_call_target="tpu_custom_call" | custom-call | flops 10000000000 | tf_op jit(solution)/shard_map/pallas_call | solution.py:187
  141.4 3.7 %all-to-all-start.7 = ((f32[32,4,128]{2,1,0:T(4,128)}), f32[32,4,128]{2,1,0:T(4,128)S(1)}, u32[]{:S(2)}, u32[]{:S(2)}) async-start(f32[32,4,128]{2,1,0:T(4,128)} %bitcast.13), calls=%async_computation.7 | async-start | bytes 131072 | tf_op jit(solution)/shard_map/all_to_all | solution.py:231
  145.2 7.4 %all-to-all-done.7 = f32[32,4,128]{2,1,0:T(4,128)S(1)} async-done(((f32[32,4,128]{2,1,0:T(4,128)}), f32[32,4,128]{2,1,0:T(4,128)S(1)}, u32[]{:S(2)}, u32[]{:S(2)}) %all-to-all-start.7) | async-done | bytes 65568 | tf_op jit(solution)/shard_map/all_to_all | solution.py:231
  152.7 0.1 broadcast_in_dim.30
  152.7 15.8 %all_to_all.54 = f32[16,1,2176]{2,1,0:T(1,128)S(1)} all-to-all(f32[16,1,2176]{2,1,0:T(1,128)S(1)} %broadcast_in_dim.30), channel_id=1, replica_groups=mesh['z'=16,'x'=4,'y'=4,'core'=2] {'z'}, dimensions={0} | all-to-all | bytes 278528 | tf_op jit(solution)/shard_map/all_to_all | solution.py:231
  168.6 14.0 %all_to_all.55 = f32[32,4,128]{2,1,0:T(4,128)S(1)} all-to-all(f32[32,4,128]{2,1,0:T(4,128)S(1)} %broadcast_in_dim.31), channel_id=1, replica_groups=mesh['z'=16,'x'=4,'y'=4,'core'=2] {'x','y','core'}, dimensions={0} | all-to-all | bytes 131072 | tf_op jit(solution)/shard_map/all_to_all | solution.py:231
  182.6 4.8 %shard_map.47 = (f32[100,512]{1,0:T(8,128)}, f32[100,256]{1,0:T(8,128)}) custom-call(f32[128,128]{1,0:T(8,128)S(1)} %bitcast.26, f32[256,128]{1,0:T(8,128)S(1)} %bitcast.23, f32[128,128]{1,0:T(8,128)S(1)} %get-tuple-element.28.y_ref, f32[128,512]{1,0:T(8,128)S(1)} %get-tuple-element.17.loadings_ref, f32[208,128]{1,0:T(8,128)S(1)} %bitcast.25), custom_call_target="tpu_custom_call" | custom-call | flops 10000000000 | tf_op jit(solution)/shard_map/pallas_call | solution.py:187
  (13 shorter events, 0.3 us)
Async XLA Ops:
  0.6 0.9 copy-start.1
  1.5 11.0 %copy-start.2 = (f32[100,256]{1,0:T(8,128)S(1)}, f32[100,256]{1,0:T(8,128)}, u32[]{:S(2)}) copy-start(f32[100,256]{1,0:T(8,128)} %pcs_ref.3) | copy-start | bytes 307204
  3.8 11.1 %collective-permute-start = (f32[4,104,512]{2,1,0:T(8,128)S(1)}, f32[4,104,512]{2,1,0:T(8,128)S(1)}, u32[]{:S(2)}, u32[]{:S(2)}) collective-permute-start(f32[4,104,512]{2,1,0:T(8,128)S(1)} %shard_map.41), channel_id=1, source_target_pairs={{0,1},{1,0},{2,3},{3,2},{4,5},{5,4},{6,7},{7,6},{8,9},{9,8},{10,11... | collective-permute-start | bytes 2555912 | tf_op jit(solution)/shard_map/ppermute | solution.py:248
  30.9 32.0 %collective-permute-start.1 = (f32[104,512]{1,0:T(8,128)S(1)}, f32[104,512]{1,0:T(8,128)S(1)}, u32[]{:S(2)}, u32[]{:S(2)}) collective-permute-start(f32[104,512]{1,0:T(8,128)S(1)} %get-tuple-element.19), channel_id=1, source_target_pairs={{0,2},{2,4},{4,6},{6,0},{1,3},{3,5},{5,7},{7,1},{8,10},{10,12},{12... | collective-permute-start | bytes 638984 | tf_op jit(solution)/shard_map/ppermute | solution.py:254
  46.5 25.2 %all-to-all-start.2 = ((f32[16,8,128]{2,1,0:T(8,128)}), f32[16,8,128]{2,1,0:T(8,128)S(1)}, u32[]{:S(2)}, u32[]{:S(2)}) async-start(f32[16,8,128]{2,1,0:T(8,128)} %broadcast_in_dim.26), calls=%async_computation.2 | async-start | bytes 131072 | tf_op jit(solution)/shard_map/all_to_all | solution.py:231
  60.1 17.9 %collective-permute-start.3 = (f32[104,512]{1,0:T(8,128)S(1)}, f32[104,512]{1,0:T(8,128)S(1)}, u32[]{:S(2)}, u32[]{:S(2)}) collective-permute-start(f32[104,512]{1,0:T(8,128)S(1)} %get-tuple-element.19), channel_id=1, source_target_pairs={{2,0},{4,2},{6,4},{0,6},{3,1},{5,3},{7,5},{1,7},{10,8},{12,10},{14... | collective-permute-start | bytes 638984 | tf_op jit(solution)/shard_map/ppermute | solution.py:255
  63.0 15.1 %collective-permute-start.2 = (f32[104,512]{1,0:T(8,128)S(1)}, f32[104,512]{1,0:T(8,128)S(1)}, u32[]{:S(2)}, u32[]{:S(2)}) collective-permute-start(f32[104,512]{1,0:T(8,128)S(1)} %collective-permute-done.1), channel_id=1, source_target_pairs={{0,2},{2,4},{4,6},{6,0},{1,3},{3,5},{5,7},{7,1},{8,10},{10,12},{12... | collective-permute-start | bytes 638984 | tf_op jit(solution)/shard_map/ppermute | solution.py:256
  72.4 13.4 %all-to-all-start.3 = ((f32[32,8,128]{2,1,0:T(8,128)}), f32[32,8,128]{2,1,0:T(8,128)S(1)}, u32[]{:S(2)}, u32[]{:S(2)}) async-start(f32[32,8,128]{2,1,0:T(8,128)} %broadcast_in_dim.27), calls=%async_computation.3 | async-start | bytes 262144 | tf_op jit(solution)/shard_map/all_to_all | solution.py:231
  78.1 12.5 %collective-permute-start.4 = (f32[4,104,512]{2,1,0:T(8,128)S(1)}, f32[4,104,512]{2,1,0:T(8,128)S(1)}, u32[]{:S(2)}, u32[]{:S(2)}) collective-permute-start(f32[4,104,512]{2,1,0:T(8,128)S(1)} %pad_maximum_fusion.near_ref), channel_id=1, source_target_pairs={{0,1},{1,0},{2,3},{3,2},{4,5},{5,4},{6,7},{7,6},{8,9},{9,8},{10,11... | collective-permute-start | bytes 2555912 | tf_op jit(solution)/shard_map/ppermute | solution.py:260
  90.7 11.4 %all-to-all-start.4 = ((f32[32,4,128]{2,1,0:T(4,128)}), f32[32,4,128]{2,1,0:T(4,128)S(1)}, u32[]{:S(2)}, u32[]{:S(2)}) async-start(f32[32,4,128]{2,1,0:T(4,128)} %bitcast.8), calls=%async_computation.4 | async-start | bytes 131072 | tf_op jit(solution)/shard_map/all_to_all | solution.py:231
  94.6 2.2 %copy-start = (f32[256,4096]{1,0:T(8,128)S(1)}, f32[256,4096]{1,0:T(8,128)}, u32[]{:S(2)}) copy-start(f32[256,4096]{1,0:T(8,128)} %field_ref.5) | copy-start | bytes 12582916
  141.4 11.1 %all-to-all-start.7 = ((f32[32,4,128]{2,1,0:T(4,128)}), f32[32,4,128]{2,1,0:T(4,128)S(1)}, u32[]{:S(2)}, u32[]{:S(2)}) async-start(f32[32,4,128]{2,1,0:T(4,128)} %bitcast.13), calls=%async_computation.7 | async-start | bytes 131072 | tf_op jit(solution)/shard_map/all_to_all | solution.py:231
